TPU v7x, 32 devices: a whole 2x2x4 slice. The times are simulated.
32 devices in a mesh: tok: 8 (over y, x, core), kv: 4 (over z).
Axes of the slice: x: 2, y: 2, z: 4, core: 2. Of those that a mesh axis runs over, the one named last changes fastest.
Arguments:
- queries: bfloat16 [2048, 8192], P('tok', 'kv'), may hold values from -12 to 12
- key_states: bfloat16 [2048, 1024], P('tok', 'kv'), may hold values from -12 to 12
- value_states: bfloat16 [2048, 1024], P('tok', 'kv'), may hold values from -6 to 6
- doc_lengths: int32 [16], replicated, may hold values from 1 to 1024, 2048 in all
- block_plan: int32 [8, 8], replicated, may hold values from 0 to 7, each once within a row
Outputs:
- attention_out: bfloat16 [2048, 8192], P(('tok', 'kv'))
- served_lse: float32 [64, 2048], P('kv', 'tok')
Inputs may be any that keep to these rules, and one draw needn't show every extreme that they name: `doc_lengths`: positive lengths that sum to 2048; the largest is exactly 1024. Every row of block_plan is a permutation of 0 to 7.
All inputs are finite; a program needn't handle non-finite values.
Results may differ from a plain program's by a relative error of at most 0.012.
The roundings to bfloat16 on the way count: a program that leaves them out, or rounds other values in their place, can miss the bound.
Values may be sent and summed in bfloat16 or wider, within the bound.
No kernel may reach another device: no remote copies, remote signals or barrier semaphores. Data moves between devices by JAX's collectives and lax.ppermute only.
A program may use at most 64 MiB of HBM per device.

v0:
```python
import math
from functools import partial

import jax
import jax.numpy as jnp
import numpy as np
from jax import lax
from jax.experimental import pallas as pl
from jax.experimental.pallas import tpu as pltpu
from jax.sharding import PartitionSpec as P

HEAD_DIM = 128
HALF = HEAD_DIM // 2
THETA = 500000.0
NEG = -1e30
LOG2E = math.log2(math.e)
SCALE = 1.0 / math.sqrt(HEAD_DIM)
VMEM_LIMIT = 48 * 1024 * 1024


def vmem():
    return pl.BlockSpec(memory_space=pltpu.VMEM)


def smem():
    return pl.BlockSpec(memory_space=pltpu.SMEM)


def hbm():
    return pl.BlockSpec(memory_space=pl.ANY)


def far_hbm():
    return pl.BlockSpec(memory_space=pltpu.HBM)


def params():
    return pltpu.CompilerParams(vmem_limit_bytes=VMEM_LIMIT)


def cost(microseconds):
    return pl.CostEstimate(flops=int(microseconds * 1.15e9), bytes_accessed=0, transcendentals=0)


def doc_starts(lengths_ref, token):
    begin = jnp.int32(0)
    start = jnp.zeros_like(token)
    for doc in range(lengths_ref.shape[0] - 1):
        begin = begin + lengths_ref[doc]
        start = jnp.where(token >= begin, begin, start)
    return start


def rotary_tables(lengths_ref, freq_ref, rows, first):
    token = first + lax.broadcasted_iota(jnp.int32, (rows, HEAD_DIM), 0)
    start = doc_starts(lengths_ref, token)
    position = token - start
    angle = position.astype(jnp.float32) * freq_ref[...]
    lane = lax.broadcasted_iota(jnp.int32, (rows, HEAD_DIM), 1)
    sine = jnp.sin(angle)
    return jnp.cos(angle), jnp.where(lane < HALF, -sine, sine), start


def turn(block, cosine, sine):
    x = block.astype(jnp.float32)
    return (x * cosine + pltpu.roll(x, HALF, 1) * sine).astype(jnp.bfloat16)


def pack(out_ref, key_ref, value_ref, cosine, sine):
    for group in range(key_ref.shape[1] // HEAD_DIM):
        cols = slice(group * HEAD_DIM, (group + 1) * HEAD_DIM)
        place = 2 * group * HEAD_DIM
        out_ref[:, place : place + HEAD_DIM] = turn(key_ref[:, cols], cosine, sine)
        out_ref[:, place + HEAD_DIM : place + 2 * HEAD_DIM] = value_ref[:, cols]


def queries_kernel(pieces, where_ref, lengths_ref, freq_ref, key_hbm, value_hbm, query_hbm, *refs):
    pack_ref, start_ref, table_ref = refs[:3]
    turn_refs = refs[3:-4]
    key_ref, value_ref, query_ref, sems = refs[-4:]
    copies = [
        pltpu.make_async_copy(key_hbm, key_ref, sems.at[0]),
        pltpu.make_async_copy(value_hbm, value_ref, sems.at[1]),
        pltpu.make_async_copy(query_hbm, query_ref, sems.at[2]),
    ]
    for c in copies:
        c.start()
    rows = query_ref.shape[0]
    shard = where_ref[0]
    cosine, sine, start = rotary_tables(lengths_ref, freq_ref, rows, shard * rows)
    start_ref[...] = start
    for c in copies[:2]:
        c.wait()
    pack(pack_ref, key_ref, value_ref, cosine, sine)
    copies[2].wait()
    tiles, stacked, _ = turn_refs[0].shape
    tile = rows // tiles
    per_group = stacked // tile
    for group, out_ref in enumerate(turn_refs):
        for head in range(per_group):
            cols = pl.ds((group * per_group + head) * HEAD_DIM, HEAD_DIM)
            turned = turn(query_ref[:, cols], cosine, sine)
            for t in range(tiles):
                out_ref[t, head * tile : (head + 1) * tile, :] = turned[t * tile : (t + 1) * tile]
    for p in range(1, pieces + 1):
        cosine, sine, _ = rotary_tables(lengths_ref, freq_ref, rows, (shard - 2 * p) * rows)
        table_ref[2 * p - 2] = cosine
        table_ref[2 * p - 1] = sine


def pack_kernel(table_ref, *refs):
    pieces = len(refs) // 2
    for p in range(pieces):
        pack(
            refs[2 * pieces].at[p],
            refs[p],
            refs[pieces + p],
            table_ref[2 * p],
            table_ref[2 * p + 1],
        )


def attend_kernel(pieces, per_group, groups, tiles_of, begun, last, where_ref, *refs):
    plan_ref = norm_ref = None
    if last:
        plan_ref, refs = refs[0], refs[1:]
    start_ref, refs = refs[0], refs[1:]
    if begun:
        norm_ref, refs = refs[0], refs[1:]
    slots = 2 * pieces + 1
    tasks = len(tiles_of)
    own_ref, beside_ref, far_ref, near_ref = refs[:4]
    refs = refs[4:]
    query_refs, refs = dict(zip(groups, refs)), refs[len(groups) :]
    out_refs, lse_ref = refs[:tasks], refs[tasks]
    staged, chosen, norms = refs[tasks + 1 :]
    shard, z = where_ref[0], where_ref[1]
    tiles, stacked, _ = query_refs[groups[0]].shape
    tile = stacked // per_group
    rows = tile * tiles
    odd = lax.rem(shard, 2) == 1
    used = slice(2 * groups[0] * HEAD_DIM, 2 * (groups[-1] + 1) * HEAD_DIM)
    for i in range(1, pieces + 1):

        @pl.when(odd)
        def _():
            before = beside_ref if i == 1 else near_ref.at[i - 2]
            chosen[i - 1, :, used] = before[:, used]

        @pl.when(jnp.logical_not(odd))
        def _():
            chosen[i - 1, :, used] = near_ref[i - 1, :, used]

    def window(group, slot, part):
        place = (2 * group + part) * HEAD_DIM
        cols = slice(place, place + HEAD_DIM)
        back = slots - 1 - slot
        if back == 0:
            return own_ref[:, cols]
        if back % 2 == 0:
            return far_ref[back // 2 - 1, :, cols]
        return chosen[(back + 1) // 2 - 1, :, cols]

    first = shard * rows
    window_first = (shard - (slots - 1)) * rows
    exponent = SCALE * LOG2E
    column = lax.broadcasted_iota(jnp.int32, (tile, HEAD_DIM), 1)
    line = lax.broadcasted_iota(jnp.int32, (tile, HEAD_DIM), 0)
    chunk = min(stacked, 256)
    inside = chunk // tile
    norms[...] = norm_ref[...] if begun else jnp.zeros(norms.shape, jnp.float32)

    def masks_of(t):
        start = start_ref[pl.ds(pl.multiple_of(t * tile, tile), tile), :]
        masks = []
        for slot in range(slots):
            begins = start - (window_first + slot * rows)
            for lane in range(0, rows, HEAD_DIM):
                allowed = column + lane >= begins
                if slot == slots - 1:
                    allowed = allowed & (column + lane <= line + t * tile)
                masks.append(allowed[None])
        return masks

    def scores_of(group, t, c, masks):
        q = query_refs[group][t, c * chunk : (c + 1) * chunk, :]
        parts, best = [], None
        for slot in range(slots):
            block = lax.dot_general(
                q,
                window(group, slot, 0),
                (((1,), (1,)), ((), ())),
                preferred_element_type=jnp.float32,
            )
            for lane in range(0, rows, HEAD_DIM):
                part = block[:, lane : lane + HEAD_DIM].reshape(inside, tile, HEAD_DIM)
                part = jnp.where(masks[len(parts)], part, NEG).reshape(chunk, HEAD_DIM)
                parts.append(part)
                best = part if best is None else jnp.maximum(best, part)
        return parts, best

    def mix(index, c, i, parts, best, gathered):
        group = groups[index]
        top = jnp.max(best, axis=1, keepdims=True) * exponent
        total, mixed = None, None
        per_slot = rows // HEAD_DIM
        for slot in range(slots):
            probs = []
            for part in parts[per_slot * slot : per_slot * (slot + 1)]:
                weights = jnp.exp2(part * exponent - top)
                total = weights if total is None else total + weights
                probs.append(weights.astype(jnp.bfloat16))
            product = jnp.dot(
                jnp.concatenate(probs, axis=1),
                window(group, slot, 1),
                preferred_element_type=jnp.float32,
            )
            mixed = product if mixed is None else mixed + product
        row_sum = jnp.sum(total, axis=1, keepdims=True)
        result = (mixed / row_sum).astype(jnp.bfloat16)
        norm = top * (1.0 / LOG2E) + jnp.log(row_sum)
        for h in range(inside):
            head = c * inside + h
            part = slice(h * tile, (h + 1) * tile)
            column_of = (index * per_group + head) * HEAD_DIM
            staged[i, :, column_of : column_of + HEAD_DIM] = result[part]
            gathered = jnp.where(column == group * per_group + head, norm[part], gathered)
        return gathered

    def step(i, carry):
        t = lax.rem(z + tiles_of.start + i * tiles_of.step, tiles)
        here = pl.ds(pl.multiple_of(t * tile, tile), tile)
        gathered = norms[here, :]
        masks = masks_of(t)
        jobs = [(index, c) for index in range(len(groups)) for c in range(stacked // chunk)]
        ready = scores_of(groups[0], t, 0, masks)
        for job, (index, c) in enumerate(jobs):
            following = None
            if job + 1 < len(jobs):
                next_index, next_c = jobs[job + 1]
                following = scores_of(groups[next_index], t, next_c, masks)
            gathered = mix(index, c, i, *ready, gathered)
            ready = following
        norms[here, :] = gathered
        return carry

    lax.fori_loop(0, len(tiles_of), step, 0, unroll=slots <= 5)

    for position, out_ref in enumerate(out_refs):
        out_ref[...] = staged[position]
    if last:
        shards = plan_ref.shape[0]
        block = rows // shards
        for s in range(shards):
            picked = pl.multiple_of(plan_ref[shard, s] * block, block)
            lse_ref[s * block : (s + 1) * block, :] = norms[pl.ds(picked, block), :]
    else:
        lse_ref[...] = norms[...]


def assemble_kernel(planes, width, groups, places, where_ref, served_ref, *refs):
    pieces, out_ref, lse_hbm, lse_ref, sems = refs[:-4], *refs[-4:]
    z = where_ref[1]
    copies = []
    for index, (s, group) in enumerate(places):
        origin = lax.rem(z - s + planes, planes)
        column = pl.multiple_of((origin * groups + group) * width, width)
        target = out_ref.at[:, pl.ds(column, pieces[index].shape[1])]
        copies.append(pltpu.make_async_copy(pieces[index], target, sems.at[index]))
    for c in copies:
        c.start()
    lse_ref[...] = served_ref[...].T[: lse_ref.shape[0]]
    lse_copy = pltpu.make_async_copy(lse_ref, lse_hbm, sems.at[len(pieces)])
    lse_copy.start()
    for c in copies:
        c.wait()
    lse_copy.wait()


def body(queries, key_states, value_states, doc_lengths, block_plan):
    shards = lax.axis_size("tok")
    planes = lax.axis_size("kv")
    shard = lax.axis_index("tok")
    z = lax.axis_index("kv")
    rows = queries.shape[0]
    groups = key_states.shape[1] // HEAD_DIM
    heads = queries.shape[1] // HEAD_DIM
    per_group = heads // groups
    tile = rows // planes
    pieces = shards // 4
    where = jnp.stack([shard, z]).astype(jnp.int32)
    half_freq = THETA ** (-np.arange(HALF, dtype=np.float64) * 2.0 / HEAD_DIM)
    freq = jnp.asarray(np.concatenate([half_freq, half_freq])[None, :], jnp.float32)

    pair = [(i, i ^ 1) for i in range(shards)]
    to_odd = [(i, i + 1) for i in range(0, shards, 2)]
    arrived = [
        [
            lax.ppermute(x, "tok", [(i, i + 2 * p) for i in range(shards - 2 * p)])
            for p in range(1, pieces + 1)
        ]
        for x in (key_states, value_states)
    ]
    pack_shape = jax.ShapeDtypeStruct((rows, 2 * groups * HEAD_DIM), jnp.bfloat16)
    with jax.named_scope("rotate"):
        result = pl.pallas_call(
            partial(queries_kernel, pieces),
            out_shape=[
                pack_shape,
                jax.ShapeDtypeStruct((rows, HEAD_DIM), jnp.int32),
                jax.ShapeDtypeStruct((2 * pieces, rows, HEAD_DIM), jnp.float32),
            ]
            + [jax.ShapeDtypeStruct((planes, per_group * tile, HEAD_DIM), jnp.bfloat16)] * groups,
            in_specs=[smem(), smem(), vmem(), hbm(), hbm(), hbm()],
            out_specs=[vmem()] * (3 + groups),
            scratch_shapes=[
                pltpu.VMEM(key_states.shape, jnp.bfloat16),
                pltpu.VMEM(value_states.shape, jnp.bfloat16),
                pltpu.VMEM(queries.shape, jnp.bfloat16),
                pltpu.SemaphoreType.DMA((3,)),
            ],
            compiler_params=params(),
            cost_estimate=cost(3.0),
        )(
            where,
            doc_lengths,
            freq,
            pltpu.with_memory_space_constraint(key_states, pltpu.HBM),
            pltpu.with_memory_space_constraint(value_states, pltpu.HBM),
            pltpu.with_memory_space_constraint(queries, pltpu.HBM),
        )
    own, start, tables = result[:3]
    turned = result[3:]
    beside = lax.ppermute(own, "tok", to_odd)
    tables, beside = lax.optimization_barrier((tables, beside))
    with jax.named_scope("pack"):
        far = pl.pallas_call(
            pack_kernel,
            out_shape=jax.ShapeDtypeStruct((pieces, *pack_shape.shape), jnp.bfloat16),
            in_specs=[vmem()] * (1 + 2 * pieces),
            out_specs=vmem(),
            compiler_params=params(),
            cost_estimate=cost(1.0),
        )(tables, *arrived[0], *arrived[1])
    near = lax.ppermute(far, "tok", pair)

    def attend(norm, used, tiles_of, last, microseconds):
        scalars = [where, block_plan] if last else [where]
        operands = [start] if norm is None else [start, norm]
        operands += [own, beside, far, near] + [turned[group] for group in used]
        tasks = len(tiles_of)
        width = len(used) * per_group * HEAD_DIM
        with jax.named_scope("attend"):
            result = pl.pallas_call(
                partial(
                    attend_kernel, pieces, per_group, used, tiles_of, norm is not None, last
                ),
                out_shape=[jax.ShapeDtypeStruct((tile, width), jnp.bfloat16)]
                * tasks
                + [jax.ShapeDtypeStruct((rows, HEAD_DIM), jnp.float32)],
                in_specs=[smem()] * len(scalars) + [vmem()] * len(operands),
                out_specs=[vmem()] * (tasks + 1),
                scratch_shapes=[
                    pltpu.VMEM((tasks, tile, width), jnp.bfloat16),
                    pltpu.VMEM((pieces, *pack_shape.shape), jnp.bfloat16),
                    pltpu.VMEM((rows, HEAD_DIM), jnp.float32),
                ],
                compiler_params=params(),
                cost_estimate=cost(microseconds),
            )(*scalars, *operands)
        return result[:tasks], result[tasks]

    def send(piece, s):
        return lax.ppermute(piece, "kv", [(i, (i + s) % planes) for i in range(planes)])

    norm, pieces_of = None, {}
    for group in range(groups):
        span = range(1, planes)
        result, norm = attend(norm, [group], span, False, 2.0 * len(span))
        for s, piece in zip(span, result):
            pieces_of[s, group] = send(piece, s)
    (piece,), norm = attend(norm, list(range(groups)), range(1), True, 4.0)
    pieces_of[0, 0] = piece
    block_rows = rows // shards
    served = lax.all_to_all(
        norm.reshape(shards, block_rows, HEAD_DIM), "tok", split_axis=0, concat_axis=0, tiled=True
    ).reshape(rows, HEAD_DIM)
    places = sorted(pieces_of)
    flat = [pieces_of[place] for place in places]
    with jax.named_scope("assemble"):
        attention_out, served_lse = pl.pallas_call(
            partial(assemble_kernel, planes, per_group * HEAD_DIM, groups, places),
            out_shape=[
                jax.ShapeDtypeStruct((tile, planes * heads * HEAD_DIM), jnp.bfloat16),
                jax.ShapeDtypeStruct((heads, rows), jnp.float32),
            ],
            in_specs=[smem(), vmem()] + [hbm()] * len(flat),
            out_specs=[hbm(), hbm()],
            scratch_shapes=[
                pltpu.VMEM((heads, rows), jnp.float32),
                pltpu.SemaphoreType.DMA((len(flat) + 1,)),
            ],
            compiler_params=params(),
        )(where, served, *flat)
    return (attention_out, served_lse)


def solution(mesh):
    return jax.shard_map(
        body,
        mesh=mesh,
        in_specs=(P("tok", "kv"), P("tok", "kv"), P("tok", "kv"), P(), P()),
        out_specs=(P(("tok", "kv"), None), P("kv", "tok")),
        check_vma=False,
    )
```

profile of v0, /device:TPU:0, one launch (start us, length us, event | category | flops | bytes accessed | tf_op | source)
XLA Modules:
  0.0 56.8 jit_solution(16588105898826139840)
XLA Ops:
  0.6 0.0 copy-start.1
  0.6 0.0 copy-start.2
  0.7 0.1 pad_add_fusion.where_ref
  0.7 0.6 copy-done.1
  1.3 0.0 copy-done.2
  1.3 0.0 copy-start.3
  1.3 0.0 copy-start.4
  1.3 3.7 %rotate.1 = (bf16[256,512]{1,0:T(8,128)(2,1)S(1)}, s32[256,128]{1,0:T(8,128)S(1)}, f32[4,256,128]{2,1,0:T(8,128)S(1)}, bf16[4,512,128]{2,1,0:T(8,128)(2,1)S(1)}, bf16[4,512,128]{2,1,0:T(8,128)(2,1)S(1)}) custom-call(s32[2]{0:T(128)S(1)} %pad_add_fusion.where_ref, s32[16]{0:T(128)S(1)} %copy-done.1, f32[1,128]{1,0:T(1,128)S(1)} %copy-done.2, ...), custom_call_target="tpu_custom_call" | custom-call | flops 3449999872 | tf_op jit(solution)/shard_map/rotate/pallas_call | solution.py:306
  5.0 2.4 %collective-permute-start = (bf16[256,512]{1,0:T(8,128)(2,1)S(1)}, bf16[256,512]{1,0:T(8,128)(2,1)S(1)}, u32[]{:S(2)}, u32[]{:S(2)}) collective-permute-start(bf16[256,512]{1,0:T(8,128)(2,1)S(1)} %get-tuple-element.20.refs_1_.refs_2_.refs_3_), channel_id=1, source_target_pairs={{0,4},{8,12},{16,20},{24,28},{1,5},{9,13},{17,21},{25,29},{2,6},{1... | collective-permute-start | bytes 786440 | tf_op jit(solution)/shard_map/ppermute | solution.py:334
  7.4 0.0 copy-done.3
  7.4 4.3 %collective-permute-start.2 = (bf16[256,256]{1,0:T(8,128)(2,1)S(1)}, bf16[256,256]{1,0:T(8,128)(2,1)S(1)}, u32[]{:S(2)}, u32[]{:S(2)}) collective-permute-start(bf16[256,256]{1,0:T(8,128)(2,1)S(1)} %copy-done.3), channel_id=1, source_target_pairs={{0,16},{4,20},{8,24},{12,28},{1,17},{5,21},{9,25},{13,29},{2,18},{... | collective-permute-start | bytes 393224 | tf_op jit(solution)/shard_map/ppermute | solution.py:299
  11.7 3.4 %collective-permute-start.1 = (bf16[256,256]{1,0:T(8,128)(2,1)S(1)}, bf16[256,256]{1,0:T(8,128)(2,1)S(1)}, u32[]{:S(2)}, u32[]{:S(2)}) collective-permute-start(bf16[256,256]{1,0:T(8,128)(2,1)S(1)} %copy-done.3), channel_id=1, source_target_pairs={{0,8},{4,12},{8,16},{12,20},{16,24},{20,28},{1,9},{5,13},{9,17},{1... | collective-permute-start | bytes 393224 | tf_op jit(solution)/shard_map/ppermute | solution.py:299
  15.1 0.0 copy-done.4
  15.1 1.3 %collective-permute-start.4 = (bf16[256,256]{1,0:T(8,128)(2,1)S(1)}, bf16[256,256]{1,0:T(8,128)(2,1)S(1)}, u32[]{:S(2)}, u32[]{:S(2)}) collective-permute-start(bf16[256,256]{1,0:T(8,128)(2,1)S(1)} %copy-done.4), channel_id=1, source_target_pairs={{0,16},{4,20},{8,24},{12,28},{1,17},{5,21},{9,25},{13,29},{2,18},{... | collective-permute-start | bytes 393224 | tf_op jit(solution)/shard_map/ppermute | solution.py:299
  16.4 1.9 %collective-permute-start.3 = (bf16[256,256]{1,0:T(8,128)(2,1)S(1)}, bf16[256,256]{1,0:T(8,128)(2,1)S(1)}, u32[]{:S(2)}, u32[]{:S(2)}) collective-permute-start(bf16[256,256]{1,0:T(8,128)(2,1)S(1)} %copy-done.4), channel_id=1, source_target_pairs={{0,8},{4,12},{8,16},{12,20},{16,24},{20,28},{1,9},{5,13},{9,17},{1... | collective-permute-start | bytes 393224 | tf_op jit(solution)/shard_map/ppermute | solution.py:299
  18.3 0.0 collective-permute-done.refs_2_.refs_3_.refs_4_
  18.4 0.0 collective-permute-done.2.refs_1_
  18.4 0.0 collective-permute-done.1.refs_0_
  18.4 4.2 %collective-permute-done.4.refs_3_ = bf16[256,256]{1,0:T(8,128)(2,1)S(1)} collective-permute-done((bf16[256,256]{1,0:T(8,128)(2,1)S(1)}, bf16[256,256]{1,0:T(8,128)(2,1)S(1)}, u32[]{:S(2)}, u32[]{:S(2)}) %collective-permute-start.4) | collective-permute-done | bytes 131104 | tf_op jit(solution)/shard_map/ppermute | solution.py:299
  22.6 0.0 collective-permute-done.3.refs_2_
  22.6 0.2 pack.1.refs_3_.refs_4_.refs_5_
  22.8 0.1 collective-permute-start.5
  22.9 1.9 %collective-permute-done.5.refs_4_.refs_5_.refs_6_ = bf16[2,256,512]{2,1,0:T(8,128)(2,1)S(1)} collective-permute-done((bf16[2,256,512]{2,1,0:T(8,128)(2,1)S(1)}, bf16[2,256,512]{2,1,0:T(8,128)(2,1)S(1)}, u32[]{:S(2)}, u32[]{:S(2)}) %collective-permute-start.5) | collective-permute-done | bytes 524320 | tf_op jit(solution)/shard_map/ppermute | solution.py:345
  24.8 4.2 %attend.3 = (bf16[64,1024]{1,0:T(8,128)(2,1)S(1)}, bf16[64,1024]{1,0:T(8,128)(2,1)S(1)}, bf16[64,1024]{1,0:T(8,128)(2,1)S(1)}, f32[256,128]{1,0:T(8,128)S(1)}) custom-call(s32[2]{0:T(128)S(1)} %pad_add_fusion.where_ref, s32[256,128]{1,0:T(8,128)S(1)} %get-tuple-element.19.refs_0_.refs_1_, bf16[256,512]{1,0:T(8,128)(2,1)S(1)} %get-tuple-element.20.refs_1_.refs_2_.refs_3_, ...), custom_call_target="tpu_custom_call" | custom-call | flops 6899999744 | tf_op jit(solution)/shard_map/attend/pallas_call | solution.py:354
  29.0 1.6 %collective-permute-start.6 = (bf16[64,1024]{1,0:T(8,128)(2,1)S(1)}, bf16[64,1024]{1,0:T(8,128)(2,1)S(1)}, u32[]{:S(2)}, u32[]{:S(2)}) collective-permute-start(bf16[64,1024]{1,0:T(8,128)(2,1)S(1)} %get-tuple-element.30), channel_id=1, source_target_pairs={{0,1},{1,2},{2,3},{3,0},{4,5},{5,6},{6,7},{7,4},{8,9},{9,10},{10,1... | collective-permute-start | bytes 393224 | tf_op jit(solution)/shard_map/ppermute | solution.py:374
  30.6 2.6 %collective-permute-start.8 = (bf16[64,1024]{1,0:T(8,128)(2,1)S(1)}, bf16[64,1024]{1,0:T(8,128)(2,1)S(1)}, u32[]{:S(2)}, u32[]{:S(2)}) collective-permute-start(bf16[64,1024]{1,0:T(8,128)(2,1)S(1)} %get-tuple-element.32), channel_id=1, source_target_pairs={{0,2},{1,3},{2,0},{3,1},{4,6},{5,7},{6,4},{7,5},{8,10},{9,11},{10,... | collective-permute-start | bytes 393224 | tf_op jit(solution)/shard_map/ppermute | solution.py:374
  33.2 1.3 %collective-permute-start.10 = (bf16[64,1024]{1,0:T(8,128)(2,1)S(1)}, bf16[64,1024]{1,0:T(8,128)(2,1)S(1)}, u32[]{:S(2)}, u32[]{:S(2)}) collective-permute-start(bf16[64,1024]{1,0:T(8,128)(2,1)S(1)} %get-tuple-element.34), channel_id=1, source_target_pairs={{0,3},{1,0},{2,1},{3,2},{4,7},{5,4},{6,5},{7,6},{8,11},{9,8},{10,9... | collective-permute-start | bytes 393224 | tf_op jit(solution)/shard_map/ppermute | solution.py:374
  34.5 4.2 %attend.4 = (bf16[64,1024]{1,0:T(8,128)(2,1)S(1)}, bf16[64,1024]{1,0:T(8,128)(2,1)S(1)}, bf16[64,1024]{1,0:T(8,128)(2,1)S(1)}, f32[256,128]{1,0:T(8,128)S(1)}) custom-call(s32[2]{0:T(128)S(1)} %pad_add_fusion.where_ref, s32[256,128]{1,0:T(8,128)S(1)} %get-tuple-element.19.refs_0_.refs_1_, f32[256,128]{1,0:T(8,128)S(1)} %get-tuple-element.25.refs_1_, ...), custom_call_target="tpu_custom_call" | custom-call | flops 6899999744 | tf_op jit(solution)/shard_map/attend/pallas_call | solution.py:354
  38.7 0.0 copy-start
  38.7 0.7 %collective-permute-start.7 = (bf16[64,1024]{1,0:T(8,128)(2,1)S(1)}, bf16[64,1024]{1,0:T(8,128)(2,1)S(1)}, u32[]{:S(2)}, u32[]{:S(2)}) collective-permute-start(bf16[64,1024]{1,0:T(8,128)(2,1)S(1)} %get-tuple-element.31), channel_id=1, source_target_pairs={{0,1},{1,2},{2,3},{3,0},{4,5},{5,6},{6,7},{7,4},{8,9},{9,10},{10,1... | collective-permute-start | bytes 393224 | tf_op jit(solution)/shard_map/ppermute | solution.py:374
  39.5 0.3 collective-permute-start.9
  39.8 0.0 collective-permute-done.6.refs_1_
  39.8 2.8 %collective-permute-start.11 = (bf16[64,1024]{1,0:T(8,128)(2,1)S(1)}, bf16[64,1024]{1,0:T(8,128)(2,1)S(1)}, u32[]{:S(2)}, u32[]{:S(2)}) collective-permute-start(bf16[64,1024]{1,0:T(8,128)(2,1)S(1)} %get-tuple-element.35), channel_id=1, source_target_pairs={{0,3},{1,0},{2,1},{3,2},{4,7},{5,4},{6,5},{7,6},{8,11},{9,8},{10,9... | collective-permute-start | bytes 393224 | tf_op jit(solution)/shard_map/ppermute | solution.py:374
  42.6 0.0 copy-done
  42.6 3.4 %attend.5 = (bf16[64,2048]{1,0:T(8,128)(2,1)S(1)}, f32[256,128]{1,0:T(8,128)S(1)}) custom-call(s32[2]{0:T(128)S(1)} %pad_add_fusion.where_ref, s32[8,8]{1,0:T(8,128)S(1)} %copy-done, s32[256,128]{1,0:T(8,128)S(1)} %get-tuple-element.19.refs_0_.refs_1_, f32[256,128]{1,0:T(8,128)S(1)} %get-tuple-element.27.refs_2_, ...), custom_call_target="tpu_custom_call" | custom-call | flops 4600000000 | tf_op jit(solution)/shard_map/attend/pallas_call | solution.py:354
  46.0 9.1 %all_to_all.5 = f32[8,32,128]{2,1,0:T(8,128)S(1)} all-to-all(f32[8,32,128]{2,1,0:T(8,128)S(1)} %bitcast.5), channel_id=1, replica_groups=mesh['tok'=8,'kv'=4] {'tok'}, dimensions={0} | all-to-all | bytes 262144 | tf_op jit(solution)/shard_map/all_to_all | solution.py:385
  55.1 0.0 collective-permute-done.8.refs_3_
  55.1 0.0 collective-permute-done.10.refs_5_
  55.1 0.0 collective-permute-done.7.refs_2_
  55.1 0.0 collective-permute-done.9.refs_4_
  55.1 0.0 collective-permute-done.11.refs_6_
  55.1 1.6 %assemble.1 = (bf16[64,8192]{1,0:T(8,128)(2,1)}, f32[16,256]{1,0:T(8,128)}) custom-call(s32[2]{0:T(128)S(1)} %pad_add_fusion.where_ref, f32[256,128]{1,0:T(8,128)S(1)} %bitcast.4, bf16[64,2048]{1,0:T(8,128)(2,1)S(1)} %get-tuple-element.29.refs_0_, bf16[64,1024]{1,0:T(8,128)(2,1)S(1)} %collective-permute-done.6.refs_1_, ...), custom_call_target="tpu_custom_call" | custom-call | tf_op jit(solution)/shard_map/assemble/pallas_call | solution.py:391
Async XLA Ops:
  0.6 0.7 %copy-start.1 = (s32[16]{0:T(128)S(1)}, s32[16]{0:T(128)}, u32[]{:S(2)}) copy-start(s32[16]{0:T(128)} %lengths_ref.1) | copy-start | bytes 196
  0.6 0.7 %copy-start.2 = (f32[1,128]{1,0:T(1,128)S(1)}, f32[1,128]{1,0:T(1,128)}, u32[]{:S(2)}) copy-start(f32[1,128]{1,0:T(1,128)} %constant.11.clone.freq_ref) | copy-start | bytes 1540
  1.3 6.1 %copy-start.3 = (bf16[256,256]{1,0:T(8,128)(2,1)S(1)}, bf16[256,256]{1,0:T(8,128)(2,1)}, u32[]{:S(2)}) copy-start(bf16[256,256]{1,0:T(8,128)(2,1)} %key_hbm.1) | copy-start | bytes 393220
  1.3 13.8 %copy-start.4 = (bf16[256,256]{1,0:T(8,128)(2,1)S(1)}, bf16[256,256]{1,0:T(8,128)(2,1)}, u32[]{:S(2)}) copy-start(bf16[256,256]{1,0:T(8,128)(2,1)} %value_hbm.1) | copy-start | bytes 393220
  5.0 13.3 %collective-permute-start = (bf16[256,512]{1,0:T(8,128)(2,1)S(1)}, bf16[256,512]{1,0:T(8,128)(2,1)S(1)}, u32[]{:S(2)}, u32[]{:S(2)}) collective-permute-start(bf16[256,512]{1,0:T(8,128)(2,1)S(1)} %get-tuple-element.20.refs_1_.refs_2_.refs_3_), channel_id=1, source_target_pairs={{0,4},{8,12},{16,20},{24,28},{1,5},{9,13},{17,21},{25,29},{2,6},{1... | collective-permute-start | bytes 786440 | tf_op jit(solution)/shard_map/ppermute | solution.py:334
  7.4 10.9 %collective-permute-start.2 = (bf16[256,256]{1,0:T(8,128)(2,1)S(1)}, bf16[256,256]{1,0:T(8,128)(2,1)S(1)}, u32[]{:S(2)}, u32[]{:S(2)}) collective-permute-start(bf16[256,256]{1,0:T(8,128)(2,1)S(1)} %copy-done.3), channel_id=1, source_target_pairs={{0,16},{4,20},{8,24},{12,28},{1,17},{5,21},{9,25},{13,29},{2,18},{... | collective-permute-start | bytes 393224 | tf_op jit(solution)/shard_map/ppermute | solution.py:299
  11.7 6.7 %collective-permute-start.1 = (bf16[256,256]{1,0:T(8,128)(2,1)S(1)}, bf16[256,256]{1,0:T(8,128)(2,1)S(1)}, u32[]{:S(2)}, u32[]{:S(2)}) collective-permute-start(bf16[256,256]{1,0:T(8,128)(2,1)S(1)} %copy-done.3), channel_id=1, source_target_pairs={{0,8},{4,12},{8,16},{12,20},{16,24},{20,28},{1,9},{5,13},{9,17},{1... | collective-permute-start | bytes 393224 | tf_op jit(solution)/shard_map/ppermute | solution.py:299
  15.1 7.5 %collective-permute-start.4 = (bf16[256,256]{1,0:T(8,128)(2,1)S(1)}, bf16[256,256]{1,0:T(8,128)(2,1)S(1)}, u32[]{:S(2)}, u32[]{:S(2)}) collective-permute-start(bf16[256,256]{1,0:T(8,128)(2,1)S(1)} %copy-done.4), channel_id=1, source_target_pairs={{0,16},{4,20},{8,24},{12,28},{1,17},{5,21},{9,25},{13,29},{2,18},{... | collective-permute-start | bytes 393224 | tf_op jit(solution)/shard_map/ppermute | solution.py:299
  16.4 6.2 %collective-permute-start.3 = (bf16[256,256]{1,0:T(8,128)(2,1)S(1)}, bf16[256,256]{1,0:T(8,128)(2,1)S(1)}, u32[]{:S(2)}, u32[]{:S(2)}) collective-permute-start(bf16[256,256]{1,0:T(8,128)(2,1)S(1)} %copy-done.4), channel_id=1, source_target_pairs={{0,8},{4,12},{8,16},{12,20},{16,24},{20,28},{1,9},{5,13},{9,17},{1... | collective-permute-start | bytes 393224 | tf_op jit(solution)/shard_map/ppermute | solution.py:299
  22.8 2.0 %collective-permute-start.5 = (bf16[2,256,512]{2,1,0:T(8,128)(2,1)S(1)}, bf16[2,256,512]{2,1,0:T(8,128)(2,1)S(1)}, u32[]{:S(2)}, u32[]{:S(2)}) collective-permute-start(bf16[2,256,512]{2,1,0:T(8,128)(2,1)S(1)} %pack.1.refs_3_.refs_4_.refs_5_), channel_id=1, source_target_pairs={{0,4},{4,0},{8,12},{12,8},{16,20},{20,16},{24,28},{28,24},{1,5},{5... | collective-permute-start | bytes 1572872 | tf_op jit(solution)/shard_map/ppermute | solution.py:345
  29.0 10.8 %collective-permute-start.6 = (bf16[64,1024]{1,0:T(8,128)(2,1)S(1)}, bf16[64,1024]{1,0:T(8,128)(2,1)S(1)}, u32[]{:S(2)}, u32[]{:S(2)}) collective-permute-start(bf16[64,1024]{1,0:T(8,128)(2,1)S(1)} %get-tuple-element.30), channel_id=1, source_target_pairs={{0,1},{1,2},{2,3},{3,0},{4,5},{5,6},{6,7},{7,4},{8,9},{9,10},{10,1... | collective-permute-start | bytes 393224 | tf_op jit(solution)/shard_map/ppermute | solution.py:374
  30.6 24.5 %collective-permute-start.8 = (bf16[64,1024]{1,0:T(8,128)(2,1)S(1)}, bf16[64,1024]{1,0:T(8,128)(2,1)S(1)}, u32[]{:S(2)}, u32[]{:S(2)}) collective-permute-start(bf16[64,1024]{1,0:T(8,128)(2,1)S(1)} %get-tuple-element.32), channel_id=1, source_target_pairs={{0,2},{1,3},{2,0},{3,1},{4,6},{5,7},{6,4},{7,5},{8,10},{9,11},{10,... | collective-permute-start | bytes 393224 | tf_op jit(solution)/shard_map/ppermute | solution.py:374
  33.2 21.9 %collective-permute-start.10 = (bf16[64,1024]{1,0:T(8,128)(2,1)S(1)}, bf16[64,1024]{1,0:T(8,128)(2,1)S(1)}, u32[]{:S(2)}, u32[]{:S(2)}) collective-permute-start(bf16[64,1024]{1,0:T(8,128)(2,1)S(1)} %get-tuple-element.34), channel_id=1, source_target_pairs={{0,3},{1,0},{2,1},{3,2},{4,7},{5,4},{6,5},{7,6},{8,11},{9,8},{10,9... | collective-permute-start | bytes 393224 | tf_op jit(solution)/shard_map/ppermute | solution.py:374
  38.7 3.9 %copy-start = (s32[8,8]{1,0:T(8,128)S(1)}, s32[8,8]{1,0:T(8,128)}, u32[]{:S(2)}) copy-start(s32[8,8]{1,0:T(8,128)} %refs_0_.1) | copy-start | bytes 772
  38.7 16.3 %collective-permute-start.7 = (bf16[64,1024]{1,0:T(8,128)(2,1)S(1)}, bf16[64,1024]{1,0:T(8,128)(2,1)S(1)}, u32[]{:S(2)}, u32[]{:S(2)}) collective-permute-start(bf16[64,1024]{1,0:T(8,128)(2,1)S(1)} %get-tuple-element.31), channel_id=1, source_target_pairs={{0,1},{1,2},{2,3},{3,0},{4,5},{5,6},{6,7},{7,4},{8,9},{9,10},{10,1... | collective-permute-start | bytes 393224 | tf_op jit(solution)/shard_map/ppermute | solution.py:374
  39.5 15.6 %collective-permute-start.9 = (bf16[64,1024]{1,0:T(8,128)(2,1)S(1)}, bf16[64,1024]{1,0:T(8,128)(2,1)S(1)}, u32[]{:S(2)}, u32[]{:S(2)}) collective-permute-start(bf16[64,1024]{1,0:T(8,128)(2,1)S(1)} %get-tuple-element.33), channel_id=1, source_target_pairs={{0,2},{1,3},{2,0},{3,1},{4,6},{5,7},{6,4},{7,5},{8,10},{9,11},{10,... | collective-permute-start | bytes 393224 | tf_op jit(solution)/shard_map/ppermute | solution.py:374
  39.8 15.3 %collective-permute-start.11 = (bf16[64,1024]{1,0:T(8,128)(2,1)S(1)}, bf16[64,1024]{1,0:T(8,128)(2,1)S(1)}, u32[]{:S(2)}, u32[]{:S(2)}) collective-permute-start(bf16[64,1024]{1,0:T(8,128)(2,1)S(1)} %get-tuple-element.35), channel_id=1, source_target_pairs={{0,3},{1,0},{2,1},{3,2},{4,7},{5,4},{6,5},{7,6},{8,11},{9,8},{10,9... | collective-permute-start | bytes 393224 | tf_op jit(solution)/shard_map/ppermute | solution.py:374
where the time goes:
time: 57.1 us; the launch traced here: 56.8 us
  starting transfers between devices  22.8 us (40%)
  Pallas kernels  17.2 us (30%)
  blocking collectives  9.09 us (16%)
  waiting for transfers between devices  6.16 us (11%)
  between operations  0.96 us (2%)
  local copies, waits for them, and re-layouts  0.59 us (1%)
    pallas_call x3, Pallas kernels, attend(): pl.pallas_call(partial(attend_kernel, pieces, per_group, used, tiles_of,...  11.7 us
    ppermute x4, starting transfers between devices, body(): lax.ppermute(x, 'tok', [(i, i + 2 * p) for i in range(shards - 2 * p)])  10.9 us
    ppermute x6, starting transfers between devices, send(): lax.ppermute(piece, 'kv', [(i, (i + s) % planes) for i in range(planes)])  9.44 us
    all_to_all x1, blocking collectives, body(): lax.all_to_all(norm.reshape(shards, block_rows, HEAD_DIM), 'tok', split_a...  9.09 us
    ppermute x4, waiting for transfers between devices, body(): lax.ppermute(x, 'tok', [(i, i + 2 * p) for i in range(shards - 2 * p)])  4.25 us
    pallas_call x1, Pallas kernels, body(): pl.pallas_call(partial(queries_kernel, pieces), out_shape=[pack_shape, ja...  3.72 us
    ppermute x1, starting transfers between devices, body(): beside = lax.ppermute(own, 'tok', to_odd)  2.37 us
    ppermute x1, waiting for transfers between devices, body(): near = lax.ppermute(far, 'tok', pair)  1.9 us
  transfers between devices with their start and end apart: 12, of which 2 were waited for; matrix products, arithmetic and copies ran while one was open for 0% of the time, Pallas kernels for 13%

commit v1 on v0

--- a/solution.py
+++ b/solution.py
@@ -74,24 +74,32 @@
         out_ref[:, place + HEAD_DIM : place + 2 * HEAD_DIM] = value_ref[:, cols]
 
 
-def queries_kernel(pieces, where_ref, lengths_ref, freq_ref, key_hbm, value_hbm, query_hbm, *refs):
+def queries_kernel(pieces, lengths_hbm, freq_hbm, key_hbm, value_hbm, query_hbm, *refs):
     pack_ref, start_ref, table_ref = refs[:3]
-    turn_refs = refs[3:-4]
-    key_ref, value_ref, query_ref, sems = refs[-4:]
+    turn_refs = refs[3:-6]
+    lengths_ref, freq_ref, key_ref, value_ref, query_ref, sems = refs[-6:]
     copies = [
         pltpu.make_async_copy(key_hbm, key_ref, sems.at[0]),
         pltpu.make_async_copy(value_hbm, value_ref, sems.at[1]),
         pltpu.make_async_copy(query_hbm, query_ref, sems.at[2]),
+        pltpu.make_async_copy(lengths_hbm, lengths_ref, sems.at[3]),
+        pltpu.make_async_copy(freq_hbm, freq_ref, sems.at[4]),
     ]
-    for c in copies:
+    for c in copies[::-1]:
         c.start()
+    for c in copies[3:]:
+        c.wait()
     rows = query_ref.shape[0]
-    shard = where_ref[0]
+    shard = lax.axis_index("tok")
     cosine, sine, start = rotary_tables(lengths_ref, freq_ref, rows, shard * rows)
     start_ref[...] = start
     for c in copies[:2]:
         c.wait()
     pack(pack_ref, key_ref, value_ref, cosine, sine)
+    for p in range(1, pieces + 1):
+        far_cosine, far_sine, _ = rotary_tables(lengths_ref, freq_ref, rows, (shard - 2 * p) * rows)
+        table_ref[2 * p - 2] = far_cosine
+        table_ref[2 * p - 1] = far_sine
     copies[2].wait()
     tiles, stacked, _ = turn_refs[0].shape
     tile = rows // tiles
@@ -102,64 +110,58 @@
             turned = turn(query_ref[:, cols], cosine, sine)
             for t in range(tiles):
                 out_ref[t, head * tile : (head + 1) * tile, :] = turned[t * tile : (t + 1) * tile]
-    for p in range(1, pieces + 1):
-        cosine, sine, _ = rotary_tables(lengths_ref, freq_ref, rows, (shard - 2 * p) * rows)
-        table_ref[2 * p - 2] = cosine
-        table_ref[2 * p - 1] = sine
-
-
-def pack_kernel(table_ref, *refs):
-    pieces = len(refs) // 2
+
+
+def pack_kernel(pieces, table_ref, own_ref, *refs):
+    mine_ref, give_ref = refs[-2:]
+    relayed = refs[2 * pieces : -2]
+    shard = lax.axis_index("tok")
+    mine_ref[0] = own_ref[...]
     for p in range(pieces):
+        keys = refs[p][...]
+        if relayed and not p:
+            keys = jnp.where(shard // 2 == 2, relayed[0][...], keys)
         pack(
-            refs[2 * pieces].at[p],
-            refs[p],
-            refs[pieces + p],
+            mine_ref.at[p + 1],
+            keys,
+            refs[pieces + p][...],
             table_ref[2 * p],
             table_ref[2 * p + 1],
         )
-
-
-def attend_kernel(pieces, per_group, groups, tiles_of, begun, last, where_ref, *refs):
-    plan_ref = norm_ref = None
+    odd = lax.rem(shard, 2)
+    for p in range(pieces):
+        give_ref[p] = mine_ref[p + odd]
+
+
+def attend_kernel(pieces, per_group, groups, tiles_of, begun, last, *refs):
+    norm_ref = None
     if last:
-        plan_ref, refs = refs[0], refs[1:]
+        plan_hbm, refs = refs[0], refs[1:]
+        plan_ref, plan_sem = refs[-2:]
+        refs = refs[:-2]
+        plan_copy = pltpu.make_async_copy(plan_hbm, plan_ref, plan_sem.at[0])
+        plan_copy.start()
     start_ref, refs = refs[0], refs[1:]
     if begun:
         norm_ref, refs = refs[0], refs[1:]
     slots = 2 * pieces + 1
     tasks = len(tiles_of)
-    own_ref, beside_ref, far_ref, near_ref = refs[:4]
-    refs = refs[4:]
+    mine_ref, theirs_ref = refs[:2]
+    refs = refs[2:]
     query_refs, refs = dict(zip(groups, refs)), refs[len(groups) :]
     out_refs, lse_ref = refs[:tasks], refs[tasks]
-    staged, chosen, norms = refs[tasks + 1 :]
-    shard, z = where_ref[0], where_ref[1]
+    staged, norms = refs[tasks + 1 :]
+    shard, z = lax.axis_index("tok"), lax.axis_index("kv")
     tiles, stacked, _ = query_refs[groups[0]].shape
     tile = stacked // per_group
     rows = tile * tiles
-    odd = lax.rem(shard, 2) == 1
-    used = slice(2 * groups[0] * HEAD_DIM, 2 * (groups[-1] + 1) * HEAD_DIM)
-    for i in range(1, pieces + 1):
-
-        @pl.when(odd)
-        def _():
-            before = beside_ref if i == 1 else near_ref.at[i - 2]
-            chosen[i - 1, :, used] = before[:, used]
-
-        @pl.when(jnp.logical_not(odd))
-        def _():
-            chosen[i - 1, :, used] = near_ref[i - 1, :, used]
-
     def window(group, slot, part):
         place = (2 * group + part) * HEAD_DIM
         cols = slice(place, place + HEAD_DIM)
         back = slots - 1 - slot
-        if back == 0:
-            return own_ref[:, cols]
         if back % 2 == 0:
-            return far_ref[back // 2 - 1, :, cols]
-        return chosen[(back + 1) // 2 - 1, :, cols]
+            return mine_ref[back // 2, :, cols]
+        return theirs_ref[back // 2, :, cols]
 
     first = shard * rows
     window_first = (shard - (slots - 1)) * rows
@@ -249,6 +251,7 @@
     for position, out_ref in enumerate(out_refs):
         out_ref[...] = staged[position]
     if last:
+        plan_copy.wait()
         shards = plan_ref.shape[0]
         block = rows // shards
         for s in range(shards):
@@ -258,9 +261,9 @@
         lse_ref[...] = norms[...]
 
 
-def assemble_kernel(planes, width, groups, places, where_ref, served_ref, *refs):
+def assemble_kernel(planes, width, groups, places, served_ref, *refs):
     pieces, out_ref, lse_hbm, lse_ref, sems = refs[:-4], *refs[-4:]
-    z = where_ref[1]
+    z = lax.axis_index("kv")
     copies = []
     for index, (s, group) in enumerate(places):
         origin = lax.rem(z - s + planes, planes)
@@ -280,27 +283,28 @@
 def body(queries, key_states, value_states, doc_lengths, block_plan):
     shards = lax.axis_size("tok")
     planes = lax.axis_size("kv")
-    shard = lax.axis_index("tok")
-    z = lax.axis_index("kv")
     rows = queries.shape[0]
     groups = key_states.shape[1] // HEAD_DIM
     heads = queries.shape[1] // HEAD_DIM
     per_group = heads // groups
     tile = rows // planes
     pieces = shards // 4
-    where = jnp.stack([shard, z]).astype(jnp.int32)
     half_freq = THETA ** (-np.arange(HALF, dtype=np.float64) * 2.0 / HEAD_DIM)
     freq = jnp.asarray(np.concatenate([half_freq, half_freq])[None, :], jnp.float32)
 
     pair = [(i, i ^ 1) for i in range(shards)]
-    to_odd = [(i, i + 1) for i in range(0, shards, 2)]
-    arrived = [
-        [
-            lax.ppermute(x, "tok", [(i, i + 2 * p) for i in range(shards - 2 * p)])
-            for p in range(1, pieces + 1)
-        ]
-        for x in (key_states, value_states)
-    ]
+
+    def forward(x, p):
+        return lax.ppermute(x, "tok", [(i, i + 2 * p) for i in range(shards - 2 * p)])
+
+    far_keys = [forward(key_states, p) for p in range(1, pieces + 1)]
+    far_values = [forward(value_states, p) for p in range(1, pieces + 1)]
+    relayed = []
+    after = queries
+    if shards == 8:
+        far_keys[0] = lax.ppermute(key_states, "tok", [(0, 2), (1, 3), (4, 6), (5, 7)])
+        relayed = [lax.ppermute(far_keys[1], "tok", [(6, 4), (7, 5)])]
+        after, _ = lax.optimization_barrier((queries, far_keys[1]))
     pack_shape = jax.ShapeDtypeStruct((rows, 2 * groups * HEAD_DIM), jnp.bfloat16)
     with jax.named_scope("rotate"):
         result = pl.pallas_call(
@@ -311,43 +315,45 @@
                 jax.ShapeDtypeStruct((2 * pieces, rows, HEAD_DIM), jnp.float32),
             ]
             + [jax.ShapeDtypeStruct((planes, per_group * tile, HEAD_DIM), jnp.bfloat16)] * groups,
-            in_specs=[smem(), smem(), vmem(), hbm(), hbm(), hbm()],
+            in_specs=[hbm()] * 5,
             out_specs=[vmem()] * (3 + groups),
             scratch_shapes=[
+                pltpu.SMEM(doc_lengths.shape, jnp.int32),
+                pltpu.VMEM(freq.shape, jnp.float32),
                 pltpu.VMEM(key_states.shape, jnp.bfloat16),
                 pltpu.VMEM(value_states.shape, jnp.bfloat16),
                 pltpu.VMEM(queries.shape, jnp.bfloat16),
-                pltpu.SemaphoreType.DMA((3,)),
+                pltpu.SemaphoreType.DMA((5,)),
             ],
             compiler_params=params(),
             cost_estimate=cost(3.0),
         )(
-            where,
-            doc_lengths,
-            freq,
+            pltpu.with_memory_space_constraint(doc_lengths, pltpu.HBM),
+            pltpu.with_memory_space_constraint(freq, pltpu.HBM),
             pltpu.with_memory_space_constraint(key_states, pltpu.HBM),
             pltpu.with_memory_space_constraint(value_states, pltpu.HBM),
-            pltpu.with_memory_space_constraint(queries, pltpu.HBM),
+            pltpu.with_memory_space_constraint(after, pltpu.HBM),
         )
     own, start, tables = result[:3]
     turned = result[3:]
-    beside = lax.ppermute(own, "tok", to_odd)
-    tables, beside = lax.optimization_barrier((tables, beside))
     with jax.named_scope("pack"):
-        far = pl.pallas_call(
-            pack_kernel,
-            out_shape=jax.ShapeDtypeStruct((pieces, *pack_shape.shape), jnp.bfloat16),
-            in_specs=[vmem()] * (1 + 2 * pieces),
-            out_specs=vmem(),
+        mine, give = pl.pallas_call(
+            partial(pack_kernel, pieces),
+            out_shape=[
+                jax.ShapeDtypeStruct((count, *pack_shape.shape), jnp.bfloat16)
+                for count in (pieces + 1, pieces)
+            ],
+            in_specs=[vmem()] * (2 + 2 * pieces + len(relayed)),
+            out_specs=[vmem()] * 2,
             compiler_params=params(),
             cost_estimate=cost(1.0),
-        )(tables, *arrived[0], *arrived[1])
-    near = lax.ppermute(far, "tok", pair)
+        )(tables, own, *far_keys, *far_values, *relayed)
+    theirs = lax.ppermute(give, "tok", pair)
 
     def attend(norm, used, tiles_of, last, microseconds):
-        scalars = [where, block_plan] if last else [where]
+        plan = [pltpu.with_memory_space_constraint(block_plan, pltpu.HBM)] if last else []
         operands = [start] if norm is None else [start, norm]
-        operands += [own, beside, far, near] + [turned[group] for group in used]
+        operands += [mine, theirs] + [turned[group] for group in used]
         tasks = len(tiles_of)
         width = len(used) * per_group * HEAD_DIM
         with jax.named_scope("attend"):
@@ -358,16 +364,17 @@
                 out_shape=[jax.ShapeDtypeStruct((tile, width), jnp.bfloat16)]
                 * tasks
                 + [jax.ShapeDtypeStruct((rows, HEAD_DIM), jnp.float32)],
-                in_specs=[smem()] * len(scalars) + [vmem()] * len(operands),
+                in_specs=[hbm()] * len(plan) + [vmem()] * len(operands),
                 out_specs=[vmem()] * (tasks + 1),
                 scratch_shapes=[
                     pltpu.VMEM((tasks, tile, width), jnp.bfloat16),
-                    pltpu.VMEM((pieces, *pack_shape.shape), jnp.bfloat16),
                     pltpu.VMEM((rows, HEAD_DIM), jnp.float32),
-                ],
+                ]
+                + [pltpu.SMEM(block_plan.shape, jnp.int32), pltpu.SemaphoreType.DMA((1,))]
+                * len(plan),
                 compiler_params=params(),
                 cost_estimate=cost(microseconds),
-            )(*scalars, *operands)
+            )(*plan, *operands)
         return result[:tasks], result[tasks]
 
     def send(piece, s):
@@ -375,10 +382,11 @@
 
     norm, pieces_of = None, {}
     for group in range(groups):
-        span = range(1, planes)
-        result, norm = attend(norm, [group], span, False, 2.0 * len(span))
-        for s, piece in zip(span, result):
-            pieces_of[s, group] = send(piece, s)
+        spans = [range(1, planes)]
+        for span in spans:
+            result, norm = attend(norm, [group], span, False, 0.01)
+            for s, piece in zip(span, result):
+                pieces_of[s, group] = send(piece, s)
     (piece,), norm = attend(norm, list(range(groups)), range(1), True, 4.0)
     pieces_of[0, 0] = piece
     block_rows = rows // shards
@@ -394,14 +402,14 @@
                 jax.ShapeDtypeStruct((tile, planes * heads * HEAD_DIM), jnp.bfloat16),
                 jax.ShapeDtypeStruct((heads, rows), jnp.float32),
             ],
-            in_specs=[smem(), vmem()] + [hbm()] * len(flat),
+            in_specs=[vmem()] + [hbm()] * len(flat),
             out_specs=[hbm(), hbm()],
             scratch_shapes=[
                 pltpu.VMEM((heads, rows), jnp.float32),
                 pltpu.SemaphoreType.DMA((len(flat) + 1,)),
             ],
             compiler_params=params(),
-        )(where, served, *flat)
+        )(served, *flat)
     return (attention_out, served_lse)
 
 

time: 57.1 us -> 48.9 us (0.86); the launches traced: 56.8 us -> 48 us
  waiting for transfers between devices: 6.16 us -> 2.15 us
  Pallas kernels: 17.2 us -> 14.7 us
  starting transfers between devices: 22.8 us -> 21.1 us
  local copies, waits for them, and re-layouts: 0.59 us -> 0 us
    ppermute x6, waiting for transfers between devices: 6.15 us -> 2.14 us  [the longest x1 1.9 us: body(): theirs = lax.ppermute(give, 'tok', pair)]
    pallas_call x3, Pallas kernels: 11.7 us -> 9.97 us  [attend(): pl.pallas_call(partial(attend_kernel, pieces, per_group, used, tiles_of,...]
    ppermute x6, starting transfers between devices: 13.3 us -> 11.6 us  [the longest x3 7.47 us: forward(): lax.ppermute(x, 'tok', [(i, i + 2 * p) for i in range(shards - 2 * p)])]
    unnamed x10 -> x0, local copies, waits for them, and re-layouts: 0.59 us -> none
  transfers between devices with their start and end apart: 12 -> 12, of which waited for: 2 -> 2; matrix products, arithmetic and copies ran while one was open for 0% -> 0% of each run, Pallas kernels for 13% -> 21%
where the time goes in v1:
time: 48.9 us; the launch traced here: 48 us
  starting transfers between devices  21.1 us (43%)
  Pallas kernels  14.7 us (30%)
  blocking collectives  9.16 us (19%)
  waiting for transfers between devices  2.15 us (4%)
  between operations  0.91 us (2%)
    pallas_call x3, Pallas kernels, attend(): pl.pallas_call(partial(attend_kernel, pieces, per_group, used, tiles_of,...  9.97 us
    ppermute x6, starting transfers between devices, send(): lax.ppermute(piece, 'kv', [(i, (i + s) % planes) for i in range(planes)])  9.44 us
    all_to_all x1, blocking collectives, body(): lax.all_to_all(norm.reshape(shards, block_rows, HEAD_DIM), 'tok', split_a...  9.16 us
    ppermute x3, starting transfers between devices, forward(): lax.ppermute(x, 'tok', [(i, i + 2 * p) for i in range(shards - 2 * p)])  7.47 us
    ppermute x1, starting transfers between devices, body(): lax.ppermute(key_states, 'tok', [(0, 2), (1, 3), (4, 6), (5, 7)])  3.4 us
    pallas_call x1, Pallas kernels, body(): pl.pallas_call(partial(queries_kernel, pieces), out_shape=[pack_shape, ja...  3.38 us
    ppermute x1, waiting for transfers between devices, body(): theirs = lax.ppermute(give, 'tok', pair)  1.9 us
    pallas_call x1, Pallas kernels, body(): pl.pallas_call(partial(assemble_kernel, planes, per_group * HEAD_DIM, gro...  1.04 us
  transfers between devices with their start and end apart: 12, of which 2 were waited for; matrix products, arithmetic and copies ran while one was open for 0% of the time, Pallas kernels for 21%

profile of v1, /device:TPU:0, one launch (start us, length us, event | category | flops | bytes accessed | tf_op | source)
XLA Modules:
  0.0 48.0 jit_solution(10348389518756417802)
XLA Ops:
  0.6 4.9 %collective-permute-start = (bf16[256,256]{1,0:T(8,128)(2,1)}, bf16[256,256]{1,0:T(8,128)(2,1)S(1)}, u32[]{:S(2)}, u32[]{:S(2)}) collective-permute-start(bf16[256,256]{1,0:T(8,128)(2,1)} %key_hbm.1), channel_id=1, source_target_pairs={{0,16},{4,20},{8,24},{12,28},{1,17},{5,21},{9,25},{13,29},{2,18},{... | collective-permute-start | bytes 393224 | tf_op jit(solution)/shard_map/ppermute | solution.py:298
  5.5 3.4 %collective-permute-start.1 = (bf16[256,256]{1,0:T(8,128)(2,1)}, bf16[256,256]{1,0:T(8,128)(2,1)S(1)}, u32[]{:S(2)}, u32[]{:S(2)}) collective-permute-start(bf16[256,256]{1,0:T(8,128)(2,1)} %key_hbm.1), channel_id=1, source_target_pairs={{0,8},{4,12},{16,24},{20,28},{1,9},{5,13},{17,25},{21,29},{2,10},{... | collective-permute-start | bytes 393224 | tf_op jit(solution)/shard_map/ppermute | solution.py:305
  8.9 1.3 %collective-permute-start.3 = (bf16[256,256]{1,0:T(8,128)(2,1)}, bf16[256,256]{1,0:T(8,128)(2,1)S(1)}, u32[]{:S(2)}, u32[]{:S(2)}) collective-permute-start(bf16[256,256]{1,0:T(8,128)(2,1)} %value_hbm.1), channel_id=1, source_target_pairs={{0,16},{4,20},{8,24},{12,28},{1,17},{5,21},{9,25},{13,29},{2,18},{... | collective-permute-start | bytes 393224 | tf_op jit(solution)/shard_map/ppermute | solution.py:298
  10.2 1.3 %collective-permute-start.2 = (bf16[256,256]{1,0:T(8,128)(2,1)}, bf16[256,256]{1,0:T(8,128)(2,1)S(1)}, u32[]{:S(2)}, u32[]{:S(2)}) collective-permute-start(bf16[256,256]{1,0:T(8,128)(2,1)} %value_hbm.1), channel_id=1, source_target_pairs={{0,8},{4,12},{8,16},{12,20},{16,24},{20,28},{1,9},{5,13},{9,17},{1... | collective-permute-start | bytes 393224 | tf_op jit(solution)/shard_map/ppermute | solution.py:298
  11.5 0.0 collective-permute-done.refs_1_
  11.5 0.7 %collective-permute-start.4 = (bf16[256,256]{1,0:T(8,128)(2,1)S(1)}, bf16[256,256]{1,0:T(8,128)(2,1)S(1)}, u32[]{:S(2)}, u32[]{:S(2)}) collective-permute-start(bf16[256,256]{1,0:T(8,128)(2,1)S(1)} %collective-permute-done.refs_1_), channel_id=1, source_target_pairs={{24,16},{28,20},{25,17},{29,21},{26,18},{30,22},{27,19},{31,23}} | collective-permute-start | bytes 393224 | tf_op jit(solution)/shard_map/ppermute | solution.py:306
  12.2 3.4 %rotate.1 = (bf16[256,512]{1,0:T(8,128)(2,1)S(1)}, s32[256,128]{1,0:T(8,128)S(1)}, f32[4,256,128]{2,1,0:T(8,128)S(1)}, bf16[4,512,128]{2,1,0:T(8,128)(2,1)S(1)}, bf16[4,512,128]{2,1,0:T(8,128)(2,1)S(1)}) custom-call(s32[16]{0:T(128)} %lengths_hbm.1, f32[1,128]{1,0:T(1,128)} %constant.2.clone.freq_hbm, bf16[256,256]{1,0:T(8,128)(2,1)} %key_hbm.1, ...), custom_call_target="tpu_custom_call" | custom-call | flops 3449999872 | tf_op jit(solution)/shard_map/rotate/pallas_call | solution.py:310
  15.6 0.0 collective-permute-done.1.refs_0_
  15.6 0.2 collective-permute-done.3.refs_3_
  15.8 0.0 collective-permute-done.2.refs_2_
  15.9 0.0 collective-permute-done.4.refs_4_
  15.9 0.3 pack.1
  16.2 0.1 collective-permute-start.5
  16.2 1.9 %collective-permute-done.5.refs_2_.refs_3_.refs_4_ = bf16[2,256,512]{2,1,0:T(8,128)(2,1)S(1)} collective-permute-done((bf16[2,256,512]{2,1,0:T(8,128)(2,1)S(1)}, bf16[2,256,512]{2,1,0:T(8,128)(2,1)S(1)}, u32[]{:S(2)}, u32[]{:S(2)}) %collective-permute-start.5) | collective-permute-done | bytes 524320 | tf_op jit(solution)/shard_map/ppermute | solution.py:351
  18.1 3.5 %attend.3 = (bf16[64,1024]{1,0:T(8,128)(2,1)S(1)}, bf16[64,1024]{1,0:T(8,128)(2,1)S(1)}, bf16[64,1024]{1,0:T(8,128)(2,1)S(1)}, f32[256,128]{1,0:T(8,128)S(1)}) custom-call(s32[256,128]{1,0:T(8,128)S(1)} %get-tuple-element.21.refs_0_.refs_1_, bf16[3,256,512]{2,1,0:T(8,128)(2,1)S(1)} %get-tuple-element.24.refs_1_.refs_2_.refs_3_, ...), custom_call_target="tpu_custom_call" | custom-call | flops 11500000 | tf_op jit(solution)/shard_map/attend/pallas_call | solution.py:360
  21.6 1.6 %collective-permute-start.6 = (bf16[64,1024]{1,0:T(8,128)(2,1)S(1)}, bf16[64,1024]{1,0:T(8,128)(2,1)S(1)}, u32[]{:S(2)}, u32[]{:S(2)}) collective-permute-start(bf16[64,1024]{1,0:T(8,128)(2,1)S(1)} %get-tuple-element.32), channel_id=1, source_target_pairs={{0,1},{1,2},{2,3},{3,0},{4,5},{5,6},{6,7},{7,4},{8,9},{9,10},{10,1... | collective-permute-start | bytes 393224 | tf_op jit(solution)/shard_map/ppermute | solution.py:381
  23.2 2.6 %collective-permute-start.8 = (bf16[64,1024]{1,0:T(8,128)(2,1)S(1)}, bf16[64,1024]{1,0:T(8,128)(2,1)S(1)}, u32[]{:S(2)}, u32[]{:S(2)}) collective-permute-start(bf16[64,1024]{1,0:T(8,128)(2,1)S(1)} %get-tuple-element.34), channel_id=1, source_target_pairs={{0,2},{1,3},{2,0},{3,1},{4,6},{5,7},{6,4},{7,5},{8,10},{9,11},{10,... | collective-permute-start | bytes 393224 | tf_op jit(solution)/shard_map/ppermute | solution.py:381
  25.8 1.3 %collective-permute-start.10 = (bf16[64,1024]{1,0:T(8,128)(2,1)S(1)}, bf16[64,1024]{1,0:T(8,128)(2,1)S(1)}, u32[]{:S(2)}, u32[]{:S(2)}) collective-permute-start(bf16[64,1024]{1,0:T(8,128)(2,1)S(1)} %get-tuple-element.36), channel_id=1, source_target_pairs={{0,3},{1,0},{2,1},{3,2},{4,7},{5,4},{6,5},{7,6},{8,11},{9,8},{10,9... | collective-permute-start | bytes 393224 | tf_op jit(solution)/shard_map/ppermute | solution.py:381
  27.1 3.4 %attend.4 = (bf16[64,1024]{1,0:T(8,128)(2,1)S(1)}, bf16[64,1024]{1,0:T(8,128)(2,1)S(1)}, bf16[64,1024]{1,0:T(8,128)(2,1)S(1)}, f32[256,128]{1,0:T(8,128)S(1)}) custom-call(s32[256,128]{1,0:T(8,128)S(1)} %get-tuple-element.21.refs_0_.refs_1_, f32[256,128]{1,0:T(8,128)S(1)} %get-tuple-element.27.refs_1_, ...), custom_call_target="tpu_custom_call" | custom-call | flops 11500000 | tf_op jit(solution)/shard_map/attend/pallas_call | solution.py:360
  30.6 0.7 %collective-permute-start.7 = (bf16[64,1024]{1,0:T(8,128)(2,1)S(1)}, bf16[64,1024]{1,0:T(8,128)(2,1)S(1)}, u32[]{:S(2)}, u32[]{:S(2)}) collective-permute-start(bf16[64,1024]{1,0:T(8,128)(2,1)S(1)} %get-tuple-element.33), channel_id=1, source_target_pairs={{0,1},{1,2},{2,3},{3,0},{4,5},{5,6},{6,7},{7,4},{8,9},{9,10},{10,1... | collective-permute-start | bytes 393224 | tf_op jit(solution)/shard_map/ppermute | solution.py:381
  31.3 0.3 collective-permute-start.9
  31.7 0.0 collective-permute-done.6.refs_1_
  31.7 2.8 %collective-permute-start.11 = (bf16[64,1024]{1,0:T(8,128)(2,1)S(1)}, bf16[64,1024]{1,0:T(8,128)(2,1)S(1)}, u32[]{:S(2)}, u32[]{:S(2)}) collective-permute-start(bf16[64,1024]{1,0:T(8,128)(2,1)S(1)} %get-tuple-element.37), channel_id=1, source_target_pairs={{0,3},{1,0},{2,1},{3,2},{4,7},{5,4},{6,5},{7,6},{8,11},{9,8},{10,9... | collective-permute-start | bytes 393224 | tf_op jit(solution)/shard_map/ppermute | solution.py:381
  34.5 3.1 %attend.5 = (bf16[64,2048]{1,0:T(8,128)(2,1)S(1)}, f32[256,128]{1,0:T(8,128)S(1)}) custom-call(s32[8,8]{1,0:T(8,128)} %refs_0_.1, s32[256,128]{1,0:T(8,128)S(1)} %get-tuple-element.21.refs_0_.refs_1_, f32[256,128]{1,0:T(8,128)S(1)} %get-tuple-element.29.refs_2_, bf16[3,256,512]{2,1,0:T(8,128)(2,1)S(1)} %get-tuple-element.24.refs_1_.refs_2_.refs_3_, ...), custom_call_target="tpu_custom_call" | custom-call | flops 4600000000 | tf_op jit(solution)/shard_map/attend/pallas_call | solution.py:360
  37.6 9.2 %all_to_all.5 = f32[8,32,128]{2,1,0:T(8,128)S(1)} all-to-all(f32[8,32,128]{2,1,0:T(8,128)S(1)} %bitcast.3), channel_id=1, replica_groups=mesh['tok'=8,'kv'=4] {'tok'}, dimensions={0} | all-to-all | bytes 262144 | tf_op jit(solution)/shard_map/all_to_all | solution.py:393
  46.7 0.0 collective-permute-done.8.refs_3_
  46.7 0.0 collective-permute-done.10.refs_5_
  46.7 0.0 collective-permute-done.7.refs_2_
  46.7 0.0 collective-permute-done.9.refs_4_
  46.7 0.0 collective-permute-done.11.refs_6_
  46.8 1.0 %assemble.1 = (bf16[64,8192]{1,0:T(8,128)(2,1)}, f32[16,256]{1,0:T(8,128)}) custom-call(f32[256,128]{1,0:T(8,128)S(1)} %bitcast.2, bf16[64,2048]{1,0:T(8,128)(2,1)S(1)} %get-tuple-element.31.refs_0_, bf16[64,1024]{1,0:T(8,128)(2,1)S(1)} %collective-permute-done.6.refs_1_, bf16[64,1024]{1,0:T(8,128)(2,1)S(1)} %collective-permute-done.7.refs_2_, ...), custom_call_target="tpu_custom_call" | custom-call | tf_op jit(solution)/shard_map/assemble/pallas_call | solution.py:399
Async XLA Ops:
  0.6 10.9 %collective-permute-start = (bf16[256,256]{1,0:T(8,128)(2,1)}, bf16[256,256]{1,0:T(8,128)(2,1)S(1)}, u32[]{:S(2)}, u32[]{:S(2)}) collective-permute-start(bf16[256,256]{1,0:T(8,128)(2,1)} %key_hbm.1), channel_id=1, source_target_pairs={{0,16},{4,20},{8,24},{12,28},{1,17},{5,21},{9,25},{13,29},{2,18},{... | collective-permute-start | bytes 393224 | tf_op jit(solution)/shard_map/ppermute | solution.py:298
  5.5 10.1 %collective-permute-start.1 = (bf16[256,256]{1,0:T(8,128)(2,1)}, bf16[256,256]{1,0:T(8,128)(2,1)S(1)}, u32[]{:S(2)}, u32[]{:S(2)}) collective-permute-start(bf16[256,256]{1,0:T(8,128)(2,1)} %key_hbm.1), channel_id=1, source_target_pairs={{0,8},{4,12},{16,24},{20,28},{1,9},{5,13},{17,25},{21,29},{2,10},{... | collective-permute-start | bytes 393224 | tf_op jit(solution)/shard_map/ppermute | solution.py:305
  8.9 6.9 %collective-permute-start.3 = (bf16[256,256]{1,0:T(8,128)(2,1)}, bf16[256,256]{1,0:T(8,128)(2,1)S(1)}, u32[]{:S(2)}, u32[]{:S(2)}) collective-permute-start(bf16[256,256]{1,0:T(8,128)(2,1)} %value_hbm.1), channel_id=1, source_target_pairs={{0,16},{4,20},{8,24},{12,28},{1,17},{5,21},{9,25},{13,29},{2,18},{... | collective-permute-start | bytes 393224 | tf_op jit(solution)/shard_map/ppermute | solution.py:298
  10.2 5.6 %collective-permute-start.2 = (bf16[256,256]{1,0:T(8,128)(2,1)}, bf16[256,256]{1,0:T(8,128)(2,1)S(1)}, u32[]{:S(2)}, u32[]{:S(2)}) collective-permute-start(bf16[256,256]{1,0:T(8,128)(2,1)} %value_hbm.1), channel_id=1, source_target_pairs={{0,8},{4,12},{8,16},{12,20},{16,24},{20,28},{1,9},{5,13},{9,17},{1... | collective-permute-start | bytes 393224 | tf_op jit(solution)/shard_map/ppermute | solution.py:298
  11.5 4.3 %collective-permute-start.4 = (bf16[256,256]{1,0:T(8,128)(2,1)S(1)}, bf16[256,256]{1,0:T(8,128)(2,1)S(1)}, u32[]{:S(2)}, u32[]{:S(2)}) collective-permute-start(bf16[256,256]{1,0:T(8,128)(2,1)S(1)} %collective-permute-done.refs_1_), channel_id=1, source_target_pairs={{24,16},{28,20},{25,17},{29,21},{26,18},{30,22},{27,19},{31,23}} | collective-permute-start | bytes 393224 | tf_op jit(solution)/shard_map/ppermute | solution.py:306
  16.2 2.0 %collective-permute-start.5 = (bf16[2,256,512]{2,1,0:T(8,128)(2,1)S(1)}, bf16[2,256,512]{2,1,0:T(8,128)(2,1)S(1)}, u32[]{:S(2)}, u32[]{:S(2)}) collective-permute-start(bf16[2,256,512]{2,1,0:T(8,128)(2,1)S(1)} %get-tuple-element.25), channel_id=1, source_target_pairs={{0,4},{4,0},{8,12},{12,8},{16,20},{20,16},{24,28},{28,24},{1,5},{5... | collective-permute-start | bytes 1572872 | tf_op jit(solution)/shard_map/ppermute | solution.py:351
  21.6 10.1 %collective-permute-start.6 = (bf16[64,1024]{1,0:T(8,128)(2,1)S(1)}, bf16[64,1024]{1,0:T(8,128)(2,1)S(1)}, u32[]{:S(2)}, u32[]{:S(2)}) collective-permute-start(bf16[64,1024]{1,0:T(8,128)(2,1)S(1)} %get-tuple-element.32), channel_id=1, source_target_pairs={{0,1},{1,2},{2,3},{3,0},{4,5},{5,6},{6,7},{7,4},{8,9},{9,10},{10,1... | collective-permute-start | bytes 393224 | tf_op jit(solution)/shard_map/ppermute | solution.py:381
  23.2 23.5 %collective-permute-start.8 = (bf16[64,1024]{1,0:T(8,128)(2,1)S(1)}, bf16[64,1024]{1,0:T(8,128)(2,1)S(1)}, u32[]{:S(2)}, u32[]{:S(2)}) collective-permute-start(bf16[64,1024]{1,0:T(8,128)(2,1)S(1)} %get-tuple-element.34), channel_id=1, source_target_pairs={{0,2},{1,3},{2,0},{3,1},{4,6},{5,7},{6,4},{7,5},{8,10},{9,11},{10,... | collective-permute-start | bytes 393224 | tf_op jit(solution)/shard_map/ppermute | solution.py:381
  25.8 20.9 %collective-permute-start.10 = (bf16[64,1024]{1,0:T(8,128)(2,1)S(1)}, bf16[64,1024]{1,0:T(8,128)(2,1)S(1)}, u32[]{:S(2)}, u32[]{:S(2)}) collective-permute-start(bf16[64,1024]{1,0:T(8,128)(2,1)S(1)} %get-tuple-element.36), channel_id=1, source_target_pairs={{0,3},{1,0},{2,1},{3,2},{4,7},{5,4},{6,5},{7,6},{8,11},{9,8},{10,9... | collective-permute-start | bytes 393224 | tf_op jit(solution)/shard_map/ppermute | solution.py:381
  30.6 16.1 %collective-permute-start.7 = (bf16[64,1024]{1,0:T(8,128)(2,1)S(1)}, bf16[64,1024]{1,0:T(8,128)(2,1)S(1)}, u32[]{:S(2)}, u32[]{:S(2)}) collective-permute-start(bf16[64,1024]{1,0:T(8,128)(2,1)S(1)} %get-tuple-element.33), channel_id=1, source_target_pairs={{0,1},{1,2},{2,3},{3,0},{4,5},{5,6},{6,7},{7,4},{8,9},{9,10},{10,1... | collective-permute-start | bytes 393224 | tf_op jit(solution)/shard_map/ppermute | solution.py:381
  31.3 15.4 %collective-permute-start.9 = (bf16[64,1024]{1,0:T(8,128)(2,1)S(1)}, bf16[64,1024]{1,0:T(8,128)(2,1)S(1)}, u32[]{:S(2)}, u32[]{:S(2)}) collective-permute-start(bf16[64,1024]{1,0:T(8,128)(2,1)S(1)} %get-tuple-element.35), channel_id=1, source_target_pairs={{0,2},{1,3},{2,0},{3,1},{4,6},{5,7},{6,4},{7,5},{8,10},{9,11},{10,... | collective-permute-start | bytes 393224 | tf_op jit(solution)/shard_map/ppermute | solution.py:381
  31.7 15.1 %collective-permute-start.11 = (bf16[64,1024]{1,0:T(8,128)(2,1)S(1)}, bf16[64,1024]{1,0:T(8,128)(2,1)S(1)}, u32[]{:S(2)}, u32[]{:S(2)}) collective-permute-start(bf16[64,1024]{1,0:T(8,128)(2,1)S(1)} %get-tuple-element.37), channel_id=1, source_target_pairs={{0,3},{1,0},{2,1},{3,2},{4,7},{5,4},{6,5},{7,6},{8,11},{9,8},{10,9... | collective-permute-start | bytes 393224 | tf_op jit(solution)/shard_map/ppermute | solution.py:381

commit v2 on v1

--- a/solution.py
+++ b/solution.py
@@ -381,13 +381,17 @@
         return lax.ppermute(piece, "kv", [(i, (i + s) % planes) for i in range(planes)])
 
     norm, pieces_of = None, {}
-    for group in range(groups):
-        spans = [range(1, planes)]
-        for span in spans:
-            result, norm = attend(norm, [group], span, False, 0.01)
-            for s, piece in zip(span, result):
-                pieces_of[s, group] = send(piece, s)
-    (piece,), norm = attend(norm, list(range(groups)), range(1), True, 4.0)
+    middle, both = planes // 2, list(range(groups))
+    spans = [range(middle, middle + 1), range(1, planes, 2)]
+    spans += [range(s, s + 1) for s in range(2, planes, 2) if s != middle]
+    for used in [both]:
+        (piece,), norm = attend(norm, used, spans[0], False, 2.0 * len(used))
+        pieces_of[middle, used[0]] = send(piece, middle)
+    for span in spans[1:]:
+        result, norm = attend(norm, both, span, False, 4.0 * len(span))
+        for s, piece in zip(span, result):
+            pieces_of[s, 0] = send(piece, s)
+    (piece,), norm = attend(norm, both, range(1), True, 4.0)
     pieces_of[0, 0] = piece
     block_rows = rows // shards
     served = lax.all_to_all(

time: 48.9 us -> 48.2 us (0.986); the launches traced: 48 us -> 47.9 us
  starting transfers between devices: 21.1 us -> 18.1 us
  waiting for transfers between devices: 2.15 us -> 4.92 us
    ppermute x6 -> x3, starting transfers between devices: 9.44 us -> 6.53 us  [send(): lax.ppermute(piece, 'kv', [(i, (i + s) % planes) for i in range(planes)])]
    ppermute x6 -> x3, waiting for transfers between devices: 0.02 us -> 2.78 us  [send(): lax.ppermute(piece, 'kv', [(i, (i + s) % planes) for i in range(planes)])]
  transfers between devices with their start and end apart: 12 -> 9, of which waited for: 2 -> 3; matrix products, arithmetic and copies ran while one was open for 0% -> 0% of each run, Pallas kernels for 21% -> 23%
where the time goes in v2:
time: 48.2 us; the launch traced here: 47.9 us
  starting transfers between devices  18.1 us (38%)
  Pallas kernels  14.8 us (31%)
  blocking collectives  9.16 us (19%)
  waiting for transfers between devices  4.92 us (10%)
  between operations  0.89 us (2%)
    pallas_call x3, Pallas kernels, attend(): pl.pallas_call(partial(attend_kernel, pieces, per_group, used, tiles_of,...  10.1 us
    all_to_all x1, blocking collectives, body(): lax.all_to_all(norm.reshape(shards, block_rows, HEAD_DIM), 'tok', split_a...  9.16 us
    ppermute x3, starting transfers between devices, forward(): lax.ppermute(x, 'tok', [(i, i + 2 * p) for i in range(shards - 2 * p)])  7.47 us
    ppermute x3, starting transfers between devices, send(): lax.ppermute(piece, 'kv', [(i, (i + s) % planes) for i in range(planes)])  6.53 us
    ppermute x1, starting transfers between devices, body(): lax.ppermute(key_states, 'tok', [(0, 2), (1, 3), (4, 6), (5, 7)])  3.4 us
    pallas_call x1, Pallas kernels, body(): pl.pallas_call(partial(queries_kernel, pieces), out_shape=[pack_shape, ja...  3.38 us
    ppermute x3, waiting for transfers between devices, send(): lax.ppermute(piece, 'kv', [(i, (i + s) % planes) for i in range(planes)])  2.78 us
    ppermute x1, waiting for transfers between devices, body(): theirs = lax.ppermute(give, 'tok', pair)  1.9 us
  transfers between devices with their start and end apart: 9, of which 3 were waited for; matrix products, arithmetic and copies ran while one was open for 0% of the time, Pallas kernels for 23%

profile of v2, /device:TPU:0, one launch (start us, length us, event | category | flops | bytes accessed | tf_op | source)
XLA Modules:
  0.0 47.9 jit_solution(7463689994832864349)
XLA Ops:
  0.6 4.9 %collective-permute-start = (bf16[256,256]{1,0:T(8,128)(2,1)}, bf16[256,256]{1,0:T(8,128)(2,1)S(1)}, u32[]{:S(2)}, u32[]{:S(2)}) collective-permute-start(bf16[256,256]{1,0:T(8,128)(2,1)} %key_hbm.1), channel_id=1, source_target_pairs={{0,16},{4,20},{8,24},{12,28},{1,17},{5,21},{9,25},{13,29},{2,18},{... | collective-permute-start | bytes 393224 | tf_op jit(solution)/shard_map/ppermute | solution.py:298
  5.5 3.4 %collective-permute-start.1 = (bf16[256,256]{1,0:T(8,128)(2,1)}, bf16[256,256]{1,0:T(8,128)(2,1)S(1)}, u32[]{:S(2)}, u32[]{:S(2)}) collective-permute-start(bf16[256,256]{1,0:T(8,128)(2,1)} %key_hbm.1), channel_id=1, source_target_pairs={{0,8},{4,12},{16,24},{20,28},{1,9},{5,13},{17,25},{21,29},{2,10},{... | collective-permute-start | bytes 393224 | tf_op jit(solution)/shard_map/ppermute | solution.py:305
  8.9 1.3 %collective-permute-start.3 = (bf16[256,256]{1,0:T(8,128)(2,1)}, bf16[256,256]{1,0:T(8,128)(2,1)S(1)}, u32[]{:S(2)}, u32[]{:S(2)}) collective-permute-start(bf16[256,256]{1,0:T(8,128)(2,1)} %value_hbm.1), channel_id=1, source_target_pairs={{0,16},{4,20},{8,24},{12,28},{1,17},{5,21},{9,25},{13,29},{2,18},{... | collective-permute-start | bytes 393224 | tf_op jit(solution)/shard_map/ppermute | solution.py:298
  10.2 1.3 %collective-permute-start.2 = (bf16[256,256]{1,0:T(8,128)(2,1)}, bf16[256,256]{1,0:T(8,128)(2,1)S(1)}, u32[]{:S(2)}, u32[]{:S(2)}) collective-permute-start(bf16[256,256]{1,0:T(8,128)(2,1)} %value_hbm.1), channel_id=1, source_target_pairs={{0,8},{4,12},{8,16},{12,20},{16,24},{20,28},{1,9},{5,13},{9,17},{1... | collective-permute-start | bytes 393224 | tf_op jit(solution)/shard_map/ppermute | solution.py:298
  11.5 0.0 collective-permute-done.refs_1_
  11.5 0.7 %collective-permute-start.4 = (bf16[256,256]{1,0:T(8,128)(2,1)S(1)}, bf16[256,256]{1,0:T(8,128)(2,1)S(1)}, u32[]{:S(2)}, u32[]{:S(2)}) collective-permute-start(bf16[256,256]{1,0:T(8,128)(2,1)S(1)} %collective-permute-done.refs_1_), channel_id=1, source_target_pairs={{24,16},{28,20},{25,17},{29,21},{26,18},{30,22},{27,19},{31,23}} | collective-permute-start | bytes 393224 | tf_op jit(solution)/shard_map/ppermute | solution.py:306
  12.2 3.4 %rotate.1 = (bf16[256,512]{1,0:T(8,128)(2,1)S(1)}, s32[256,128]{1,0:T(8,128)S(1)}, f32[4,256,128]{2,1,0:T(8,128)S(1)}, bf16[4,512,128]{2,1,0:T(8,128)(2,1)S(1)}, bf16[4,512,128]{2,1,0:T(8,128)(2,1)S(1)}) custom-call(s32[16]{0:T(128)} %lengths_hbm.1, f32[1,128]{1,0:T(1,128)} %constant.2.clone.freq_hbm, bf16[256,256]{1,0:T(8,128)(2,1)} %key_hbm.1, ...), custom_call_target="tpu_custom_call" | custom-call | flops 3449999872 | tf_op jit(solution)/shard_map/rotate/pallas_call | solution.py:310
  15.6 0.0 collective-permute-done.1.refs_0_
  15.6 0.2 collective-permute-done.3.refs_3_
  15.8 0.0 collective-permute-done.2.refs_2_
  15.9 0.0 collective-permute-done.4.refs_4_
  15.9 0.3 pack.1
  16.2 0.1 collective-permute-start.5
  16.2 1.9 %collective-permute-done.5.refs_2_.refs_3_.refs_4_ = bf16[2,256,512]{2,1,0:T(8,128)(2,1)S(1)} collective-permute-done((bf16[2,256,512]{2,1,0:T(8,128)(2,1)S(1)}, bf16[2,256,512]{2,1,0:T(8,128)(2,1)S(1)}, u32[]{:S(2)}, u32[]{:S(2)}) %collective-permute-start.5) | collective-permute-done | bytes 524320 | tf_op jit(solution)/shard_map/ppermute | solution.py:351
  18.1 2.5 %attend.3 = (bf16[64,2048]{1,0:T(8,128)(2,1)S(1)}, f32[256,128]{1,0:T(8,128)S(1)}) custom-call(s32[256,128]{1,0:T(8,128)S(1)} %get-tuple-element.18.refs_0_.refs_1_, bf16[3,256,512]{2,1,0:T(8,128)(2,1)S(1)} %get-tuple-element.21.refs_1_.refs_2_.refs_3_, bf16[2,256,512]{2,1,0:T(8,128)(2,1)S(1)} %collective-permute-done.5.refs_2_.refs_3_.refs_4_, ...), custom_call_target="tpu_custom_call" | custom-call | flops 4600000000 | tf_op jit(solution)/shard_map/attend/pallas_call | solution.py:360
  20.6 2.7 %collective-permute-start.7 = (bf16[64,2048]{1,0:T(8,128)(2,1)S(1)}, bf16[64,2048]{1,0:T(8,128)(2,1)S(1)}, u32[]{:S(2)}, u32[]{:S(2)}) collective-permute-start(bf16[64,2048]{1,0:T(8,128)(2,1)S(1)} %get-tuple-element.30), channel_id=1, source_target_pairs={{0,2},{1,3},{2,0},{3,1},{4,6},{5,7},{6,4},{7,5},{8,10},{9,11},{10,... | collective-permute-start | bytes 786440 | tf_op jit(solution)/shard_map/ppermute | solution.py:381
  23.2 4.6 %attend.4 = (bf16[64,2048]{1,0:T(8,128)(2,1)S(1)}, bf16[64,2048]{1,0:T(8,128)(2,1)S(1)}, f32[256,128]{1,0:T(8,128)S(1)}) custom-call(s32[256,128]{1,0:T(8,128)S(1)} %get-tuple-element.18.refs_0_.refs_1_, f32[256,128]{1,0:T(8,128)S(1)} %get-tuple-element.25.refs_1_, bf16[3,256,512]{2,1,0:T(8,128)(2,1)S(1)} %get-tuple-element.21.refs_1_.refs_2_.refs_3_, ...), custom_call_target="tpu_custom_call" | custom-call | flops 9200000000 | tf_op jit(solution)/shard_map/attend/pallas_call | solution.py:360
  27.8 1.6 %collective-permute-start.6 = (bf16[64,2048]{1,0:T(8,128)(2,1)S(1)}, bf16[64,2048]{1,0:T(8,128)(2,1)S(1)}, u32[]{:S(2)}, u32[]{:S(2)}) collective-permute-start(bf16[64,2048]{1,0:T(8,128)(2,1)S(1)} %get-tuple-element.29), channel_id=1, source_target_pairs={{0,1},{1,2},{2,3},{3,0},{4,5},{5,6},{6,7},{7,4},{8,9},{9,10},{10,1... | collective-permute-start | bytes 786440 | tf_op jit(solution)/shard_map/ppermute | solution.py:381
  29.5 2.2 %collective-permute-start.8 = (bf16[64,2048]{1,0:T(8,128)(2,1)S(1)}, bf16[64,2048]{1,0:T(8,128)(2,1)S(1)}, u32[]{:S(2)}, u32[]{:S(2)}) collective-permute-start(bf16[64,2048]{1,0:T(8,128)(2,1)S(1)} %get-tuple-element.31), channel_id=1, source_target_pairs={{0,3},{1,0},{2,1},{3,2},{4,7},{5,4},{6,5},{7,6},{8,11},{9,8},{10,9... | collective-permute-start | bytes 786440 | tf_op jit(solution)/shard_map/ppermute | solution.py:381
  31.7 3.1 %attend.5 = (bf16[64,2048]{1,0:T(8,128)(2,1)S(1)}, f32[256,128]{1,0:T(8,128)S(1)}) custom-call(s32[8,8]{1,0:T(8,128)} %refs_0_.1, s32[256,128]{1,0:T(8,128)S(1)} %get-tuple-element.18.refs_0_.refs_1_, f32[256,128]{1,0:T(8,128)S(1)} %get-tuple-element.26.refs_2_, bf16[3,256,512]{2,1,0:T(8,128)(2,1)S(1)} %get-tuple-element.21.refs_1_.refs_2_.refs_3_, ...), custom_call_target="tpu_custom_call" | custom-call | flops 4600000000 | tf_op jit(solution)/shard_map/attend/pallas_call | solution.py:360
  34.8 9.2 %all_to_all.5 = f32[8,32,128]{2,1,0:T(8,128)S(1)} all-to-all(f32[8,32,128]{2,1,0:T(8,128)S(1)} %bitcast.3), channel_id=1, replica_groups=mesh['tok'=8,'kv'=4] {'tok'}, dimensions={0} | all-to-all | bytes 262144 | tf_op jit(solution)/shard_map/all_to_all | solution.py:397
  44.0 0.0 collective-permute-done.7.refs_2_
  44.0 0.0 collective-permute-done.6.refs_1_
  44.0 2.8 %collective-permute-done.8.refs_3_ = bf16[64,2048]{1,0:T(8,128)(2,1)S(1)} collective-permute-done((bf16[64,2048]{1,0:T(8,128)(2,1)S(1)}, bf16[64,2048]{1,0:T(8,128)(2,1)S(1)}, u32[]{:S(2)}, u32[]{:S(2)}) %collective-permute-start.8) | collective-permute-done | bytes 262176 | tf_op jit(solution)/shard_map/ppermute | solution.py:381
  46.8 1.0 %assemble.1 = (bf16[64,8192]{1,0:T(8,128)(2,1)}, f32[16,256]{1,0:T(8,128)}) custom-call(f32[256,128]{1,0:T(8,128)S(1)} %bitcast.2, bf16[64,2048]{1,0:T(8,128)(2,1)S(1)} %get-tuple-element.28.refs_0_, bf16[64,2048]{1,0:T(8,128)(2,1)S(1)} %collective-permute-done.6.refs_1_, bf16[64,2048]{1,0:T(8,128)(2,1)S(1)} %collective-permute-done.7.refs_2_, ...), custom_call_target="tpu_custom_call" | custom-call | tf_op jit(solution)/shard_map/assemble/pallas_call | solution.py:403
Async XLA Ops:
  0.6 10.9 %collective-permute-start = (bf16[256,256]{1,0:T(8,128)(2,1)}, bf16[256,256]{1,0:T(8,128)(2,1)S(1)}, u32[]{:S(2)}, u32[]{:S(2)}) collective-permute-start(bf16[256,256]{1,0:T(8,128)(2,1)} %key_hbm.1), channel_id=1, source_target_pairs={{0,16},{4,20},{8,24},{12,28},{1,17},{5,21},{9,25},{13,29},{2,18},{... | collective-permute-start | bytes 393224 | tf_op jit(solution)/shard_map/ppermute | solution.py:298
  5.5 10.1 %collective-permute-start.1 = (bf16[256,256]{1,0:T(8,128)(2,1)}, bf16[256,256]{1,0:T(8,128)(2,1)S(1)}, u32[]{:S(2)}, u32[]{:S(2)}) collective-permute-start(bf16[256,256]{1,0:T(8,128)(2,1)} %key_hbm.1), channel_id=1, source_target_pairs={{0,8},{4,12},{16,24},{20,28},{1,9},{5,13},{17,25},{21,29},{2,10},{... | collective-permute-start | bytes 393224 | tf_op jit(solution)/shard_map/ppermute | solution.py:305
  8.9 6.9 %collective-permute-start.3 = (bf16[256,256]{1,0:T(8,128)(2,1)}, bf16[256,256]{1,0:T(8,128)(2,1)S(1)}, u32[]{:S(2)}, u32[]{:S(2)}) collective-permute-start(bf16[256,256]{1,0:T(8,128)(2,1)} %value_hbm.1), channel_id=1, source_target_pairs={{0,16},{4,20},{8,24},{12,28},{1,17},{5,21},{9,25},{13,29},{2,18},{... | collective-permute-start | bytes 393224 | tf_op jit(solution)/shard_map/ppermute | solution.py:298
  10.2 5.6 %collective-permute-start.2 = (bf16[256,256]{1,0:T(8,128)(2,1)}, bf16[256,256]{1,0:T(8,128)(2,1)S(1)}, u32[]{:S(2)}, u32[]{:S(2)}) collective-permute-start(bf16[256,256]{1,0:T(8,128)(2,1)} %value_hbm.1), channel_id=1, source_target_pairs={{0,8},{4,12},{8,16},{12,20},{16,24},{20,28},{1,9},{5,13},{9,17},{1... | collective-permute-start | bytes 393224 | tf_op jit(solution)/shard_map/ppermute | solution.py:298
  11.5 4.3 %collective-permute-start.4 = (bf16[256,256]{1,0:T(8,128)(2,1)S(1)}, bf16[256,256]{1,0:T(8,128)(2,1)S(1)}, u32[]{:S(2)}, u32[]{:S(2)}) collective-permute-start(bf16[256,256]{1,0:T(8,128)(2,1)S(1)} %collective-permute-done.refs_1_), channel_id=1, source_target_pairs={{24,16},{28,20},{25,17},{29,21},{26,18},{30,22},{27,19},{31,23}} | collective-permute-start | bytes 393224 | tf_op jit(solution)/shard_map/ppermute | solution.py:306
  16.2 2.0 %collective-permute-start.5 = (bf16[2,256,512]{2,1,0:T(8,128)(2,1)S(1)}, bf16[2,256,512]{2,1,0:T(8,128)(2,1)S(1)}, u32[]{:S(2)}, u32[]{:S(2)}) collective-permute-start(bf16[2,256,512]{2,1,0:T(8,128)(2,1)S(1)} %get-tuple-element.22), channel_id=1, source_target_pairs={{0,4},{4,0},{8,12},{12,8},{16,20},{20,16},{24,28},{28,24},{1,5},{5... | collective-permute-start | bytes 1572872 | tf_op jit(solution)/shard_map/ppermute | solution.py:351
  20.6 23.4 %collective-permute-start.7 = (bf16[64,2048]{1,0:T(8,128)(2,1)S(1)}, bf16[64,2048]{1,0:T(8,128)(2,1)S(1)}, u32[]{:S(2)}, u32[]{:S(2)}) collective-permute-start(bf16[64,2048]{1,0:T(8,128)(2,1)S(1)} %get-tuple-element.30), channel_id=1, source_target_pairs={{0,2},{1,3},{2,0},{3,1},{4,6},{5,7},{6,4},{7,5},{8,10},{9,11},{10,... | collective-permute-start | bytes 786440 | tf_op jit(solution)/shard_map/ppermute | solution.py:381
  27.8 16.1 %collective-permute-start.6 = (bf16[64,2048]{1,0:T(8,128)(2,1)S(1)}, bf16[64,2048]{1,0:T(8,128)(2,1)S(1)}, u32[]{:S(2)}, u32[]{:S(2)}) collective-permute-start(bf16[64,2048]{1,0:T(8,128)(2,1)S(1)} %get-tuple-element.29), channel_id=1, source_target_pairs={{0,1},{1,2},{2,3},{3,0},{4,5},{5,6},{6,7},{7,4},{8,9},{9,10},{10,1... | collective-permute-start | bytes 786440 | tf_op jit(solution)/shard_map/ppermute | solution.py:381
  29.5 17.3 %collective-permute-start.8 = (bf16[64,2048]{1,0:T(8,128)(2,1)S(1)}, bf16[64,2048]{1,0:T(8,128)(2,1)S(1)}, u32[]{:S(2)}, u32[]{:S(2)}) collective-permute-start(bf16[64,2048]{1,0:T(8,128)(2,1)S(1)} %get-tuple-element.31), channel_id=1, source_target_pairs={{0,3},{1,0},{2,1},{3,2},{4,7},{5,4},{6,5},{7,6},{8,11},{9,8},{10,9... | collective-permute-start | bytes 786440 | tf_op jit(solution)/shard_map/ppermute | solution.py:381

commit v3 on v2

--- a/solution.py
+++ b/solution.py
@@ -170,6 +170,7 @@
     line = lax.broadcasted_iota(jnp.int32, (tile, HEAD_DIM), 0)
     chunk = min(stacked, 256)
     inside = chunk // tile
+    ones = jnp.ones((rows, HEAD_DIM), jnp.bfloat16)
     norms[...] = norm_ref[...] if begun else jnp.zeros(norms.shape, jnp.float32)
 
     def masks_of(t):
@@ -204,22 +205,20 @@
     def mix(index, c, i, parts, best, gathered):
         group = groups[index]
         top = jnp.max(best, axis=1, keepdims=True) * exponent
-        total, mixed = None, None
+        mixed = None
         per_slot = rows // HEAD_DIM
         for slot in range(slots):
             probs = []
             for part in parts[per_slot * slot : per_slot * (slot + 1)]:
                 weights = jnp.exp2(part * exponent - top)
-                total = weights if total is None else total + weights
                 probs.append(weights.astype(jnp.bfloat16))
+            values = jnp.concatenate([window(group, slot, 1), ones], axis=1)
             product = jnp.dot(
-                jnp.concatenate(probs, axis=1),
-                window(group, slot, 1),
-                preferred_element_type=jnp.float32,
+                jnp.concatenate(probs, axis=1), values, preferred_element_type=jnp.float32
             )
             mixed = product if mixed is None else mixed + product
-        row_sum = jnp.sum(total, axis=1, keepdims=True)
-        result = (mixed / row_sum).astype(jnp.bfloat16)
+        row_sum = mixed[:, HEAD_DIM:]
+        result = (mixed[:, :HEAD_DIM] / row_sum).astype(jnp.bfloat16)
         norm = top * (1.0 / LOG2E) + jnp.log(row_sum)
         for h in range(inside):
             head = c * inside + h

time: 48.2 us -> 47.6 us (0.988)
  Pallas kernels: 14.8 us -> 13.3 us
  waiting for transfers between devices: 4.92 us -> 6.08 us
    pallas_call x3, Pallas kernels: 10.1 us -> 8.58 us  [attend(): pl.pallas_call(partial(attend_kernel, pieces, per_group, used, tiles_of,...]
    ppermute x3, waiting for transfers between devices: 2.78 us -> 3.94 us  [send(): lax.ppermute(piece, 'kv', [(i, (i + s) % planes) for i in range(planes)])]
  transfers between devices with their start and end apart: 9 -> 9, of which waited for: 3 -> 3; matrix products, arithmetic and copies ran while one was open for 0% -> 0% of each run, Pallas kernels for 23% -> 21%
where the time goes in v3:
time: 47.6 us; the launch traced here: 47.4 us
  starting transfers between devices  18.1 us (38%)
  Pallas kernels  13.3 us (28%)
  blocking collectives  9.15 us (19%)
  waiting for transfers between devices  6.08 us (13%)
  between operations  0.73 us (2%)
    all_to_all x1, blocking collectives, body(): lax.all_to_all(norm.reshape(shards, block_rows, HEAD_DIM), 'tok', split_a...  9.15 us
    pallas_call x3, Pallas kernels, attend(): pl.pallas_call(partial(attend_kernel, pieces, per_group, used, tiles_of,...  8.58 us
    ppermute x3, starting transfers between devices, forward(): lax.ppermute(x, 'tok', [(i, i + 2 * p) for i in range(shards - 2 * p)])  7.47 us
    ppermute x3, starting transfers between devices, send(): lax.ppermute(piece, 'kv', [(i, (i + s) % planes) for i in range(planes)])  6.53 us
    ppermute x3, waiting for transfers between devices, send(): lax.ppermute(piece, 'kv', [(i, (i + s) % planes) for i in range(planes)])  3.94 us
    ppermute x1, starting transfers between devices, body(): lax.ppermute(key_states, 'tok', [(0, 2), (1, 3), (4, 6), (5, 7)])  3.4 us
    pallas_call x1, Pallas kernels, body(): pl.pallas_call(partial(queries_kernel, pieces), out_shape=[pack_shape, ja...  3.38 us
    ppermute x1, waiting for transfers between devices, body(): theirs = lax.ppermute(give, 'tok', pair)  1.9 us
  transfers between devices with their start and end apart: 9, of which 3 were waited for; matrix products, arithmetic and copies ran while one was open for 0% of the time, Pallas kernels for 21%

profile of v3, /device:TPU:0, one launch (start us, length us, event | category | flops | bytes accessed | tf_op | source)
XLA Modules:
  0.0 47.4 jit_solution(6326632532866688827)
XLA Ops:
  0.6 4.9 %collective-permute-start = (bf16[256,256]{1,0:T(8,128)(2,1)}, bf16[256,256]{1,0:T(8,128)(2,1)S(1)}, u32[]{:S(2)}, u32[]{:S(2)}) collective-permute-start(bf16[256,256]{1,0:T(8,128)(2,1)} %key_hbm.1), channel_id=1, source_target_pairs={{0,16},{4,20},{8,24},{12,28},{1,17},{5,21},{9,25},{13,29},{2,18},{... | collective-permute-start | bytes 393224 | tf_op jit(solution)/shard_map/ppermute | solution.py:297
  5.5 3.4 %collective-permute-start.1 = (bf16[256,256]{1,0:T(8,128)(2,1)}, bf16[256,256]{1,0:T(8,128)(2,1)S(1)}, u32[]{:S(2)}, u32[]{:S(2)}) collective-permute-start(bf16[256,256]{1,0:T(8,128)(2,1)} %key_hbm.1), channel_id=1, source_target_pairs={{0,8},{4,12},{16,24},{20,28},{1,9},{5,13},{17,25},{21,29},{2,10},{... | collective-permute-start | bytes 393224 | tf_op jit(solution)/shard_map/ppermute | solution.py:304
  8.9 1.3 %collective-permute-start.3 = (bf16[256,256]{1,0:T(8,128)(2,1)}, bf16[256,256]{1,0:T(8,128)(2,1)S(1)}, u32[]{:S(2)}, u32[]{:S(2)}) collective-permute-start(bf16[256,256]{1,0:T(8,128)(2,1)} %value_hbm.1), channel_id=1, source_target_pairs={{0,16},{4,20},{8,24},{12,28},{1,17},{5,21},{9,25},{13,29},{2,18},{... | collective-permute-start | bytes 393224 | tf_op jit(solution)/shard_map/ppermute | solution.py:297
  10.2 1.3 %collective-permute-start.2 = (bf16[256,256]{1,0:T(8,128)(2,1)}, bf16[256,256]{1,0:T(8,128)(2,1)S(1)}, u32[]{:S(2)}, u32[]{:S(2)}) collective-permute-start(bf16[256,256]{1,0:T(8,128)(2,1)} %value_hbm.1), channel_id=1, source_target_pairs={{0,8},{4,12},{8,16},{12,20},{16,24},{20,28},{1,9},{5,13},{9,17},{1... | collective-permute-start | bytes 393224 | tf_op jit(solution)/shard_map/ppermute | solution.py:297
  11.5 0.0 collective-permute-done.refs_1_
  11.5 0.7 %collective-permute-start.4 = (bf16[256,256]{1,0:T(8,128)(2,1)S(1)}, bf16[256,256]{1,0:T(8,128)(2,1)S(1)}, u32[]{:S(2)}, u32[]{:S(2)}) collective-permute-start(bf16[256,256]{1,0:T(8,128)(2,1)S(1)} %collective-permute-done.refs_1_), channel_id=1, source_target_pairs={{24,16},{28,20},{25,17},{29,21},{26,18},{30,22},{27,19},{31,23}} | collective-permute-start | bytes 393224 | tf_op jit(solution)/shard_map/ppermute | solution.py:305
  12.2 3.4 %rotate.1 = (bf16[256,512]{1,0:T(8,128)(2,1)S(1)}, s32[256,128]{1,0:T(8,128)S(1)}, f32[4,256,128]{2,1,0:T(8,128)S(1)}, bf16[4,512,128]{2,1,0:T(8,128)(2,1)S(1)}, bf16[4,512,128]{2,1,0:T(8,128)(2,1)S(1)}) custom-call(s32[16]{0:T(128)} %lengths_hbm.1, f32[1,128]{1,0:T(1,128)} %constant.2.clone.freq_hbm, bf16[256,256]{1,0:T(8,128)(2,1)} %key_hbm.1, ...), custom_call_target="tpu_custom_call" | custom-call | flops 3449999872 | tf_op jit(solution)/shard_map/rotate/pallas_call | solution.py:309
  15.6 0.0 collective-permute-done.1.refs_0_
  15.6 0.2 collective-permute-done.3.refs_3_
  15.8 0.0 collective-permute-done.2.refs_2_
  15.9 0.0 collective-permute-done.4.refs_4_
  15.9 0.3 pack.1
  16.2 0.1 collective-permute-start.5
  16.2 1.9 %collective-permute-done.5.refs_2_.refs_3_.refs_4_ = bf16[2,256,512]{2,1,0:T(8,128)(2,1)S(1)} collective-permute-done((bf16[2,256,512]{2,1,0:T(8,128)(2,1)S(1)}, bf16[2,256,512]{2,1,0:T(8,128)(2,1)S(1)}, u32[]{:S(2)}, u32[]{:S(2)}) %collective-permute-start.5) | collective-permute-done | bytes 524320 | tf_op jit(solution)/shard_map/ppermute | solution.py:350
  18.1 2.0 %attend.3 = (bf16[64,2048]{1,0:T(8,128)(2,1)S(1)}, f32[256,128]{1,0:T(8,128)S(1)}) custom-call(s32[256,128]{1,0:T(8,128)S(1)} %get-tuple-element.18.refs_0_.refs_1_, bf16[3,256,512]{2,1,0:T(8,128)(2,1)S(1)} %get-tuple-element.21.refs_1_.refs_2_.refs_3_, bf16[2,256,512]{2,1,0:T(8,128)(2,1)S(1)} %collective-permute-done.5.refs_2_.refs_3_.refs_4_, ...), custom_call_target="tpu_custom_call" | custom-call | flops 4600000000 | tf_op jit(solution)/shard_map/attend/pallas_call | solution.py:359
  20.2 2.7 %collective-permute-start.7 = (bf16[64,2048]{1,0:T(8,128)(2,1)S(1)}, bf16[64,2048]{1,0:T(8,128)(2,1)S(1)}, u32[]{:S(2)}, u32[]{:S(2)}) collective-permute-start(bf16[64,2048]{1,0:T(8,128)(2,1)S(1)} %get-tuple-element.30), channel_id=1, source_target_pairs={{0,2},{1,3},{2,0},{3,1},{4,6},{5,7},{6,4},{7,5},{8,10},{9,11},{10,... | collective-permute-start | bytes 786440 | tf_op jit(solution)/shard_map/ppermute | solution.py:380
  22.8 4.0 %attend.4 = (bf16[64,2048]{1,0:T(8,128)(2,1)S(1)}, bf16[64,2048]{1,0:T(8,128)(2,1)S(1)}, f32[256,128]{1,0:T(8,128)S(1)}) custom-call(s32[256,128]{1,0:T(8,128)S(1)} %get-tuple-element.18.refs_0_.refs_1_, f32[256,128]{1,0:T(8,128)S(1)} %get-tuple-element.25.refs_1_, bf16[3,256,512]{2,1,0:T(8,128)(2,1)S(1)} %get-tuple-element.21.refs_1_.refs_2_.refs_3_, ...), custom_call_target="tpu_custom_call" | custom-call | flops 9200000000 | tf_op jit(solution)/shard_map/attend/pallas_call | solution.py:359
  26.9 1.6 %collective-permute-start.6 = (bf16[64,2048]{1,0:T(8,128)(2,1)S(1)}, bf16[64,2048]{1,0:T(8,128)(2,1)S(1)}, u32[]{:S(2)}, u32[]{:S(2)}) collective-permute-start(bf16[64,2048]{1,0:T(8,128)(2,1)S(1)} %get-tuple-element.29), channel_id=1, source_target_pairs={{0,1},{1,2},{2,3},{3,0},{4,5},{5,6},{6,7},{7,4},{8,9},{9,10},{10,1... | collective-permute-start | bytes 786440 | tf_op jit(solution)/shard_map/ppermute | solution.py:380
  28.5 2.2 %collective-permute-start.8 = (bf16[64,2048]{1,0:T(8,128)(2,1)S(1)}, bf16[64,2048]{1,0:T(8,128)(2,1)S(1)}, u32[]{:S(2)}, u32[]{:S(2)}) collective-permute-start(bf16[64,2048]{1,0:T(8,128)(2,1)S(1)} %get-tuple-element.31), channel_id=1, source_target_pairs={{0,3},{1,0},{2,1},{3,2},{4,7},{5,4},{6,5},{7,6},{8,11},{9,8},{10,9... | collective-permute-start | bytes 786440 | tf_op jit(solution)/shard_map/ppermute | solution.py:380
  30.7 2.5 %attend.5 = (bf16[64,2048]{1,0:T(8,128)(2,1)S(1)}, f32[256,128]{1,0:T(8,128)S(1)}) custom-call(s32[8,8]{1,0:T(8,128)} %refs_0_.1, s32[256,128]{1,0:T(8,128)S(1)} %get-tuple-element.18.refs_0_.refs_1_, f32[256,128]{1,0:T(8,128)S(1)} %get-tuple-element.26.refs_2_, bf16[3,256,512]{2,1,0:T(8,128)(2,1)S(1)} %get-tuple-element.21.refs_1_.refs_2_.refs_3_, ...), custom_call_target="tpu_custom_call" | custom-call | flops 4600000000 | tf_op jit(solution)/shard_map/attend/pallas_call | solution.py:359
  33.3 9.2 %all_to_all.5 = f32[8,32,128]{2,1,0:T(8,128)S(1)} all-to-all(f32[8,32,128]{2,1,0:T(8,128)S(1)} %bitcast.3), channel_id=1, replica_groups=mesh['tok'=8,'kv'=4] {'tok'}, dimensions={0} | all-to-all | bytes 262144 | tf_op jit(solution)/shard_map/all_to_all | solution.py:396
  42.4 0.0 collective-permute-done.7.refs_2_
  42.4 0.0 collective-permute-done.6.refs_1_
  42.4 3.9 %collective-permute-done.8.refs_3_ = bf16[64,2048]{1,0:T(8,128)(2,1)S(1)} collective-permute-done((bf16[64,2048]{1,0:T(8,128)(2,1)S(1)}, bf16[64,2048]{1,0:T(8,128)(2,1)S(1)}, u32[]{:S(2)}, u32[]{:S(2)}) %collective-permute-start.8) | collective-permute-done | bytes 262176 | tf_op jit(solution)/shard_map/ppermute | solution.py:380
  46.4 1.0 %assemble.1 = (bf16[64,8192]{1,0:T(8,128)(2,1)}, f32[16,256]{1,0:T(8,128)}) custom-call(f32[256,128]{1,0:T(8,128)S(1)} %bitcast.2, bf16[64,2048]{1,0:T(8,128)(2,1)S(1)} %get-tuple-element.28.refs_0_, bf16[64,2048]{1,0:T(8,128)(2,1)S(1)} %collective-permute-done.6.refs_1_, bf16[64,2048]{1,0:T(8,128)(2,1)S(1)} %collective-permute-done.7.refs_2_, ...), custom_call_target="tpu_custom_call" | custom-call | tf_op jit(solution)/shard_map/assemble/pallas_call | solution.py:402
Async XLA Ops:
  0.6 10.9 %collective-permute-start = (bf16[256,256]{1,0:T(8,128)(2,1)}, bf16[256,256]{1,0:T(8,128)(2,1)S(1)}, u32[]{:S(2)}, u32[]{:S(2)}) collective-permute-start(bf16[256,256]{1,0:T(8,128)(2,1)} %key_hbm.1), channel_id=1, source_target_pairs={{0,16},{4,20},{8,24},{12,28},{1,17},{5,21},{9,25},{13,29},{2,18},{... | collective-permute-start | bytes 393224 | tf_op jit(solution)/shard_map/ppermute | solution.py:297
  5.5 10.1 %collective-permute-start.1 = (bf16[256,256]{1,0:T(8,128)(2,1)}, bf16[256,256]{1,0:T(8,128)(2,1)S(1)}, u32[]{:S(2)}, u32[]{:S(2)}) collective-permute-start(bf16[256,256]{1,0:T(8,128)(2,1)} %key_hbm.1), channel_id=1, source_target_pairs={{0,8},{4,12},{16,24},{20,28},{1,9},{5,13},{17,25},{21,29},{2,10},{... | collective-permute-start | bytes 393224 | tf_op jit(solution)/shard_map/ppermute | solution.py:304
  8.9 6.9 %collective-permute-start.3 = (bf16[256,256]{1,0:T(8,128)(2,1)}, bf16[256,256]{1,0:T(8,128)(2,1)S(1)}, u32[]{:S(2)}, u32[]{:S(2)}) collective-permute-start(bf16[256,256]{1,0:T(8,128)(2,1)} %value_hbm.1), channel_id=1, source_target_pairs={{0,16},{4,20},{8,24},{12,28},{1,17},{5,21},{9,25},{13,29},{2,18},{... | collective-permute-start | bytes 393224 | tf_op jit(solution)/shard_map/ppermute | solution.py:297
  10.2 5.6 %collective-permute-start.2 = (bf16[256,256]{1,0:T(8,128)(2,1)}, bf16[256,256]{1,0:T(8,128)(2,1)S(1)}, u32[]{:S(2)}, u32[]{:S(2)}) collective-permute-start(bf16[256,256]{1,0:T(8,128)(2,1)} %value_hbm.1), channel_id=1, source_target_pairs={{0,8},{4,12},{8,16},{12,20},{16,24},{20,28},{1,9},{5,13},{9,17},{1... | collective-permute-start | bytes 393224 | tf_op jit(solution)/shard_map/ppermute | solution.py:297
  11.5 4.3 %collective-permute-start.4 = (bf16[256,256]{1,0:T(8,128)(2,1)S(1)}, bf16[256,256]{1,0:T(8,128)(2,1)S(1)}, u32[]{:S(2)}, u32[]{:S(2)}) collective-permute-start(bf16[256,256]{1,0:T(8,128)(2,1)S(1)} %collective-permute-done.refs_1_), channel_id=1, source_target_pairs={{24,16},{28,20},{25,17},{29,21},{26,18},{30,22},{27,19},{31,23}} | collective-permute-start | bytes 393224 | tf_op jit(solution)/shard_map/ppermute | solution.py:305
  16.2 2.0 %collective-permute-start.5 = (bf16[2,256,512]{2,1,0:T(8,128)(2,1)S(1)}, bf16[2,256,512]{2,1,0:T(8,128)(2,1)S(1)}, u32[]{:S(2)}, u32[]{:S(2)}) collective-permute-start(bf16[2,256,512]{2,1,0:T(8,128)(2,1)S(1)} %get-tuple-element.22), channel_id=1, source_target_pairs={{0,4},{4,0},{8,12},{12,8},{16,20},{20,16},{24,28},{28,24},{1,5},{5... | collective-permute-start | bytes 1572872 | tf_op jit(solution)/shard_map/ppermute | solution.py:350
  20.2 22.2 %collective-permute-start.7 = (bf16[64,2048]{1,0:T(8,128)(2,1)S(1)}, bf16[64,2048]{1,0:T(8,128)(2,1)S(1)}, u32[]{:S(2)}, u32[]{:S(2)}) collective-permute-start(bf16[64,2048]{1,0:T(8,128)(2,1)S(1)} %get-tuple-element.30), channel_id=1, source_target_pairs={{0,2},{1,3},{2,0},{3,1},{4,6},{5,7},{6,4},{7,5},{8,10},{9,11},{10,... | collective-permute-start | bytes 786440 | tf_op jit(solution)/shard_map/ppermute | solution.py:380
  26.9 15.6 %collective-permute-start.6 = (bf16[64,2048]{1,0:T(8,128)(2,1)S(1)}, bf16[64,2048]{1,0:T(8,128)(2,1)S(1)}, u32[]{:S(2)}, u32[]{:S(2)}) collective-permute-start(bf16[64,2048]{1,0:T(8,128)(2,1)S(1)} %get-tuple-element.29), channel_id=1, source_target_pairs={{0,1},{1,2},{2,3},{3,0},{4,5},{5,6},{6,7},{7,4},{8,9},{9,10},{10,1... | collective-permute-start | bytes 786440 | tf_op jit(solution)/shard_map/ppermute | solution.py:380
  28.5 17.9 %collective-permute-start.8 = (bf16[64,2048]{1,0:T(8,128)(2,1)S(1)}, bf16[64,2048]{1,0:T(8,128)(2,1)S(1)}, u32[]{:S(2)}, u32[]{:S(2)}) collective-permute-start(bf16[64,2048]{1,0:T(8,128)(2,1)S(1)} %get-tuple-element.31), channel_id=1, source_target_pairs={{0,3},{1,0},{2,1},{3,2},{4,7},{5,4},{6,5},{7,6},{8,11},{9,8},{10,9... | collective-permute-start | bytes 786440 | tf_op jit(solution)/shard_map/ppermute | solution.py:380

commit v4 on v3

--- a/solution.py
+++ b/solution.py
@@ -260,8 +260,7 @@
         lse_ref[...] = norms[...]
 
 
-def assemble_kernel(planes, width, groups, places, served_ref, *refs):
-    pieces, out_ref, lse_hbm, lse_ref, sems = refs[:-4], *refs[-4:]
+def placed(planes, width, groups, places, pieces, out_ref, sems):
     z = lax.axis_index("kv")
     copies = []
     for index, (s, group) in enumerate(places):
@@ -269,6 +268,21 @@
         column = pl.multiple_of((origin * groups + group) * width, width)
         target = out_ref.at[:, pl.ds(column, pieces[index].shape[1])]
         copies.append(pltpu.make_async_copy(pieces[index], target, sems.at[index]))
+    return copies
+
+
+def begin_kernel(planes, width, groups, places, *refs):
+    pieces, out_ref, sems = refs[:-2], *refs[-2:]
+    copies = placed(planes, width, groups, places, pieces, out_ref, sems)
+    for c in copies:
+        c.start()
+    for c in copies:
+        c.wait()
+
+
+def assemble_kernel(planes, width, groups, places, served_ref, *refs):
+    pieces, out_ref, lse_hbm, lse_ref, sems = refs[:-5], *refs[-4:]
+    copies = placed(planes, width, groups, places, pieces, out_ref, sems)
     for c in copies:
         c.start()
     lse_ref[...] = served_ref[...].T[: lse_ref.shape[0]]
@@ -380,13 +394,8 @@
         return lax.ppermute(piece, "kv", [(i, (i + s) % planes) for i in range(planes)])
 
     norm, pieces_of = None, {}
-    middle, both = planes // 2, list(range(groups))
-    spans = [range(middle, middle + 1), range(1, planes, 2)]
-    spans += [range(s, s + 1) for s in range(2, planes, 2) if s != middle]
-    for used in [both]:
-        (piece,), norm = attend(norm, used, spans[0], False, 2.0 * len(used))
-        pieces_of[middle, used[0]] = send(piece, middle)
-    for span in spans[1:]:
+    both = list(range(groups))
+    for span in (range(1, 2), range(2, planes)):
         result, norm = attend(norm, both, span, False, 4.0 * len(span))
         for s, piece in zip(span, result):
             pieces_of[s, 0] = send(piece, s)
@@ -396,23 +405,32 @@
     served = lax.all_to_all(
         norm.reshape(shards, block_rows, HEAD_DIM), "tok", split_axis=0, concat_axis=0, tiled=True
     ).reshape(rows, HEAD_DIM)
-    places = sorted(pieces_of)
-    flat = [pieces_of[place] for place in places]
+    width = per_group * HEAD_DIM
+    out_shape = jax.ShapeDtypeStruct((tile, planes * heads * HEAD_DIM), jnp.bfloat16)
+    soon = [place for place in sorted(pieces_of) if place[0] < 2]
+    late = [place for place in sorted(pieces_of) if place[0] >= 2]
+    with jax.named_scope("begin"):
+        begun = pl.pallas_call(
+            partial(begin_kernel, planes, width, groups, soon),
+            out_shape=out_shape,
+            in_specs=[hbm()] * len(soon),
+            out_specs=hbm(),
+            scratch_shapes=[pltpu.SemaphoreType.DMA((len(soon),))],
+            compiler_params=params(),
+        )(*[pieces_of[place] for place in soon])
     with jax.named_scope("assemble"):
         attention_out, served_lse = pl.pallas_call(
-            partial(assemble_kernel, planes, per_group * HEAD_DIM, groups, places),
-            out_shape=[
-                jax.ShapeDtypeStruct((tile, planes * heads * HEAD_DIM), jnp.bfloat16),
-                jax.ShapeDtypeStruct((heads, rows), jnp.float32),
-            ],
-            in_specs=[vmem()] + [hbm()] * len(flat),
+            partial(assemble_kernel, planes, width, groups, late),
+            out_shape=[out_shape, jax.ShapeDtypeStruct((heads, rows), jnp.float32)],
+            in_specs=[vmem()] + [hbm()] * (len(late) + 1),
             out_specs=[hbm(), hbm()],
             scratch_shapes=[
                 pltpu.VMEM((heads, rows), jnp.float32),
-                pltpu.SemaphoreType.DMA((len(flat) + 1,)),
+                pltpu.SemaphoreType.DMA((len(late) + 1,)),
             ],
+            input_output_aliases={len(late) + 1: 0},
             compiler_params=params(),
-        )(served, *flat)
+        )(served, *[pieces_of[place] for place in late], begun)
     return (attention_out, served_lse)
 
 

time: 47.6 us -> 47.3 us (level)
  the two profiles are of different devices: /device:TPU:0 before, /device:TPU:13 now
where the time goes in v4:
time: 47.3 us; the launch traced here: 46.9 us
  starting transfers between devices  18.8 us (40%)
  Pallas kernels  14.5 us (31%)
  waiting for transfers between devices  12.8 us (27%)
  between operations  0.73 us (2%)
    pallas_call x3, Pallas kernels, attend(): pl.pallas_call(partial(attend_kernel, pieces, per_group, used, tiles_of,...  9.23 us
    ppermute x3, waiting for transfers between devices, send(): lax.ppermute(piece, 'kv', [(i, (i + s) % planes) for i in range(planes)])  7.23 us
    ppermute x3, starting transfers between devices, forward(): lax.ppermute(x, 'tok', [(i, i + 2 * p) for i in range(shards - 2 * p)])  4.5 us
    all_to_all x1, starting transfers between devices, body(): lax.all_to_all(norm.reshape(shards, block_rows, HEAD_DIM), 'tok', split_a...  4.16 us
    ppermute x3, starting transfers between devices, send(): lax.ppermute(piece, 'kv', [(i, (i + s) % planes) for i in range(planes)])  3.89 us
    pallas_call x1, Pallas kernels, body(): pl.pallas_call(partial(queries_kernel, pieces), out_shape=[pack_shape, ja...  3.38 us
    ppermute x1, starting transfers between devices, body(): lax.ppermute(key_states, 'tok', [(0, 2), (1, 3), (4, 6), (5, 7)])  3.12 us
    all_to_all x1, waiting for transfers between devices, body(): lax.all_to_all(norm.reshape(shards, block_rows, HEAD_DIM), 'tok', split_a...  2.74 us
  transfers between devices with their start and end apart: 10, of which 6 were waited for; matrix products, arithmetic and copies ran while one was open for 0% of the time, Pallas kernels for 24%

profile of v4, /device:TPU:13, one launch (start us, length us, event | category | flops | bytes accessed | tf_op | source)
XLA Modules:
  0.0 46.9 jit_solution(6880509295120329346)
XLA Ops:
  0.6 1.3 %collective-permute-start = (bf16[256,256]{1,0:T(8,128)(2,1)}, bf16[256,256]{1,0:T(8,128)(2,1)S(1)}, u32[]{:S(2)}, u32[]{:S(2)}) collective-permute-start(bf16[256,256]{1,0:T(8,128)(2,1)} %key_hbm.1), channel_id=1, source_target_pairs={{0,16},{4,20},{8,24},{12,28},{1,17},{5,21},{9,25},{13,29},{2,18},{... | collective-permute-start | bytes 393224 | tf_op jit(solution)/shard_map/ppermute | solution.py:311
  1.9 3.1 %collective-permute-start.1 = (bf16[256,256]{1,0:T(8,128)(2,1)}, bf16[256,256]{1,0:T(8,128)(2,1)S(1)}, u32[]{:S(2)}, u32[]{:S(2)}) collective-permute-start(bf16[256,256]{1,0:T(8,128)(2,1)} %key_hbm.1), channel_id=1, source_target_pairs={{0,8},{4,12},{16,24},{20,28},{1,9},{5,13},{17,25},{21,29},{2,10},{... | collective-permute-start | bytes 393224 | tf_op jit(solution)/shard_map/ppermute | solution.py:318
  5.1 1.3 %collective-permute-start.3 = (bf16[256,256]{1,0:T(8,128)(2,1)}, bf16[256,256]{1,0:T(8,128)(2,1)S(1)}, u32[]{:S(2)}, u32[]{:S(2)}) collective-permute-start(bf16[256,256]{1,0:T(8,128)(2,1)} %value_hbm.1), channel_id=1, source_target_pairs={{0,16},{4,20},{8,24},{12,28},{1,17},{5,21},{9,25},{13,29},{2,18},{... | collective-permute-start | bytes 393224 | tf_op jit(solution)/shard_map/ppermute | solution.py:311
  6.4 1.9 %collective-permute-start.2 = (bf16[256,256]{1,0:T(8,128)(2,1)}, bf16[256,256]{1,0:T(8,128)(2,1)S(1)}, u32[]{:S(2)}, u32[]{:S(2)}) collective-permute-start(bf16[256,256]{1,0:T(8,128)(2,1)} %value_hbm.1), channel_id=1, source_target_pairs={{0,8},{4,12},{8,16},{12,20},{16,24},{20,28},{1,9},{5,13},{9,17},{1... | collective-permute-start | bytes 393224 | tf_op jit(solution)/shard_map/ppermute | solution.py:311
  8.3 0.0 collective-permute-done.refs_1_
  8.3 1.3 %collective-permute-start.4 = (bf16[256,256]{1,0:T(8,128)(2,1)S(1)}, bf16[256,256]{1,0:T(8,128)(2,1)S(1)}, u32[]{:S(2)}, u32[]{:S(2)}) collective-permute-start(bf16[256,256]{1,0:T(8,128)(2,1)S(1)} %collective-permute-done.refs_1_), channel_id=1, source_target_pairs={{24,16},{28,20},{25,17},{29,21},{26,18},{30,22},{27,19},{31,23}} | collective-permute-start | bytes 393224 | tf_op jit(solution)/shard_map/ppermute | solution.py:319
  9.6 3.4 %rotate.1 = (bf16[256,512]{1,0:T(8,128)(2,1)S(1)}, s32[256,128]{1,0:T(8,128)S(1)}, f32[4,256,128]{2,1,0:T(8,128)S(1)}, bf16[4,512,128]{2,1,0:T(8,128)(2,1)S(1)}, bf16[4,512,128]{2,1,0:T(8,128)(2,1)S(1)}) custom-call(s32[16]{0:T(128)} %lengths_hbm.1, f32[1,128]{1,0:T(1,128)} %constant.2.clone.freq_hbm, bf16[256,256]{1,0:T(8,128)(2,1)} %key_hbm.1, ...), custom_call_target="tpu_custom_call" | custom-call | flops 3449999872 | tf_op jit(solution)/shard_map/rotate/pallas_call | solution.py:323
  13.0 0.0 collective-permute-done.1.refs_0_
  13.0 0.0 collective-permute-done.3.refs_3_
  13.0 0.3 collective-permute-done.2.refs_2_
  13.3 1.0 %collective-permute-done.4.refs_4_ = bf16[256,256]{1,0:T(8,128)(2,1)S(1)} collective-permute-done((bf16[256,256]{1,0:T(8,128)(2,1)S(1)}, bf16[256,256]{1,0:T(8,128)(2,1)S(1)}, u32[]{:S(2)}, u32[]{:S(2)}) %collective-permute-start.4) | collective-permute-done | bytes 131104 | tf_op jit(solution)/shard_map/ppermute | solution.py:319
  14.3 0.3 pack.1
  14.6 1.9 %collective-permute-start.5 = (bf16[2,256,512]{2,1,0:T(8,128)(2,1)S(1)}, bf16[2,256,512]{2,1,0:T(8,128)(2,1)S(1)}, u32[]{:S(2)}, u32[]{:S(2)}) collective-permute-start(bf16[2,256,512]{2,1,0:T(8,128)(2,1)S(1)} %get-tuple-element.22), channel_id=1, source_target_pairs={{0,4},{4,0},{8,12},{12,8},{16,20},{20,16},{24,28},{28,24},{1,5},{5... | collective-permute-start | bytes 1572872 | tf_op jit(solution)/shard_map/ppermute | solution.py:364
  16.5 1.5 %collective-permute-done.5.refs_2_.refs_3_.refs_4_ = bf16[2,256,512]{2,1,0:T(8,128)(2,1)S(1)} collective-permute-done((bf16[2,256,512]{2,1,0:T(8,128)(2,1)S(1)}, bf16[2,256,512]{2,1,0:T(8,128)(2,1)S(1)}, u32[]{:S(2)}, u32[]{:S(2)}) %collective-permute-start.5) | collective-permute-done | bytes 524320 | tf_op jit(solution)/shard_map/ppermute | solution.py:364
  18.0 2.0 %attend.3 = (bf16[64,2048]{1,0:T(8,128)(2,1)S(1)}, f32[256,128]{1,0:T(8,128)S(1)}) custom-call(s32[256,128]{1,0:T(8,128)S(1)} %get-tuple-element.18.refs_0_.refs_1_, bf16[3,256,512]{2,1,0:T(8,128)(2,1)S(1)} %get-tuple-element.21.refs_1_.refs_2_.refs_3_, bf16[2,256,512]{2,1,0:T(8,128)(2,1)S(1)} %collective-permute-done.5.refs_2_.refs_3_.refs_4_, ...), custom_call_target="tpu_custom_call" | custom-call | flops 4600000000 | tf_op jit(solution)/shard_map/attend/pallas_call | solution.py:373
  20.1 1.3 %collective-permute-start.8 = (bf16[64,2048]{1,0:T(8,128)(2,1)S(1)}, bf16[64,2048]{1,0:T(8,128)(2,1)S(1)}, u32[]{:S(2)}, u32[]{:S(2)}) collective-permute-start(bf16[64,2048]{1,0:T(8,128)(2,1)S(1)} %get-tuple-element.31), channel_id=1, source_target_pairs={{0,1},{1,2},{2,3},{3,0},{4,5},{5,6},{6,7},{7,4},{8,9},{9,10},{10,1... | collective-permute-start | bytes 786440 | tf_op jit(solution)/shard_map/ppermute | solution.py:394
  21.4 4.0 %attend.4 = (bf16[64,2048]{1,0:T(8,128)(2,1)S(1)}, bf16[64,2048]{1,0:T(8,128)(2,1)S(1)}, f32[256,128]{1,0:T(8,128)S(1)}) custom-call(s32[256,128]{1,0:T(8,128)S(1)} %get-tuple-element.18.refs_0_.refs_1_, f32[256,128]{1,0:T(8,128)S(1)} %get-tuple-element.25.refs_1_, bf16[3,256,512]{2,1,0:T(8,128)(2,1)S(1)} %get-tuple-element.21.refs_1_.refs_2_.refs_3_, ...), custom_call_target="tpu_custom_call" | custom-call | flops 9200000000 | tf_op jit(solution)/shard_map/attend/pallas_call | solution.py:373
  25.4 1.1 %collective-permute-start.6 = (bf16[64,2048]{1,0:T(8,128)(2,1)S(1)}, bf16[64,2048]{1,0:T(8,128)(2,1)S(1)}, u32[]{:S(2)}, u32[]{:S(2)}) collective-permute-start(bf16[64,2048]{1,0:T(8,128)(2,1)S(1)} %get-tuple-element.28), channel_id=1, source_target_pairs={{0,2},{1,3},{2,0},{3,1},{4,6},{5,7},{6,4},{7,5},{8,10},{9,11},{10,... | collective-permute-start | bytes 786440 | tf_op jit(solution)/shard_map/ppermute | solution.py:394
  26.5 1.4 %collective-permute-start.7 = (bf16[64,2048]{1,0:T(8,128)(2,1)S(1)}, bf16[64,2048]{1,0:T(8,128)(2,1)S(1)}, u32[]{:S(2)}, u32[]{:S(2)}) collective-permute-start(bf16[64,2048]{1,0:T(8,128)(2,1)S(1)} %get-tuple-element.29), channel_id=1, source_target_pairs={{0,3},{1,0},{2,1},{3,2},{4,7},{5,4},{6,5},{7,6},{8,11},{9,8},{10,9... | collective-permute-start | bytes 786440 | tf_op jit(solution)/shard_map/ppermute | solution.py:394
  28.0 3.2 %attend.5 = (bf16[64,2048]{1,0:T(8,128)(2,1)S(1)}, f32[256,128]{1,0:T(8,128)}) custom-call(s32[8,8]{1,0:T(8,128)} %refs_0_.1, s32[256,128]{1,0:T(8,128)S(1)} %get-tuple-element.18.refs_0_.refs_1_, f32[256,128]{1,0:T(8,128)S(1)} %get-tuple-element.26.refs_2_, bf16[3,256,512]{2,1,0:T(8,128)(2,1)S(1)} %get-tuple-element.21.refs_1_.refs_2_.refs_3_, ...), custom_call_target="tpu_custom_call" | custom-call | flops 4600000000 | tf_op jit(solution)/shard_map/attend/pallas_call | solution.py:373
  31.2 4.2 %all-to-all-start = ((f32[8,32,128]{2,1,0:T(8,128)}), f32[8,32,128]{2,1,0:T(8,128)S(1)}, u32[]{:S(2)}, u32[]{:S(2)}) async-start(f32[8,32,128]{2,1,0:T(8,128)} %bitcast), calls=%async_computation | async-start | bytes 262144 | tf_op jit(solution)/shard_map/all_to_all | solution.py:405
  35.3 0.0 collective-permute-done.8.refs_1_
  35.3 0.8 %begin.1.refs_2_ = bf16[64,8192]{1,0:T(8,128)(2,1)} custom-call(bf16[64,2048]{1,0:T(8,128)(2,1)S(1)} %get-tuple-element.30.refs_0_, bf16[64,2048]{1,0:T(8,128)(2,1)S(1)} %collective-permute-done.8.refs_1_), custom_call_target="tpu_custom_call" | custom-call | tf_op jit(solution)/shard_map/begin/pallas_call | solution.py:413
  36.1 2.7 %all-to-all-done = f32[8,32,128]{2,1,0:T(8,128)S(1)} async-done(((f32[8,32,128]{2,1,0:T(8,128)}), f32[8,32,128]{2,1,0:T(8,128)S(1)}, u32[]{:S(2)}, u32[]{:S(2)}) %all-to-all-start) | async-done | bytes 131104 | tf_op jit(solution)/shard_map/all_to_all | solution.py:405
  38.9 5.0 %collective-permute-done.6.refs_0_ = bf16[64,2048]{1,0:T(8,128)(2,1)S(1)} collective-permute-done((bf16[64,2048]{1,0:T(8,128)(2,1)S(1)}, bf16[64,2048]{1,0:T(8,128)(2,1)S(1)}, u32[]{:S(2)}, u32[]{:S(2)}) %collective-permute-start.6) | collective-permute-done | bytes 262176 | tf_op jit(solution)/shard_map/ppermute | solution.py:394
  43.9 2.2 %collective-permute-done.7.refs_1_ = bf16[64,2048]{1,0:T(8,128)(2,1)S(1)} collective-permute-done((bf16[64,2048]{1,0:T(8,128)(2,1)S(1)}, bf16[64,2048]{1,0:T(8,128)(2,1)S(1)}, u32[]{:S(2)}, u32[]{:S(2)}) %collective-permute-start.7) | collective-permute-done | bytes 262176 | tf_op jit(solution)/shard_map/ppermute | solution.py:394
  46.1 0.8 %assemble.1 = (bf16[64,8192]{1,0:T(8,128)(2,1)}, f32[16,256]{1,0:T(8,128)}) custom-call(f32[256,128]{1,0:T(8,128)S(1)} %bitcast.2, bf16[64,2048]{1,0:T(8,128)(2,1)S(1)} %collective-permute-done.6.refs_0_, bf16[64,2048]{1,0:T(8,128)(2,1)S(1)} %collective-permute-done.7.refs_1_, bf16[64,8192]{1,0:T(8,128)(2,1)} %begin.1.refs_2_), custom_call_target="tpu_custom_call", output_to_operand_aliasing={{0}: (3, {})} | custom-call | tf_op jit(solution)/shard_map/assemble/pallas_call | solution.py:422
Async XLA Ops:
  0.6 7.7 %collective-permute-start = (bf16[256,256]{1,0:T(8,128)(2,1)}, bf16[256,256]{1,0:T(8,128)(2,1)S(1)}, u32[]{:S(2)}, u32[]{:S(2)}) collective-permute-start(bf16[256,256]{1,0:T(8,128)(2,1)} %key_hbm.1), channel_id=1, source_target_pairs={{0,16},{4,20},{8,24},{12,28},{1,17},{5,21},{9,25},{13,29},{2,18},{... | collective-permute-start | bytes 393224 | tf_op jit(solution)/shard_map/ppermute | solution.py:311
  1.9 11.1 %collective-permute-start.1 = (bf16[256,256]{1,0:T(8,128)(2,1)}, bf16[256,256]{1,0:T(8,128)(2,1)S(1)}, u32[]{:S(2)}, u32[]{:S(2)}) collective-permute-start(bf16[256,256]{1,0:T(8,128)(2,1)} %key_hbm.1), channel_id=1, source_target_pairs={{0,8},{4,12},{16,24},{20,28},{1,9},{5,13},{17,25},{21,29},{2,10},{... | collective-permute-start | bytes 393224 | tf_op jit(solution)/shard_map/ppermute | solution.py:318
  5.1 7.9 %collective-permute-start.3 = (bf16[256,256]{1,0:T(8,128)(2,1)}, bf16[256,256]{1,0:T(8,128)(2,1)S(1)}, u32[]{:S(2)}, u32[]{:S(2)}) collective-permute-start(bf16[256,256]{1,0:T(8,128)(2,1)} %value_hbm.1), channel_id=1, source_target_pairs={{0,16},{4,20},{8,24},{12,28},{1,17},{5,21},{9,25},{13,29},{2,18},{... | collective-permute-start | bytes 393224 | tf_op jit(solution)/shard_map/ppermute | solution.py:311
  6.4 6.9 %collective-permute-start.2 = (bf16[256,256]{1,0:T(8,128)(2,1)}, bf16[256,256]{1,0:T(8,128)(2,1)S(1)}, u32[]{:S(2)}, u32[]{:S(2)}) collective-permute-start(bf16[256,256]{1,0:T(8,128)(2,1)} %value_hbm.1), channel_id=1, source_target_pairs={{0,8},{4,12},{8,16},{12,20},{16,24},{20,28},{1,9},{5,13},{9,17},{1... | collective-permute-start | bytes 393224 | tf_op jit(solution)/shard_map/ppermute | solution.py:311
  8.3 6.0 %collective-permute-start.4 = (bf16[256,256]{1,0:T(8,128)(2,1)S(1)}, bf16[256,256]{1,0:T(8,128)(2,1)S(1)}, u32[]{:S(2)}, u32[]{:S(2)}) collective-permute-start(bf16[256,256]{1,0:T(8,128)(2,1)S(1)} %collective-permute-done.refs_1_), channel_id=1, source_target_pairs={{24,16},{28,20},{25,17},{29,21},{26,18},{30,22},{27,19},{31,23}} | collective-permute-start | bytes 393224 | tf_op jit(solution)/shard_map/ppermute | solution.py:319
  14.6 3.4 %collective-permute-start.5 = (bf16[2,256,512]{2,1,0:T(8,128)(2,1)S(1)}, bf16[2,256,512]{2,1,0:T(8,128)(2,1)S(1)}, u32[]{:S(2)}, u32[]{:S(2)}) collective-permute-start(bf16[2,256,512]{2,1,0:T(8,128)(2,1)S(1)} %get-tuple-element.22), channel_id=1, source_target_pairs={{0,4},{4,0},{8,12},{12,8},{16,20},{20,16},{24,28},{28,24},{1,5},{5... | collective-permute-start | bytes 1572872 | tf_op jit(solution)/shard_map/ppermute | solution.py:364
  20.1 15.2 %collective-permute-start.8 = (bf16[64,2048]{1,0:T(8,128)(2,1)S(1)}, bf16[64,2048]{1,0:T(8,128)(2,1)S(1)}, u32[]{:S(2)}, u32[]{:S(2)}) collective-permute-start(bf16[64,2048]{1,0:T(8,128)(2,1)S(1)} %get-tuple-element.31), channel_id=1, source_target_pairs={{0,1},{1,2},{2,3},{3,0},{4,5},{5,6},{6,7},{7,4},{8,9},{9,10},{10,1... | collective-permute-start | bytes 786440 | tf_op jit(solution)/shard_map/ppermute | solution.py:394
  25.4 18.4 %collective-permute-start.6 = (bf16[64,2048]{1,0:T(8,128)(2,1)S(1)}, bf16[64,2048]{1,0:T(8,128)(2,1)S(1)}, u32[]{:S(2)}, u32[]{:S(2)}) collective-permute-start(bf16[64,2048]{1,0:T(8,128)(2,1)S(1)} %get-tuple-element.28), channel_id=1, source_target_pairs={{0,2},{1,3},{2,0},{3,1},{4,6},{5,7},{6,4},{7,5},{8,10},{9,11},{10,... | collective-permute-start | bytes 786440 | tf_op jit(solution)/shard_map/ppermute | solution.py:394
  26.5 19.6 %collective-permute-start.7 = (bf16[64,2048]{1,0:T(8,128)(2,1)S(1)}, bf16[64,2048]{1,0:T(8,128)(2,1)S(1)}, u32[]{:S(2)}, u32[]{:S(2)}) collective-permute-start(bf16[64,2048]{1,0:T(8,128)(2,1)S(1)} %get-tuple-element.29), channel_id=1, source_target_pairs={{0,3},{1,0},{2,1},{3,2},{4,7},{5,4},{6,5},{7,6},{8,11},{9,8},{10,9... | collective-permute-start | bytes 786440 | tf_op jit(solution)/shard_map/ppermute | solution.py:394
  31.2 7.7 %all-to-all-start = ((f32[8,32,128]{2,1,0:T(8,128)}), f32[8,32,128]{2,1,0:T(8,128)S(1)}, u32[]{:S(2)}, u32[]{:S(2)}) async-start(f32[8,32,128]{2,1,0:T(8,128)} %bitcast), calls=%async_computation | async-start | bytes 262144 | tf_op jit(solution)/shard_map/all_to_all | solution.py:405

commit v5 on v4

--- a/solution.py
+++ b/solution.py
@@ -171,6 +171,7 @@
     chunk = min(stacked, 256)
     inside = chunk // tile
     ones = jnp.ones((rows, HEAD_DIM), jnp.bfloat16)
+    unrolled = slots <= 5
     norms[...] = norm_ref[...] if begun else jnp.zeros(norms.shape, jnp.float32)
 
     def masks_of(t):
@@ -224,7 +225,10 @@
             head = c * inside + h
             part = slice(h * tile, (h + 1) * tile)
             column_of = (index * per_group + head) * HEAD_DIM
-            staged[i, :, column_of : column_of + HEAD_DIM] = result[part]
+            if unrolled:
+                out_refs[i][:, column_of : column_of + HEAD_DIM] = result[part]
+            else:
+                staged[i, :, column_of : column_of + HEAD_DIM] = result[part]
             gathered = jnp.where(column == group * per_group + head, norm[part], gathered)
         return gathered
 
@@ -245,10 +249,13 @@
         norms[here, :] = gathered
         return carry
 
-    lax.fori_loop(0, len(tiles_of), step, 0, unroll=slots <= 5)
-
-    for position, out_ref in enumerate(out_refs):
-        out_ref[...] = staged[position]
+    if unrolled:
+        for i in range(len(tiles_of)):
+            step(i, 0)
+    else:
+        lax.fori_loop(0, len(tiles_of), step, 0)
+        for position, out_ref in enumerate(out_refs):
+            out_ref[...] = staged[position]
     if last:
         plan_copy.wait()
         shards = plan_ref.shape[0]

time: 47.3 us -> 47.2 us (level)
  Pallas kernels: 14.5 us -> 13.9 us
  waiting for transfers between devices: 12.8 us -> 13.4 us
    pallas_call x3, Pallas kernels: 9.23 us -> 8.62 us  [attend(): pl.pallas_call(partial(attend_kernel, pieces, per_group, used, tiles_of,...]
    ppermute x3, waiting for transfers between devices: 7.23 us -> 7.79 us  [send(): lax.ppermute(piece, 'kv', [(i, (i + s) % planes) for i in range(planes)])]
  transfers between devices with their start and end apart: 10 -> 10, of which waited for: 6 -> 6; matrix products, arithmetic and copies ran while one was open for 0% -> 0% of each run, Pallas kernels for 24% -> 23%
where the time goes in v5:
time: 47.2 us; the launch traced here: 46.9 us
  starting transfers between devices  18.9 us (40%)
  Pallas kernels  13.9 us (29%)
  waiting for transfers between devices  13.4 us (28%)
  between operations  0.73 us (2%)
    pallas_call x3, Pallas kernels, attend(): pl.pallas_call(partial(attend_kernel, pieces, per_group, used, tiles_of,...  8.62 us
    ppermute x3, waiting for transfers between devices, send(): lax.ppermute(piece, 'kv', [(i, (i + s) % planes) for i in range(planes)])  7.79 us
    ppermute x3, starting transfers between devices, forward(): lax.ppermute(x, 'tok', [(i, i + 2 * p) for i in range(shards - 2 * p)])  4.5 us
    all_to_all x1, starting transfers between devices, body(): lax.all_to_all(norm.reshape(shards, block_rows, HEAD_DIM), 'tok', split_a...  4.16 us
    ppermute x3, starting transfers between devices, send(): lax.ppermute(piece, 'kv', [(i, (i + s) % planes) for i in range(planes)])  3.9 us
    pallas_call x1, Pallas kernels, body(): pl.pallas_call(partial(queries_kernel, pieces), out_shape=[pack_shape, ja...  3.38 us
    ppermute x1, starting transfers between devices, body(): lax.ppermute(key_states, 'tok', [(0, 2), (1, 3), (4, 6), (5, 7)])  3.12 us
    all_to_all x1, waiting for transfers between devices, body(): lax.all_to_all(norm.reshape(shards, block_rows, HEAD_DIM), 'tok', split_a...  2.74 us
  transfers between devices with their start and end apart: 10, of which 6 were waited for; matrix products, arithmetic and copies ran while one was open for 0% of the time, Pallas kernels for 23%

profile of v5, /device:TPU:13, one launch (start us, length us, event | category | flops | bytes accessed | tf_op | source)
XLA Modules:
  0.0 46.9 jit_solution(5541582724064259703)
XLA Ops:
  0.6 1.3 %collective-permute-start = (bf16[256,256]{1,0:T(8,128)(2,1)}, bf16[256,256]{1,0:T(8,128)(2,1)S(1)}, u32[]{:S(2)}, u32[]{:S(2)}) collective-permute-start(bf16[256,256]{1,0:T(8,128)(2,1)} %key_hbm.1), channel_id=1, source_target_pairs={{0,16},{4,20},{8,24},{12,28},{1,17},{5,21},{9,25},{13,29},{2,18},{... | collective-permute-start | bytes 393224 | tf_op jit(solution)/shard_map/ppermute | solution.py:318
  1.9 3.1 %collective-permute-start.1 = (bf16[256,256]{1,0:T(8,128)(2,1)}, bf16[256,256]{1,0:T(8,128)(2,1)S(1)}, u32[]{:S(2)}, u32[]{:S(2)}) collective-permute-start(bf16[256,256]{1,0:T(8,128)(2,1)} %key_hbm.1), channel_id=1, source_target_pairs={{0,8},{4,12},{16,24},{20,28},{1,9},{5,13},{17,25},{21,29},{2,10},{... | collective-permute-start | bytes 393224 | tf_op jit(solution)/shard_map/ppermute | solution.py:325
  5.1 1.3 %collective-permute-start.3 = (bf16[256,256]{1,0:T(8,128)(2,1)}, bf16[256,256]{1,0:T(8,128)(2,1)S(1)}, u32[]{:S(2)}, u32[]{:S(2)}) collective-permute-start(bf16[256,256]{1,0:T(8,128)(2,1)} %value_hbm.1), channel_id=1, source_target_pairs={{0,16},{4,20},{8,24},{12,28},{1,17},{5,21},{9,25},{13,29},{2,18},{... | collective-permute-start | bytes 393224 | tf_op jit(solution)/shard_map/ppermute | solution.py:318
  6.4 1.9 %collective-permute-start.2 = (bf16[256,256]{1,0:T(8,128)(2,1)}, bf16[256,256]{1,0:T(8,128)(2,1)S(1)}, u32[]{:S(2)}, u32[]{:S(2)}) collective-permute-start(bf16[256,256]{1,0:T(8,128)(2,1)} %value_hbm.1), channel_id=1, source_target_pairs={{0,8},{4,12},{8,16},{12,20},{16,24},{20,28},{1,9},{5,13},{9,17},{1... | collective-permute-start | bytes 393224 | tf_op jit(solution)/shard_map/ppermute | solution.py:318
  8.3 0.0 collective-permute-done.refs_1_
  8.3 1.3 %collective-permute-start.4 = (bf16[256,256]{1,0:T(8,128)(2,1)S(1)}, bf16[256,256]{1,0:T(8,128)(2,1)S(1)}, u32[]{:S(2)}, u32[]{:S(2)}) collective-permute-start(bf16[256,256]{1,0:T(8,128)(2,1)S(1)} %collective-permute-done.refs_1_), channel_id=1, source_target_pairs={{24,16},{28,20},{25,17},{29,21},{26,18},{30,22},{27,19},{31,23}} | collective-permute-start | bytes 393224 | tf_op jit(solution)/shard_map/ppermute | solution.py:326
  9.6 3.4 %rotate.1 = (bf16[256,512]{1,0:T(8,128)(2,1)S(1)}, s32[256,128]{1,0:T(8,128)S(1)}, f32[4,256,128]{2,1,0:T(8,128)S(1)}, bf16[4,512,128]{2,1,0:T(8,128)(2,1)S(1)}, bf16[4,512,128]{2,1,0:T(8,128)(2,1)S(1)}) custom-call(s32[16]{0:T(128)} %lengths_hbm.1, f32[1,128]{1,0:T(1,128)} %constant.2.clone.freq_hbm, bf16[256,256]{1,0:T(8,128)(2,1)} %key_hbm.1, ...), custom_call_target="tpu_custom_call" | custom-call | flops 3449999872 | tf_op jit(solution)/shard_map/rotate/pallas_call | solution.py:330
  13.0 0.0 collective-permute-done.1.refs_0_
  13.0 0.0 collective-permute-done.3.refs_3_
  13.0 0.3 collective-permute-done.2.refs_2_
  13.3 1.0 %collective-permute-done.4.refs_4_ = bf16[256,256]{1,0:T(8,128)(2,1)S(1)} collective-permute-done((bf16[256,256]{1,0:T(8,128)(2,1)S(1)}, bf16[256,256]{1,0:T(8,128)(2,1)S(1)}, u32[]{:S(2)}, u32[]{:S(2)}) %collective-permute-start.4) | collective-permute-done | bytes 131104 | tf_op jit(solution)/shard_map/ppermute | solution.py:326
  14.3 0.3 pack.1
  14.6 1.9 %collective-permute-start.5 = (bf16[2,256,512]{2,1,0:T(8,128)(2,1)S(1)}, bf16[2,256,512]{2,1,0:T(8,128)(2,1)S(1)}, u32[]{:S(2)}, u32[]{:S(2)}) collective-permute-start(bf16[2,256,512]{2,1,0:T(8,128)(2,1)S(1)} %get-tuple-element.22), channel_id=1, source_target_pairs={{0,4},{4,0},{8,12},{12,8},{16,20},{20,16},{24,28},{28,24},{1,5},{5... | collective-permute-start | bytes 1572872 | tf_op jit(solution)/shard_map/ppermute | solution.py:371
  16.5 1.5 %collective-permute-done.5.refs_2_.refs_3_.refs_4_ = bf16[2,256,512]{2,1,0:T(8,128)(2,1)S(1)} collective-permute-done((bf16[2,256,512]{2,1,0:T(8,128)(2,1)S(1)}, bf16[2,256,512]{2,1,0:T(8,128)(2,1)S(1)}, u32[]{:S(2)}, u32[]{:S(2)}) %collective-permute-start.5) | collective-permute-done | bytes 524320 | tf_op jit(solution)/shard_map/ppermute | solution.py:371
  18.0 2.0 %attend.3 = (bf16[64,2048]{1,0:T(8,128)(2,1)S(1)}, f32[256,128]{1,0:T(8,128)S(1)}) custom-call(s32[256,128]{1,0:T(8,128)S(1)} %get-tuple-element.18.refs_0_.refs_1_, bf16[3,256,512]{2,1,0:T(8,128)(2,1)S(1)} %get-tuple-element.21.refs_1_.refs_2_.refs_3_, bf16[2,256,512]{2,1,0:T(8,128)(2,1)S(1)} %collective-permute-done.5.refs_2_.refs_3_.refs_4_, ...), custom_call_target="tpu_custom_call" | custom-call | flops 4600000000 | tf_op jit(solution)/shard_map/attend/pallas_call | solution.py:380
  20.0 1.4 %collective-permute-start.8 = (bf16[64,2048]{1,0:T(8,128)(2,1)S(1)}, bf16[64,2048]{1,0:T(8,128)(2,1)S(1)}, u32[]{:S(2)}, u32[]{:S(2)}) collective-permute-start(bf16[64,2048]{1,0:T(8,128)(2,1)S(1)} %get-tuple-element.31), channel_id=1, source_target_pairs={{0,1},{1,2},{2,3},{3,0},{4,5},{5,6},{6,7},{7,4},{8,9},{9,10},{10,1... | collective-permute-start | bytes 786440 | tf_op jit(solution)/shard_map/ppermute | solution.py:401
  21.4 3.9 %attend.4 = (bf16[64,2048]{1,0:T(8,128)(2,1)S(1)}, bf16[64,2048]{1,0:T(8,128)(2,1)S(1)}, f32[256,128]{1,0:T(8,128)S(1)}) custom-call(s32[256,128]{1,0:T(8,128)S(1)} %get-tuple-element.18.refs_0_.refs_1_, f32[256,128]{1,0:T(8,128)S(1)} %get-tuple-element.25.refs_1_, bf16[3,256,512]{2,1,0:T(8,128)(2,1)S(1)} %get-tuple-element.21.refs_1_.refs_2_.refs_3_, ...), custom_call_target="tpu_custom_call" | custom-call | flops 9200000000 | tf_op jit(solution)/shard_map/attend/pallas_call | solution.py:380
  25.3 1.1 %collective-permute-start.6 = (bf16[64,2048]{1,0:T(8,128)(2,1)S(1)}, bf16[64,2048]{1,0:T(8,128)(2,1)S(1)}, u32[]{:S(2)}, u32[]{:S(2)}) collective-permute-start(bf16[64,2048]{1,0:T(8,128)(2,1)S(1)} %get-tuple-element.28), channel_id=1, source_target_pairs={{0,2},{1,3},{2,0},{3,1},{4,6},{5,7},{6,4},{7,5},{8,10},{9,11},{10,... | collective-permute-start | bytes 786440 | tf_op jit(solution)/shard_map/ppermute | solution.py:401
  26.4 1.4 %collective-permute-start.7 = (bf16[64,2048]{1,0:T(8,128)(2,1)S(1)}, bf16[64,2048]{1,0:T(8,128)(2,1)S(1)}, u32[]{:S(2)}, u32[]{:S(2)}) collective-permute-start(bf16[64,2048]{1,0:T(8,128)(2,1)S(1)} %get-tuple-element.29), channel_id=1, source_target_pairs={{0,3},{1,0},{2,1},{3,2},{4,7},{5,4},{6,5},{7,6},{8,11},{9,8},{10,9... | collective-permute-start | bytes 786440 | tf_op jit(solution)/shard_map/ppermute | solution.py:401
  27.8 2.7 %attend.5 = (bf16[64,2048]{1,0:T(8,128)(2,1)S(1)}, f32[256,128]{1,0:T(8,128)}) custom-call(s32[8,8]{1,0:T(8,128)} %refs_0_.1, s32[256,128]{1,0:T(8,128)S(1)} %get-tuple-element.18.refs_0_.refs_1_, f32[256,128]{1,0:T(8,128)S(1)} %get-tuple-element.26.refs_2_, bf16[3,256,512]{2,1,0:T(8,128)(2,1)S(1)} %get-tuple-element.21.refs_1_.refs_2_.refs_3_, ...), custom_call_target="tpu_custom_call" | custom-call | flops 4600000000 | tf_op jit(solution)/shard_map/attend/pallas_call | solution.py:380
  30.6 4.2 %all-to-all-start = ((f32[8,32,128]{2,1,0:T(8,128)}), f32[8,32,128]{2,1,0:T(8,128)S(1)}, u32[]{:S(2)}, u32[]{:S(2)}) async-start(f32[8,32,128]{2,1,0:T(8,128)} %bitcast), calls=%async_computation | async-start | bytes 262144 | tf_op jit(solution)/shard_map/all_to_all | solution.py:412
  34.7 0.0 collective-permute-done.8.refs_1_
  34.7 0.8 %begin.1.refs_2_ = bf16[64,8192]{1,0:T(8,128)(2,1)} custom-call(bf16[64,2048]{1,0:T(8,128)(2,1)S(1)} %get-tuple-element.30.refs_0_, bf16[64,2048]{1,0:T(8,128)(2,1)S(1)} %collective-permute-done.8.refs_1_), custom_call_target="tpu_custom_call" | custom-call | tf_op jit(solution)/shard_map/begin/pallas_call | solution.py:420
  35.5 2.7 %all-to-all-done = f32[8,32,128]{2,1,0:T(8,128)S(1)} async-done(((f32[8,32,128]{2,1,0:T(8,128)}), f32[8,32,128]{2,1,0:T(8,128)S(1)}, u32[]{:S(2)}, u32[]{:S(2)}) %all-to-all-start) | async-done | bytes 131104 | tf_op jit(solution)/shard_map/all_to_all | solution.py:412
  38.3 5.6 %collective-permute-done.6.refs_0_ = bf16[64,2048]{1,0:T(8,128)(2,1)S(1)} collective-permute-done((bf16[64,2048]{1,0:T(8,128)(2,1)S(1)}, bf16[64,2048]{1,0:T(8,128)(2,1)S(1)}, u32[]{:S(2)}, u32[]{:S(2)}) %collective-permute-start.6) | collective-permute-done | bytes 262176 | tf_op jit(solution)/shard_map/ppermute | solution.py:401
  43.8 2.2 %collective-permute-done.7.refs_1_ = bf16[64,2048]{1,0:T(8,128)(2,1)S(1)} collective-permute-done((bf16[64,2048]{1,0:T(8,128)(2,1)S(1)}, bf16[64,2048]{1,0:T(8,128)(2,1)S(1)}, u32[]{:S(2)}, u32[]{:S(2)}) %collective-permute-start.7) | collective-permute-done | bytes 262176 | tf_op jit(solution)/shard_map/ppermute | solution.py:401
  46.1 0.8 %assemble.1 = (bf16[64,8192]{1,0:T(8,128)(2,1)}, f32[16,256]{1,0:T(8,128)}) custom-call(f32[256,128]{1,0:T(8,128)S(1)} %bitcast.2, bf16[64,2048]{1,0:T(8,128)(2,1)S(1)} %collective-permute-done.6.refs_0_, bf16[64,2048]{1,0:T(8,128)(2,1)S(1)} %collective-permute-done.7.refs_1_, bf16[64,8192]{1,0:T(8,128)(2,1)} %begin.1.refs_2_), custom_call_target="tpu_custom_call", output_to_operand_aliasing={{0}: (3, {})} | custom-call | tf_op jit(solution)/shard_map/assemble/pallas_call | solution.py:429
Async XLA Ops:
  0.6 7.7 %collective-permute-start = (bf16[256,256]{1,0:T(8,128)(2,1)}, bf16[256,256]{1,0:T(8,128)(2,1)S(1)}, u32[]{:S(2)}, u32[]{:S(2)}) collective-permute-start(bf16[256,256]{1,0:T(8,128)(2,1)} %key_hbm.1), channel_id=1, source_target_pairs={{0,16},{4,20},{8,24},{12,28},{1,17},{5,21},{9,25},{13,29},{2,18},{... | collective-permute-start | bytes 393224 | tf_op jit(solution)/shard_map/ppermute | solution.py:318
  1.9 11.1 %collective-permute-start.1 = (bf16[256,256]{1,0:T(8,128)(2,1)}, bf16[256,256]{1,0:T(8,128)(2,1)S(1)}, u32[]{:S(2)}, u32[]{:S(2)}) collective-permute-start(bf16[256,256]{1,0:T(8,128)(2,1)} %key_hbm.1), channel_id=1, source_target_pairs={{0,8},{4,12},{16,24},{20,28},{1,9},{5,13},{17,25},{21,29},{2,10},{... | collective-permute-start | bytes 393224 | tf_op jit(solution)/shard_map/ppermute | solution.py:325
  5.1 7.9 %collective-permute-start.3 = (bf16[256,256]{1,0:T(8,128)(2,1)}, bf16[256,256]{1,0:T(8,128)(2,1)S(1)}, u32[]{:S(2)}, u32[]{:S(2)}) collective-permute-start(bf16[256,256]{1,0:T(8,128)(2,1)} %value_hbm.1), channel_id=1, source_target_pairs={{0,16},{4,20},{8,24},{12,28},{1,17},{5,21},{9,25},{13,29},{2,18},{... | collective-permute-start | bytes 393224 | tf_op jit(solution)/shard_map/ppermute | solution.py:318
  6.4 6.9 %collective-permute-start.2 = (bf16[256,256]{1,0:T(8,128)(2,1)}, bf16[256,256]{1,0:T(8,128)(2,1)S(1)}, u32[]{:S(2)}, u32[]{:S(2)}) collective-permute-start(bf16[256,256]{1,0:T(8,128)(2,1)} %value_hbm.1), channel_id=1, source_target_pairs={{0,8},{4,12},{8,16},{12,20},{16,24},{20,28},{1,9},{5,13},{9,17},{1... | collective-permute-start | bytes 393224 | tf_op jit(solution)/shard_map/ppermute | solution.py:318
  8.3 6.0 %collective-permute-start.4 = (bf16[256,256]{1,0:T(8,128)(2,1)S(1)}, bf16[256,256]{1,0:T(8,128)(2,1)S(1)}, u32[]{:S(2)}, u32[]{:S(2)}) collective-permute-start(bf16[256,256]{1,0:T(8,128)(2,1)S(1)} %collective-permute-done.refs_1_), channel_id=1, source_target_pairs={{24,16},{28,20},{25,17},{29,21},{26,18},{30,22},{27,19},{31,23}} | collective-permute-start | bytes 393224 | tf_op jit(solution)/shard_map/ppermute | solution.py:326
  14.6 3.4 %collective-permute-start.5 = (bf16[2,256,512]{2,1,0:T(8,128)(2,1)S(1)}, bf16[2,256,512]{2,1,0:T(8,128)(2,1)S(1)}, u32[]{:S(2)}, u32[]{:S(2)}) collective-permute-start(bf16[2,256,512]{2,1,0:T(8,128)(2,1)S(1)} %get-tuple-element.22), channel_id=1, source_target_pairs={{0,4},{4,0},{8,12},{12,8},{16,20},{20,16},{24,28},{28,24},{1,5},{5... | collective-permute-start | bytes 1572872 | tf_op jit(solution)/shard_map/ppermute | solution.py:371
  20.0 14.7 %collective-permute-start.8 = (bf16[64,2048]{1,0:T(8,128)(2,1)S(1)}, bf16[64,2048]{1,0:T(8,128)(2,1)S(1)}, u32[]{:S(2)}, u32[]{:S(2)}) collective-permute-start(bf16[64,2048]{1,0:T(8,128)(2,1)S(1)} %get-tuple-element.31), channel_id=1, source_target_pairs={{0,1},{1,2},{2,3},{3,0},{4,5},{5,6},{6,7},{7,4},{8,9},{9,10},{10,1... | collective-permute-start | bytes 786440 | tf_op jit(solution)/shard_map/ppermute | solution.py:401
  25.3 18.5 %collective-permute-start.6 = (bf16[64,2048]{1,0:T(8,128)(2,1)S(1)}, bf16[64,2048]{1,0:T(8,128)(2,1)S(1)}, u32[]{:S(2)}, u32[]{:S(2)}) collective-permute-start(bf16[64,2048]{1,0:T(8,128)(2,1)S(1)} %get-tuple-element.28), channel_id=1, source_target_pairs={{0,2},{1,3},{2,0},{3,1},{4,6},{5,7},{6,4},{7,5},{8,10},{9,11},{10,... | collective-permute-start | bytes 786440 | tf_op jit(solution)/shard_map/ppermute | solution.py:401
  26.4 19.7 %collective-permute-start.7 = (bf16[64,2048]{1,0:T(8,128)(2,1)S(1)}, bf16[64,2048]{1,0:T(8,128)(2,1)S(1)}, u32[]{:S(2)}, u32[]{:S(2)}) collective-permute-start(bf16[64,2048]{1,0:T(8,128)(2,1)S(1)} %get-tuple-element.29), channel_id=1, source_target_pairs={{0,3},{1,0},{2,1},{3,2},{4,7},{5,4},{6,5},{7,6},{8,11},{9,8},{10,9... | collective-permute-start | bytes 786440 | tf_op jit(solution)/shard_map/ppermute | solution.py:401
  30.6 7.7 %all-to-all-start = ((f32[8,32,128]{2,1,0:T(8,128)}), f32[8,32,128]{2,1,0:T(8,128)S(1)}, u32[]{:S(2)}, u32[]{:S(2)}) async-start(f32[8,32,128]{2,1,0:T(8,128)} %bitcast), calls=%async_computation | async-start | bytes 262144 | tf_op jit(solution)/shard_map/all_to_all | solution.py:412

commit v6 on v5

--- a/solution.py
+++ b/solution.py
@@ -402,7 +402,10 @@
 
     norm, pieces_of = None, {}
     both = list(range(groups))
-    for span in (range(1, 2), range(2, planes)):
+    middle = planes // 2
+    spans = [range(middle, middle + 1), range(1, planes, 2)]
+    spans += [range(s, s + 1) for s in range(2, planes, 2) if s != middle]
+    for span in spans:
         result, norm = attend(norm, both, span, False, 4.0 * len(span))
         for s, piece in zip(span, result):
             pieces_of[s, 0] = send(piece, s)
@@ -414,8 +417,8 @@
     ).reshape(rows, HEAD_DIM)
     width = per_group * HEAD_DIM
     out_shape = jax.ShapeDtypeStruct((tile, planes * heads * HEAD_DIM), jnp.bfloat16)
-    soon = [place for place in sorted(pieces_of) if place[0] < 2]
-    late = [place for place in sorted(pieces_of) if place[0] >= 2]
+    soon = [place for place in sorted(pieces_of) if place[0] in (0, planes // 2)]
+    late = [place for place in sorted(pieces_of) if place not in soon]
     with jax.named_scope("begin"):
         begun = pl.pallas_call(
             partial(begin_kernel, planes, width, groups, soon),

time: 47.2 us -> 47.4 us (level)
  the two profiles are of different devices: /device:TPU:13 before, /device:TPU:0 now
where the time goes in v6:
time: 47.4 us; the launch traced here: 47.1 us
  starting transfers between devices  22 us (46%)
  Pallas kernels  13.9 us (29%)
  waiting for transfers between devices  10.5 us (22%)
  between operations  0.74 us (2%)
    pallas_call x3, Pallas kernels, attend(): pl.pallas_call(partial(attend_kernel, pieces, per_group, used, tiles_of,...  8.62 us
    ppermute x3, waiting for transfers between devices, send(): lax.ppermute(piece, 'kv', [(i, (i + s) % planes) for i in range(planes)])  8 us
    ppermute x3, starting transfers between devices, forward(): lax.ppermute(x, 'tok', [(i, i + 2 * p) for i in range(shards - 2 * p)])  7.47 us
    ppermute x3, starting transfers between devices, send(): lax.ppermute(piece, 'kv', [(i, (i + s) % planes) for i in range(planes)])  6.53 us
    all_to_all x1, starting transfers between devices, body(): lax.all_to_all(norm.reshape(shards, block_rows, HEAD_DIM), 'tok', split_a...  3.83 us
    ppermute x1, starting transfers between devices, body(): lax.ppermute(key_states, 'tok', [(0, 2), (1, 3), (4, 6), (5, 7)])  3.4 us
    pallas_call x1, Pallas kernels, body(): pl.pallas_call(partial(queries_kernel, pieces), out_shape=[pack_shape, ja...  3.38 us
    ppermute x1, waiting for transfers between devices, body(): theirs = lax.ppermute(give, 'tok', pair)  1.9 us
  transfers between devices with their start and end apart: 10, of which 5 were waited for; matrix products, arithmetic and copies ran while one was open for 0% of the time, Pallas kernels for 23%

profile of v6, /device:TPU:0, one launch (start us, length us, event | category | flops | bytes accessed | tf_op | source)
XLA Modules:
  0.0 47.1 jit_solution(1963154739810109455)
XLA Ops:
  0.6 4.9 %collective-permute-start = (bf16[256,256]{1,0:T(8,128)(2,1)}, bf16[256,256]{1,0:T(8,128)(2,1)S(1)}, u32[]{:S(2)}, u32[]{:S(2)}) collective-permute-start(bf16[256,256]{1,0:T(8,128)(2,1)} %key_hbm.1), channel_id=1, source_target_pairs={{0,16},{4,20},{8,24},{12,28},{1,17},{5,21},{9,25},{13,29},{2,18},{... | collective-permute-start | bytes 393224 | tf_op jit(solution)/shard_map/ppermute | solution.py:318
  5.5 3.4 %collective-permute-start.1 = (bf16[256,256]{1,0:T(8,128)(2,1)}, bf16[256,256]{1,0:T(8,128)(2,1)S(1)}, u32[]{:S(2)}, u32[]{:S(2)}) collective-permute-start(bf16[256,256]{1,0:T(8,128)(2,1)} %key_hbm.1), channel_id=1, source_target_pairs={{0,8},{4,12},{16,24},{20,28},{1,9},{5,13},{17,25},{21,29},{2,10},{... | collective-permute-start | bytes 393224 | tf_op jit(solution)/shard_map/ppermute | solution.py:325
  8.9 1.3 %collective-permute-start.3 = (bf16[256,256]{1,0:T(8,128)(2,1)}, bf16[256,256]{1,0:T(8,128)(2,1)S(1)}, u32[]{:S(2)}, u32[]{:S(2)}) collective-permute-start(bf16[256,256]{1,0:T(8,128)(2,1)} %value_hbm.1), channel_id=1, source_target_pairs={{0,16},{4,20},{8,24},{12,28},{1,17},{5,21},{9,25},{13,29},{2,18},{... | collective-permute-start | bytes 393224 | tf_op jit(solution)/shard_map/ppermute | solution.py:318
  10.2 1.3 %collective-permute-start.2 = (bf16[256,256]{1,0:T(8,128)(2,1)}, bf16[256,256]{1,0:T(8,128)(2,1)S(1)}, u32[]{:S(2)}, u32[]{:S(2)}) collective-permute-start(bf16[256,256]{1,0:T(8,128)(2,1)} %value_hbm.1), channel_id=1, source_target_pairs={{0,8},{4,12},{8,16},{12,20},{16,24},{20,28},{1,9},{5,13},{9,17},{1... | collective-permute-start | bytes 393224 | tf_op jit(solution)/shard_map/ppermute | solution.py:318
  11.5 0.0 collective-permute-done.refs_1_
  11.5 0.7 %collective-permute-start.4 = (bf16[256,256]{1,0:T(8,128)(2,1)S(1)}, bf16[256,256]{1,0:T(8,128)(2,1)S(1)}, u32[]{:S(2)}, u32[]{:S(2)}) collective-permute-start(bf16[256,256]{1,0:T(8,128)(2,1)S(1)} %collective-permute-done.refs_1_), channel_id=1, source_target_pairs={{24,16},{28,20},{25,17},{29,21},{26,18},{30,22},{27,19},{31,23}} | collective-permute-start | bytes 393224 | tf_op jit(solution)/shard_map/ppermute | solution.py:326
  12.2 3.4 %rotate.1 = (bf16[256,512]{1,0:T(8,128)(2,1)S(1)}, s32[256,128]{1,0:T(8,128)S(1)}, f32[4,256,128]{2,1,0:T(8,128)S(1)}, bf16[4,512,128]{2,1,0:T(8,128)(2,1)S(1)}, bf16[4,512,128]{2,1,0:T(8,128)(2,1)S(1)}) custom-call(s32[16]{0:T(128)} %lengths_hbm.1, f32[1,128]{1,0:T(1,128)} %constant.2.clone.freq_hbm, bf16[256,256]{1,0:T(8,128)(2,1)} %key_hbm.1, ...), custom_call_target="tpu_custom_call" | custom-call | flops 3449999872 | tf_op jit(solution)/shard_map/rotate/pallas_call | solution.py:330
  15.6 0.0 collective-permute-done.1.refs_0_
  15.6 0.2 collective-permute-done.3.refs_3_
  15.8 0.0 collective-permute-done.2.refs_2_
  15.9 0.0 collective-permute-done.4.refs_4_
  15.9 0.3 pack.1
  16.2 0.1 collective-permute-start.5
  16.2 1.9 %collective-permute-done.5.refs_2_.refs_3_.refs_4_ = bf16[2,256,512]{2,1,0:T(8,128)(2,1)S(1)} collective-permute-done((bf16[2,256,512]{2,1,0:T(8,128)(2,1)S(1)}, bf16[2,256,512]{2,1,0:T(8,128)(2,1)S(1)}, u32[]{:S(2)}, u32[]{:S(2)}) %collective-permute-start.5) | collective-permute-done | bytes 524320 | tf_op jit(solution)/shard_map/ppermute | solution.py:371
  18.1 2.0 %attend.3 = (bf16[64,2048]{1,0:T(8,128)(2,1)S(1)}, f32[256,128]{1,0:T(8,128)S(1)}) custom-call(s32[256,128]{1,0:T(8,128)S(1)} %get-tuple-element.18.refs_0_.refs_1_, bf16[3,256,512]{2,1,0:T(8,128)(2,1)S(1)} %get-tuple-element.21.refs_1_.refs_2_.refs_3_, bf16[2,256,512]{2,1,0:T(8,128)(2,1)S(1)} %collective-permute-done.5.refs_2_.refs_3_.refs_4_, ...), custom_call_target="tpu_custom_call" | custom-call | flops 4600000000 | tf_op jit(solution)/shard_map/attend/pallas_call | solution.py:380
  20.1 2.7 %collective-permute-start.8 = (bf16[64,2048]{1,0:T(8,128)(2,1)S(1)}, bf16[64,2048]{1,0:T(8,128)(2,1)S(1)}, u32[]{:S(2)}, u32[]{:S(2)}) collective-permute-start(bf16[64,2048]{1,0:T(8,128)(2,1)S(1)} %get-tuple-element.31), channel_id=1, source_target_pairs={{0,2},{1,3},{2,0},{3,1},{4,6},{5,7},{6,4},{7,5},{8,10},{9,11},{10,... | collective-permute-start | bytes 786440 | tf_op jit(solution)/shard_map/ppermute | solution.py:401
  22.8 3.9 %attend.4 = (bf16[64,2048]{1,0:T(8,128)(2,1)S(1)}, bf16[64,2048]{1,0:T(8,128)(2,1)S(1)}, f32[256,128]{1,0:T(8,128)S(1)}) custom-call(s32[256,128]{1,0:T(8,128)S(1)} %get-tuple-element.18.refs_0_.refs_1_, f32[256,128]{1,0:T(8,128)S(1)} %get-tuple-element.25.refs_1_, bf16[3,256,512]{2,1,0:T(8,128)(2,1)S(1)} %get-tuple-element.21.refs_1_.refs_2_.refs_3_, ...), custom_call_target="tpu_custom_call" | custom-call | flops 9200000000 | tf_op jit(solution)/shard_map/attend/pallas_call | solution.py:380
  26.7 1.6 %collective-permute-start.6 = (bf16[64,2048]{1,0:T(8,128)(2,1)S(1)}, bf16[64,2048]{1,0:T(8,128)(2,1)S(1)}, u32[]{:S(2)}, u32[]{:S(2)}) collective-permute-start(bf16[64,2048]{1,0:T(8,128)(2,1)S(1)} %get-tuple-element.28), channel_id=1, source_target_pairs={{0,1},{1,2},{2,3},{3,0},{4,5},{5,6},{6,7},{7,4},{8,9},{9,10},{10,1... | collective-permute-start | bytes 786440 | tf_op jit(solution)/shard_map/ppermute | solution.py:401
  28.4 2.2 %collective-permute-start.7 = (bf16[64,2048]{1,0:T(8,128)(2,1)S(1)}, bf16[64,2048]{1,0:T(8,128)(2,1)S(1)}, u32[]{:S(2)}, u32[]{:S(2)}) collective-permute-start(bf16[64,2048]{1,0:T(8,128)(2,1)S(1)} %get-tuple-element.29), channel_id=1, source_target_pairs={{0,3},{1,0},{2,1},{3,2},{4,7},{5,4},{6,5},{7,6},{8,11},{9,8},{10,9... | collective-permute-start | bytes 786440 | tf_op jit(solution)/shard_map/ppermute | solution.py:401
  30.6 2.7 %attend.5 = (bf16[64,2048]{1,0:T(8,128)(2,1)S(1)}, f32[256,128]{1,0:T(8,128)}) custom-call(s32[8,8]{1,0:T(8,128)} %refs_0_.1, s32[256,128]{1,0:T(8,128)S(1)} %get-tuple-element.18.refs_0_.refs_1_, f32[256,128]{1,0:T(8,128)S(1)} %get-tuple-element.26.refs_2_, bf16[3,256,512]{2,1,0:T(8,128)(2,1)S(1)} %get-tuple-element.21.refs_1_.refs_2_.refs_3_, ...), custom_call_target="tpu_custom_call" | custom-call | flops 4600000000 | tf_op jit(solution)/shard_map/attend/pallas_call | solution.py:380
  33.3 3.8 %all-to-all-start = ((f32[8,32,128]{2,1,0:T(8,128)}), f32[8,32,128]{2,1,0:T(8,128)S(1)}, u32[]{:S(2)}, u32[]{:S(2)}) async-start(f32[8,32,128]{2,1,0:T(8,128)} %bitcast), calls=%async_computation | async-start | bytes 262144 | tf_op jit(solution)/shard_map/all_to_all | solution.py:415
  37.1 4.4 %collective-permute-done.8.refs_1_ = bf16[64,2048]{1,0:T(8,128)(2,1)S(1)} collective-permute-done((bf16[64,2048]{1,0:T(8,128)(2,1)S(1)}, bf16[64,2048]{1,0:T(8,128)(2,1)S(1)}, u32[]{:S(2)}, u32[]{:S(2)}) %collective-permute-start.8) | collective-permute-done | bytes 262176 | tf_op jit(solution)/shard_map/ppermute | solution.py:401
  41.5 0.8 %begin.1.refs_2_ = bf16[64,8192]{1,0:T(8,128)(2,1)} custom-call(bf16[64,2048]{1,0:T(8,128)(2,1)S(1)} %get-tuple-element.30.refs_0_, bf16[64,2048]{1,0:T(8,128)(2,1)S(1)} %collective-permute-done.8.refs_1_), custom_call_target="tpu_custom_call" | custom-call | tf_op jit(solution)/shard_map/begin/pallas_call | solution.py:423
  42.4 0.3 all-to-all-done
  42.7 0.0 collective-permute-done.6.refs_0_
  42.7 3.6 %collective-permute-done.7.refs_1_ = bf16[64,2048]{1,0:T(8,128)(2,1)S(1)} collective-permute-done((bf16[64,2048]{1,0:T(8,128)(2,1)S(1)}, bf16[64,2048]{1,0:T(8,128)(2,1)S(1)}, u32[]{:S(2)}, u32[]{:S(2)}) %collective-permute-start.7) | collective-permute-done | bytes 262176 | tf_op jit(solution)/shard_map/ppermute | solution.py:401
  46.3 0.8 %assemble.1 = (bf16[64,8192]{1,0:T(8,128)(2,1)}, f32[16,256]{1,0:T(8,128)}) custom-call(f32[256,128]{1,0:T(8,128)S(1)} %bitcast.2, bf16[64,2048]{1,0:T(8,128)(2,1)S(1)} %collective-permute-done.6.refs_0_, bf16[64,2048]{1,0:T(8,128)(2,1)S(1)} %collective-permute-done.7.refs_1_, bf16[64,8192]{1,0:T(8,128)(2,1)} %begin.1.refs_2_), custom_call_target="tpu_custom_call", output_to_operand_aliasing={{0}: (3, {})} | custom-call | tf_op jit(solution)/shard_map/assemble/pallas_call | solution.py:432
Async XLA Ops:
  0.6 10.9 %collective-permute-start = (bf16[256,256]{1,0:T(8,128)(2,1)}, bf16[256,256]{1,0:T(8,128)(2,1)S(1)}, u32[]{:S(2)}, u32[]{:S(2)}) collective-permute-start(bf16[256,256]{1,0:T(8,128)(2,1)} %key_hbm.1), channel_id=1, source_target_pairs={{0,16},{4,20},{8,24},{12,28},{1,17},{5,21},{9,25},{13,29},{2,18},{... | collective-permute-start | bytes 393224 | tf_op jit(solution)/shard_map/ppermute | solution.py:318
  5.5 10.1 %collective-permute-start.1 = (bf16[256,256]{1,0:T(8,128)(2,1)}, bf16[256,256]{1,0:T(8,128)(2,1)S(1)}, u32[]{:S(2)}, u32[]{:S(2)}) collective-permute-start(bf16[256,256]{1,0:T(8,128)(2,1)} %key_hbm.1), channel_id=1, source_target_pairs={{0,8},{4,12},{16,24},{20,28},{1,9},{5,13},{17,25},{21,29},{2,10},{... | collective-permute-start | bytes 393224 | tf_op jit(solution)/shard_map/ppermute | solution.py:325
  8.9 6.9 %collective-permute-start.3 = (bf16[256,256]{1,0:T(8,128)(2,1)}, bf16[256,256]{1,0:T(8,128)(2,1)S(1)}, u32[]{:S(2)}, u32[]{:S(2)}) collective-permute-start(bf16[256,256]{1,0:T(8,128)(2,1)} %value_hbm.1), channel_id=1, source_target_pairs={{0,16},{4,20},{8,24},{12,28},{1,17},{5,21},{9,25},{13,29},{2,18},{... | collective-permute-start | bytes 393224 | tf_op jit(solution)/shard_map/ppermute | solution.py:318
  10.2 5.6 %collective-permute-start.2 = (bf16[256,256]{1,0:T(8,128)(2,1)}, bf16[256,256]{1,0:T(8,128)(2,1)S(1)}, u32[]{:S(2)}, u32[]{:S(2)}) collective-permute-start(bf16[256,256]{1,0:T(8,128)(2,1)} %value_hbm.1), channel_id=1, source_target_pairs={{0,8},{4,12},{8,16},{12,20},{16,24},{20,28},{1,9},{5,13},{9,17},{1... | collective-permute-start | bytes 393224 | tf_op jit(solution)/shard_map/ppermute | solution.py:318
  11.5 4.3 %collective-permute-start.4 = (bf16[256,256]{1,0:T(8,128)(2,1)S(1)}, bf16[256,256]{1,0:T(8,128)(2,1)S(1)}, u32[]{:S(2)}, u32[]{:S(2)}) collective-permute-start(bf16[256,256]{1,0:T(8,128)(2,1)S(1)} %collective-permute-done.refs_1_), channel_id=1, source_target_pairs={{24,16},{28,20},{25,17},{29,21},{26,18},{30,22},{27,19},{31,23}} | collective-permute-start | bytes 393224 | tf_op jit(solution)/shard_map/ppermute | solution.py:326
  16.2 2.0 %collective-permute-start.5 = (bf16[2,256,512]{2,1,0:T(8,128)(2,1)S(1)}, bf16[2,256,512]{2,1,0:T(8,128)(2,1)S(1)}, u32[]{:S(2)}, u32[]{:S(2)}) collective-permute-start(bf16[2,256,512]{2,1,0:T(8,128)(2,1)S(1)} %get-tuple-element.22), channel_id=1, source_target_pairs={{0,4},{4,0},{8,12},{12,8},{16,20},{20,16},{24,28},{28,24},{1,5},{5... | collective-permute-start | bytes 1572872 | tf_op jit(solution)/shard_map/ppermute | solution.py:371
  20.1 21.4 %collective-permute-start.8 = (bf16[64,2048]{1,0:T(8,128)(2,1)S(1)}, bf16[64,2048]{1,0:T(8,128)(2,1)S(1)}, u32[]{:S(2)}, u32[]{:S(2)}) collective-permute-start(bf16[64,2048]{1,0:T(8,128)(2,1)S(1)} %get-tuple-element.31), channel_id=1, source_target_pairs={{0,2},{1,3},{2,0},{3,1},{4,6},{5,7},{6,4},{7,5},{8,10},{9,11},{10,... | collective-permute-start | bytes 786440 | tf_op jit(solution)/shard_map/ppermute | solution.py:401
  26.7 15.9 %collective-permute-start.6 = (bf16[64,2048]{1,0:T(8,128)(2,1)S(1)}, bf16[64,2048]{1,0:T(8,128)(2,1)S(1)}, u32[]{:S(2)}, u32[]{:S(2)}) collective-permute-start(bf16[64,2048]{1,0:T(8,128)(2,1)S(1)} %get-tuple-element.28), channel_id=1, source_target_pairs={{0,1},{1,2},{2,3},{3,0},{4,5},{5,6},{6,7},{7,4},{8,9},{9,10},{10,1... | collective-permute-start | bytes 786440 | tf_op jit(solution)/shard_map/ppermute | solution.py:401
  28.4 17.9 %collective-permute-start.7 = (bf16[64,2048]{1,0:T(8,128)(2,1)S(1)}, bf16[64,2048]{1,0:T(8,128)(2,1)S(1)}, u32[]{:S(2)}, u32[]{:S(2)}) collective-permute-start(bf16[64,2048]{1,0:T(8,128)(2,1)S(1)} %get-tuple-element.29), channel_id=1, source_target_pairs={{0,3},{1,0},{2,1},{3,2},{4,7},{5,4},{6,5},{7,6},{8,11},{9,8},{10,9... | collective-permute-start | bytes 786440 | tf_op jit(solution)/shard_map/ppermute | solution.py:401
  33.3 9.4 %all-to-all-start = ((f32[8,32,128]{2,1,0:T(8,128)}), f32[8,32,128]{2,1,0:T(8,128)S(1)}, u32[]{:S(2)}, u32[]{:S(2)}) async-start(f32[8,32,128]{2,1,0:T(8,128)} %bitcast), calls=%async_computation | async-start | bytes 262144 | tf_op jit(solution)/shard_map/all_to_all | solution.py:415

commit v7 on v5

--- a/solution.py
+++ b/solution.py
@@ -219,7 +219,7 @@
             )
             mixed = product if mixed is None else mixed + product
         row_sum = mixed[:, HEAD_DIM:]
-        result = (mixed[:, :HEAD_DIM] / row_sum).astype(jnp.bfloat16)
+        result = (mixed[:, :HEAD_DIM] * pl.reciprocal(row_sum)).astype(jnp.bfloat16)
         norm = top * (1.0 / LOG2E) + jnp.log(row_sum)
         for h in range(inside):
             head = c * inside + h

time: 47.2 us -> 47.2 us (level)
  no operation moved by 1% of the time
where the time goes in v7:
time: 47.2 us; the launch traced here: 46.9 us
  starting transfers between devices  18.9 us (40%)
  Pallas kernels  13.9 us (29%)
  waiting for transfers between devices  13.4 us (28%)
  between operations  0.73 us (2%)
    pallas_call x3, Pallas kernels, attend(): pl.pallas_call(partial(attend_kernel, pieces, per_group, used, tiles_of,...  8.62 us
    ppermute x3, waiting for transfers between devices, send(): lax.ppermute(piece, 'kv', [(i, (i + s) % planes) for i in range(planes)])  7.79 us
    ppermute x3, starting transfers between devices, forward(): lax.ppermute(x, 'tok', [(i, i + 2 * p) for i in range(shards - 2 * p)])  4.5 us
    all_to_all x1, starting transfers between devices, body(): lax.all_to_all(norm.reshape(shards, block_rows, HEAD_DIM), 'tok', split_a...  4.16 us
    ppermute x3, starting transfers between devices, send(): lax.ppermute(piece, 'kv', [(i, (i + s) % planes) for i in range(planes)])  3.9 us
    pallas_call x1, Pallas kernels, body(): pl.pallas_call(partial(queries_kernel, pieces), out_shape=[pack_shape, ja...  3.38 us
    ppermute x1, starting transfers between devices, body(): lax.ppermute(key_states, 'tok', [(0, 2), (1, 3), (4, 6), (5, 7)])  3.12 us
    all_to_all x1, waiting for transfers between devices, body(): lax.all_to_all(norm.reshape(shards, block_rows, HEAD_DIM), 'tok', split_a...  2.74 us
  transfers between devices with their start and end apart: 10, of which 6 were waited for; matrix products, arithmetic and copies ran while one was open for 0% of the time, Pallas kernels for 23%

profile of v7, /device:TPU:13, one launch (start us, length us, event | category | flops | bytes accessed | tf_op | source)
XLA Modules:
  0.0 46.9 jit_solution(5541582724064259703)
XLA Ops:
  0.6 1.3 %collective-permute-start = (bf16[256,256]{1,0:T(8,128)(2,1)}, bf16[256,256]{1,0:T(8,128)(2,1)S(1)}, u32[]{:S(2)}, u32[]{:S(2)}) collective-permute-start(bf16[256,256]{1,0:T(8,128)(2,1)} %key_hbm.1), channel_id=1, source_target_pairs={{0,16},{4,20},{8,24},{12,28},{1,17},{5,21},{9,25},{13,29},{2,18},{... | collective-permute-start | bytes 393224 | tf_op jit(solution)/shard_map/ppermute | solution.py:318
  1.9 3.1 %collective-permute-start.1 = (bf16[256,256]{1,0:T(8,128)(2,1)}, bf16[256,256]{1,0:T(8,128)(2,1)S(1)}, u32[]{:S(2)}, u32[]{:S(2)}) collective-permute-start(bf16[256,256]{1,0:T(8,128)(2,1)} %key_hbm.1), channel_id=1, source_target_pairs={{0,8},{4,12},{16,24},{20,28},{1,9},{5,13},{17,25},{21,29},{2,10},{... | collective-permute-start | bytes 393224 | tf_op jit(solution)/shard_map/ppermute | solution.py:325
  5.1 1.3 %collective-permute-start.3 = (bf16[256,256]{1,0:T(8,128)(2,1)}, bf16[256,256]{1,0:T(8,128)(2,1)S(1)}, u32[]{:S(2)}, u32[]{:S(2)}) collective-permute-start(bf16[256,256]{1,0:T(8,128)(2,1)} %value_hbm.1), channel_id=1, source_target_pairs={{0,16},{4,20},{8,24},{12,28},{1,17},{5,21},{9,25},{13,29},{2,18},{... | collective-permute-start | bytes 393224 | tf_op jit(solution)/shard_map/ppermute | solution.py:318
  6.4 1.9 %collective-permute-start.2 = (bf16[256,256]{1,0:T(8,128)(2,1)}, bf16[256,256]{1,0:T(8,128)(2,1)S(1)}, u32[]{:S(2)}, u32[]{:S(2)}) collective-permute-start(bf16[256,256]{1,0:T(8,128)(2,1)} %value_hbm.1), channel_id=1, source_target_pairs={{0,8},{4,12},{8,16},{12,20},{16,24},{20,28},{1,9},{5,13},{9,17},{1... | collective-permute-start | bytes 393224 | tf_op jit(solution)/shard_map/ppermute | solution.py:318
  8.3 0.0 collective-permute-done.refs_1_
  8.3 1.3 %collective-permute-start.4 = (bf16[256,256]{1,0:T(8,128)(2,1)S(1)}, bf16[256,256]{1,0:T(8,128)(2,1)S(1)}, u32[]{:S(2)}, u32[]{:S(2)}) collective-permute-start(bf16[256,256]{1,0:T(8,128)(2,1)S(1)} %collective-permute-done.refs_1_), channel_id=1, source_target_pairs={{24,16},{28,20},{25,17},{29,21},{26,18},{30,22},{27,19},{31,23}} | collective-permute-start | bytes 393224 | tf_op jit(solution)/shard_map/ppermute | solution.py:326
  9.6 3.4 %rotate.1 = (bf16[256,512]{1,0:T(8,128)(2,1)S(1)}, s32[256,128]{1,0:T(8,128)S(1)}, f32[4,256,128]{2,1,0:T(8,128)S(1)}, bf16[4,512,128]{2,1,0:T(8,128)(2,1)S(1)}, bf16[4,512,128]{2,1,0:T(8,128)(2,1)S(1)}) custom-call(s32[16]{0:T(128)} %lengths_hbm.1, f32[1,128]{1,0:T(1,128)} %constant.2.clone.freq_hbm, bf16[256,256]{1,0:T(8,128)(2,1)} %key_hbm.1, ...), custom_call_target="tpu_custom_call" | custom-call | flops 3449999872 | tf_op jit(solution)/shard_map/rotate/pallas_call | solution.py:330
  13.0 0.0 collective-permute-done.1.refs_0_
  13.0 0.0 collective-permute-done.3.refs_3_
  13.0 0.3 collective-permute-done.2.refs_2_
  13.3 1.0 %collective-permute-done.4.refs_4_ = bf16[256,256]{1,0:T(8,128)(2,1)S(1)} collective-permute-done((bf16[256,256]{1,0:T(8,128)(2,1)S(1)}, bf16[256,256]{1,0:T(8,128)(2,1)S(1)}, u32[]{:S(2)}, u32[]{:S(2)}) %collective-permute-start.4) | collective-permute-done | bytes 131104 | tf_op jit(solution)/shard_map/ppermute | solution.py:326
  14.3 0.3 pack.1
  14.6 1.9 %collective-permute-start.5 = (bf16[2,256,512]{2,1,0:T(8,128)(2,1)S(1)}, bf16[2,256,512]{2,1,0:T(8,128)(2,1)S(1)}, u32[]{:S(2)}, u32[]{:S(2)}) collective-permute-start(bf16[2,256,512]{2,1,0:T(8,128)(2,1)S(1)} %get-tuple-element.22), channel_id=1, source_target_pairs={{0,4},{4,0},{8,12},{12,8},{16,20},{20,16},{24,28},{28,24},{1,5},{5... | collective-permute-start | bytes 1572872 | tf_op jit(solution)/shard_map/ppermute | solution.py:371
  16.5 1.5 %collective-permute-done.5.refs_2_.refs_3_.refs_4_ = bf16[2,256,512]{2,1,0:T(8,128)(2,1)S(1)} collective-permute-done((bf16[2,256,512]{2,1,0:T(8,128)(2,1)S(1)}, bf16[2,256,512]{2,1,0:T(8,128)(2,1)S(1)}, u32[]{:S(2)}, u32[]{:S(2)}) %collective-permute-start.5) | collective-permute-done | bytes 524320 | tf_op jit(solution)/shard_map/ppermute | solution.py:371
  18.0 2.0 %attend.3 = (bf16[64,2048]{1,0:T(8,128)(2,1)S(1)}, f32[256,128]{1,0:T(8,128)S(1)}) custom-call(s32[256,128]{1,0:T(8,128)S(1)} %get-tuple-element.18.refs_0_.refs_1_, bf16[3,256,512]{2,1,0:T(8,128)(2,1)S(1)} %get-tuple-element.21.refs_1_.refs_2_.refs_3_, bf16[2,256,512]{2,1,0:T(8,128)(2,1)S(1)} %collective-permute-done.5.refs_2_.refs_3_.refs_4_, ...), custom_call_target="tpu_custom_call" | custom-call | flops 4600000000 | tf_op jit(solution)/shard_map/attend/pallas_call | solution.py:380
  20.0 1.4 %collective-permute-start.8 = (bf16[64,2048]{1,0:T(8,128)(2,1)S(1)}, bf16[64,2048]{1,0:T(8,128)(2,1)S(1)}, u32[]{:S(2)}, u32[]{:S(2)}) collective-permute-start(bf16[64,2048]{1,0:T(8,128)(2,1)S(1)} %get-tuple-element.31), channel_id=1, source_target_pairs={{0,1},{1,2},{2,3},{3,0},{4,5},{5,6},{6,7},{7,4},{8,9},{9,10},{10,1... | collective-permute-start | bytes 786440 | tf_op jit(solution)/shard_map/ppermute | solution.py:401
  21.4 3.9 %attend.4 = (bf16[64,2048]{1,0:T(8,128)(2,1)S(1)}, bf16[64,2048]{1,0:T(8,128)(2,1)S(1)}, f32[256,128]{1,0:T(8,128)S(1)}) custom-call(s32[256,128]{1,0:T(8,128)S(1)} %get-tuple-element.18.refs_0_.refs_1_, f32[256,128]{1,0:T(8,128)S(1)} %get-tuple-element.25.refs_1_, bf16[3,256,512]{2,1,0:T(8,128)(2,1)S(1)} %get-tuple-element.21.refs_1_.refs_2_.refs_3_, ...), custom_call_target="tpu_custom_call" | custom-call | flops 9200000000 | tf_op jit(solution)/shard_map/attend/pallas_call | solution.py:380
  25.3 1.1 %collective-permute-start.6 = (bf16[64,2048]{1,0:T(8,128)(2,1)S(1)}, bf16[64,2048]{1,0:T(8,128)(2,1)S(1)}, u32[]{:S(2)}, u32[]{:S(2)}) collective-permute-start(bf16[64,2048]{1,0:T(8,128)(2,1)S(1)} %get-tuple-element.28), channel_id=1, source_target_pairs={{0,2},{1,3},{2,0},{3,1},{4,6},{5,7},{6,4},{7,5},{8,10},{9,11},{10,... | collective-permute-start | bytes 786440 | tf_op jit(solution)/shard_map/ppermute | solution.py:401
  26.4 1.4 %collective-permute-start.7 = (bf16[64,2048]{1,0:T(8,128)(2,1)S(1)}, bf16[64,2048]{1,0:T(8,128)(2,1)S(1)}, u32[]{:S(2)}, u32[]{:S(2)}) collective-permute-start(bf16[64,2048]{1,0:T(8,128)(2,1)S(1)} %get-tuple-element.29), channel_id=1, source_target_pairs={{0,3},{1,0},{2,1},{3,2},{4,7},{5,4},{6,5},{7,6},{8,11},{9,8},{10,9... | collective-permute-start | bytes 786440 | tf_op jit(solution)/shard_map/ppermute | solution.py:401
  27.8 2.7 %attend.5 = (bf16[64,2048]{1,0:T(8,128)(2,1)S(1)}, f32[256,128]{1,0:T(8,128)}) custom-call(s32[8,8]{1,0:T(8,128)} %refs_0_.1, s32[256,128]{1,0:T(8,128)S(1)} %get-tuple-element.18.refs_0_.refs_1_, f32[256,128]{1,0:T(8,128)S(1)} %get-tuple-element.26.refs_2_, bf16[3,256,512]{2,1,0:T(8,128)(2,1)S(1)} %get-tuple-element.21.refs_1_.refs_2_.refs_3_, ...), custom_call_target="tpu_custom_call" | custom-call | flops 4600000000 | tf_op jit(solution)/shard_map/attend/pallas_call | solution.py:380
  30.6 4.2 %all-to-all-start = ((f32[8,32,128]{2,1,0:T(8,128)}), f32[8,32,128]{2,1,0:T(8,128)S(1)}, u32[]{:S(2)}, u32[]{:S(2)}) async-start(f32[8,32,128]{2,1,0:T(8,128)} %bitcast), calls=%async_computation | async-start | bytes 262144 | tf_op jit(solution)/shard_map/all_to_all | solution.py:412
  34.7 0.0 collective-permute-done.8.refs_1_
  34.7 0.8 %begin.1.refs_2_ = bf16[64,8192]{1,0:T(8,128)(2,1)} custom-call(bf16[64,2048]{1,0:T(8,128)(2,1)S(1)} %get-tuple-element.30.refs_0_, bf16[64,2048]{1,0:T(8,128)(2,1)S(1)} %collective-permute-done.8.refs_1_), custom_call_target="tpu_custom_call" | custom-call | tf_op jit(solution)/shard_map/begin/pallas_call | solution.py:420
  35.5 2.7 %all-to-all-done = f32[8,32,128]{2,1,0:T(8,128)S(1)} async-done(((f32[8,32,128]{2,1,0:T(8,128)}), f32[8,32,128]{2,1,0:T(8,128)S(1)}, u32[]{:S(2)}, u32[]{:S(2)}) %all-to-all-start) | async-done | bytes 131104 | tf_op jit(solution)/shard_map/all_to_all | solution.py:412
  38.3 5.6 %collective-permute-done.6.refs_0_ = bf16[64,2048]{1,0:T(8,128)(2,1)S(1)} collective-permute-done((bf16[64,2048]{1,0:T(8,128)(2,1)S(1)}, bf16[64,2048]{1,0:T(8,128)(2,1)S(1)}, u32[]{:S(2)}, u32[]{:S(2)}) %collective-permute-start.6) | collective-permute-done | bytes 262176 | tf_op jit(solution)/shard_map/ppermute | solution.py:401
  43.8 2.2 %collective-permute-done.7.refs_1_ = bf16[64,2048]{1,0:T(8,128)(2,1)S(1)} collective-permute-done((bf16[64,2048]{1,0:T(8,128)(2,1)S(1)}, bf16[64,2048]{1,0:T(8,128)(2,1)S(1)}, u32[]{:S(2)}, u32[]{:S(2)}) %collective-permute-start.7) | collective-permute-done | bytes 262176 | tf_op jit(solution)/shard_map/ppermute | solution.py:401
  46.1 0.8 %assemble.1 = (bf16[64,8192]{1,0:T(8,128)(2,1)}, f32[16,256]{1,0:T(8,128)}) custom-call(f32[256,128]{1,0:T(8,128)S(1)} %bitcast.2, bf16[64,2048]{1,0:T(8,128)(2,1)S(1)} %collective-permute-done.6.refs_0_, bf16[64,2048]{1,0:T(8,128)(2,1)S(1)} %collective-permute-done.7.refs_1_, bf16[64,8192]{1,0:T(8,128)(2,1)} %begin.1.refs_2_), custom_call_target="tpu_custom_call", output_to_operand_aliasing={{0}: (3, {})} | custom-call | tf_op jit(solution)/shard_map/assemble/pallas_call | solution.py:429
Async XLA Ops:
  0.6 7.7 %collective-permute-start = (bf16[256,256]{1,0:T(8,128)(2,1)}, bf16[256,256]{1,0:T(8,128)(2,1)S(1)}, u32[]{:S(2)}, u32[]{:S(2)}) collective-permute-start(bf16[256,256]{1,0:T(8,128)(2,1)} %key_hbm.1), channel_id=1, source_target_pairs={{0,16},{4,20},{8,24},{12,28},{1,17},{5,21},{9,25},{13,29},{2,18},{... | collective-permute-start | bytes 393224 | tf_op jit(solution)/shard_map/ppermute | solution.py:318
  1.9 11.1 %collective-permute-start.1 = (bf16[256,256]{1,0:T(8,128)(2,1)}, bf16[256,256]{1,0:T(8,128)(2,1)S(1)}, u32[]{:S(2)}, u32[]{:S(2)}) collective-permute-start(bf16[256,256]{1,0:T(8,128)(2,1)} %key_hbm.1), channel_id=1, source_target_pairs={{0,8},{4,12},{16,24},{20,28},{1,9},{5,13},{17,25},{21,29},{2,10},{... | collective-permute-start | bytes 393224 | tf_op jit(solution)/shard_map/ppermute | solution.py:325
  5.1 7.9 %collective-permute-start.3 = (bf16[256,256]{1,0:T(8,128)(2,1)}, bf16[256,256]{1,0:T(8,128)(2,1)S(1)}, u32[]{:S(2)}, u32[]{:S(2)}) collective-permute-start(bf16[256,256]{1,0:T(8,128)(2,1)} %value_hbm.1), channel_id=1, source_target_pairs={{0,16},{4,20},{8,24},{12,28},{1,17},{5,21},{9,25},{13,29},{2,18},{... | collective-permute-start | bytes 393224 | tf_op jit(solution)/shard_map/ppermute | solution.py:318
  6.4 6.9 %collective-permute-start.2 = (bf16[256,256]{1,0:T(8,128)(2,1)}, bf16[256,256]{1,0:T(8,128)(2,1)S(1)}, u32[]{:S(2)}, u32[]{:S(2)}) collective-permute-start(bf16[256,256]{1,0:T(8,128)(2,1)} %value_hbm.1), channel_id=1, source_target_pairs={{0,8},{4,12},{8,16},{12,20},{16,24},{20,28},{1,9},{5,13},{9,17},{1... | collective-permute-start | bytes 393224 | tf_op jit(solution)/shard_map/ppermute | solution.py:318
  8.3 6.0 %collective-permute-start.4 = (bf16[256,256]{1,0:T(8,128)(2,1)S(1)}, bf16[256,256]{1,0:T(8,128)(2,1)S(1)}, u32[]{:S(2)}, u32[]{:S(2)}) collective-permute-start(bf16[256,256]{1,0:T(8,128)(2,1)S(1)} %collective-permute-done.refs_1_), channel_id=1, source_target_pairs={{24,16},{28,20},{25,17},{29,21},{26,18},{30,22},{27,19},{31,23}} | collective-permute-start | bytes 393224 | tf_op jit(solution)/shard_map/ppermute | solution.py:326
  14.6 3.4 %collective-permute-start.5 = (bf16[2,256,512]{2,1,0:T(8,128)(2,1)S(1)}, bf16[2,256,512]{2,1,0:T(8,128)(2,1)S(1)}, u32[]{:S(2)}, u32[]{:S(2)}) collective-permute-start(bf16[2,256,512]{2,1,0:T(8,128)(2,1)S(1)} %get-tuple-element.22), channel_id=1, source_target_pairs={{0,4},{4,0},{8,12},{12,8},{16,20},{20,16},{24,28},{28,24},{1,5},{5... | collective-permute-start | bytes 1572872 | tf_op jit(solution)/shard_map/ppermute | solution.py:371
  20.0 14.7 %collective-permute-start.8 = (bf16[64,2048]{1,0:T(8,128)(2,1)S(1)}, bf16[64,2048]{1,0:T(8,128)(2,1)S(1)}, u32[]{:S(2)}, u32[]{:S(2)}) collective-permute-start(bf16[64,2048]{1,0:T(8,128)(2,1)S(1)} %get-tuple-element.31), channel_id=1, source_target_pairs={{0,1},{1,2},{2,3},{3,0},{4,5},{5,6},{6,7},{7,4},{8,9},{9,10},{10,1... | collective-permute-start | bytes 786440 | tf_op jit(solution)/shard_map/ppermute | solution.py:401
  25.3 18.5 %collective-permute-start.6 = (bf16[64,2048]{1,0:T(8,128)(2,1)S(1)}, bf16[64,2048]{1,0:T(8,128)(2,1)S(1)}, u32[]{:S(2)}, u32[]{:S(2)}) collective-permute-start(bf16[64,2048]{1,0:T(8,128)(2,1)S(1)} %get-tuple-element.28), channel_id=1, source_target_pairs={{0,2},{1,3},{2,0},{3,1},{4,6},{5,7},{6,4},{7,5},{8,10},{9,11},{10,... | collective-permute-start | bytes 786440 | tf_op jit(solution)/shard_map/ppermute | solution.py:401
  26.4 19.7 %collective-permute-start.7 = (bf16[64,2048]{1,0:T(8,128)(2,1)S(1)}, bf16[64,2048]{1,0:T(8,128)(2,1)S(1)}, u32[]{:S(2)}, u32[]{:S(2)}) collective-permute-start(bf16[64,2048]{1,0:T(8,128)(2,1)S(1)} %get-tuple-element.29), channel_id=1, source_target_pairs={{0,3},{1,0},{2,1},{3,2},{4,7},{5,4},{6,5},{7,6},{8,11},{9,8},{10,9... | collective-permute-start | bytes 786440 | tf_op jit(solution)/shard_map/ppermute | solution.py:401
  30.6 7.7 %all-to-all-start = ((f32[8,32,128]{2,1,0:T(8,128)}), f32[8,32,128]{2,1,0:T(8,128)S(1)}, u32[]{:S(2)}, u32[]{:S(2)}) async-start(f32[8,32,128]{2,1,0:T(8,128)} %bitcast), calls=%async_computation | async-start | bytes 262144 | tf_op jit(solution)/shard_map/all_to_all | solution.py:412
